TPU v7x, 512 devices: a whole 4x4x16 slice. The times are simulated.
512 devices in a mesh: sub: 32 (over x_lo, z), beam: 16 (over x_hi, y, core).
Axes of the slice: x: 4 (x_hi: 2, x_lo: 2; x = x_hi * 2 + x_lo), y: 4, z: 16, core: 2. Of those that a mesh axis runs over, the one named last changes fastest.
Arguments:
- echoes: bfloat16 [64, 32, 2, 16384], P('sub', 'beam'), may hold values from -6 to 6
- matched_filter: float32 [2, 16384], replicated, may hold values from -6 to 6
- steering: bfloat16 [2, 128, 32], P(None, 'beam'), may hold values from -1 to 1
- kernels: bfloat16 [4, 2, 2, 128, 128], replicated, may hold values from -0.375 to 0.375
- blend_gains: float32 [4, 2, 2, 2], replicated, may hold values from 0.3 to 1
- beam_taps: int32 [4, 2, 2, 128], P(None, None, None, 'beam'), may hold values from -1 to 0
Outputs:
- polar_image: bfloat16 [64, 128, 2, 16384], P('sub', 'beam')
Inputs may be any that keep to these rules, and one draw needn't show every extreme that they name: `beam_taps`: a parent row n reads child rows n + t and n + t + 1.
All inputs are finite; a program needn't handle non-finite values.
Results may differ from a plain program's by a relative error of at most 0.019.
Values may be sent and summed in bfloat16 or wider, within the bound.
No kernel may reach another device: no remote copies, remote signals or barrier semaphores. Data moves between devices by JAX's collectives and lax.ppermute only.
A program may use at most 64 MiB of HBM per device.

v0:
```python
import math

import jax
import jax.numpy as jnp
import numpy as np
from jax import lax
from jax.sharding import Mesh
from jax.sharding import PartitionSpec as P

FA = 128
LEVELS = 4
HIGH = lax.Precision.HIGH


def table_product(form, left, right):
    return jnp.einsum(form, left, right, precision=HIGH)


def dft_tables(order, sign, modulus):
    index = np.arange(order)
    phase = (index[:, None] * index[None, :]) % modulus
    angle = phase * (sign * 2.0 * math.pi / modulus)
    return (jnp.asarray(np.cos(angle), jnp.float32), jnp.asarray(np.sin(angle), jnp.float32))


def four_step(real_part, imag_part, sign):
    order = real_part.shape[-1]
    cos_small, sin_small = dft_tables(order, sign, order)
    cos_turn, sin_turn = dft_tables(order, sign, order * order)
    first_real = table_product("kn,qnm->qkm", cos_small, real_part) - table_product(
        "kn,qnm->qkm", sin_small, imag_part
    )
    first_imag = table_product("kn,qnm->qkm", cos_small, imag_part) + table_product(
        "kn,qnm->qkm", sin_small, real_part
    )
    turned_real = first_real * cos_turn - first_imag * sin_turn
    turned_imag = first_real * sin_turn + first_imag * cos_turn
    out_real = table_product("qkm,mj->qjk", turned_real, cos_small) - table_product(
        "qkm,mj->qjk", turned_imag, sin_small
    )
    out_imag = table_product("qkm,mj->qjk", turned_real, sin_small) + table_product(
        "qkm,mj->qjk", turned_imag, cos_small
    )
    return (out_real, out_imag)


def compress(echoes, matched_filter):
    count = echoes.shape[0] * echoes.shape[1]
    length = echoes.shape[-1]
    signal = echoes.astype(jnp.float32).reshape(count, 2, FA, FA)
    spec_real, spec_imag = four_step(signal[:, 0], signal[:, 1], -1.0)
    matched = matched_filter.reshape(2, FA, FA)
    prod_real = spec_real * matched[0] - spec_imag * matched[1]
    prod_imag = spec_real * matched[1] + spec_imag * matched[0]
    back_real, back_imag = four_step(prod_real, prod_imag, 1.0)
    stacked = jnp.stack([back_real, back_imag], axis=1) / length
    return stacked.reshape(echoes.shape[:3] + (FA, FA)).astype(jnp.bfloat16)


def as_blocks(pair):
    real_part, imag_part = pair[..., 0, :, :], pair[..., 1, :, :]
    top = jnp.concatenate([real_part, imag_part], axis=-1)
    bottom = jnp.concatenate([-imag_part, real_part], axis=-1)
    return jnp.concatenate([top, bottom], axis=-2)


def pick(table, index):
    return lax.dynamic_index_in_dim(table, index, 0, keepdims=False)


def range_chain(kernels, bits):
    blocks = as_blocks(kernels.astype(jnp.float32))
    chain = pick(blocks[3], bits[2])
    chain = table_product("ik,kj->ij", pick(blocks[2], bits[1]), chain)
    chain = table_product("ik,kj->ij", pick(blocks[1], bits[0]), chain)
    return table_product("cik,kj->cij", blocks[0], chain).astype(jnp.bfloat16)


def band_matrices(taps, gains):
    rows = taps.shape[0]
    first = jnp.moveaxis(taps, 0, -1).astype(jnp.int32)[..., None] + jnp.arange(rows)[:, None]
    column = jnp.arange(rows)
    lower = jnp.where(column == first, gains[..., 0, None, None], 0.0)
    upper = jnp.where(column == first + 1, gains[..., 1, None, None], 0.0)
    return lower + upper


def local(echoes, matched_filter, steering, kernels, blend_gains, beam_taps):
    zh = lax.axis_index("zh")
    zl = lax.axis_index("zl")
    own_rows = steering.shape[1]
    pulses = steering.shape[2]
    own_pulses = echoes.shape[1]
    beams = pulses // own_pulses

    packed = jnp.concatenate(
        [
            jnp.moveaxis(steering, 1, 0).reshape(own_rows, 2 * pulses),
            jnp.moveaxis(beam_taps, 3, 0).reshape(own_rows, 4 * LEVELS).astype(jnp.bfloat16),
        ],
        axis=1,
    )
    packed = jnp.pad(packed, ((0, 0), (0, 128 - packed.shape[1])))
    packed = lax.all_gather(packed, "beam", axis=0, tiled=True)
    rows = packed.shape[0]

    compressed = compress(echoes, matched_filter)
    mats = range_chain(kernels, (zl & 1, zl >> 1, zh)).reshape(2, 2, FA, 2, FA)
    turned = jnp.einsum(
        "spinm,simoj->sponj", compressed, mats, preferred_element_type=jnp.float32
    ).astype(jnp.bfloat16)
    width = 2 * own_pulses * 2
    peers = 4 * beams
    message = jnp.moveaxis(turned.reshape(width, peers, -1), 1, 0)
    own = lax.all_to_all(message, ("zl", "beam"), 0, 0, tiled=True).reshape(peers * width, -1)
    other = lax.ppermute(own, "zh", [(0, 1), (1, 0)])

    steer = packed[:, : 2 * pulses].astype(jnp.float32).reshape(rows, 2, beams, own_pulses)
    taps = packed[:, 2 * pulses : 2 * pulses + 4 * LEVELS].reshape(rows, LEVELS, 2, 2)
    band = band_matrices(taps, blend_gains)
    mixing = jnp.stack(
        [jnp.stack([steer[:, 0], -steer[:, 1]], -1), jnp.stack([steer[:, 1], steer[:, 0]], -1)], 1
    )
    lead = table_product("cenm,mobpi->enobcpi", band[0], mixing).reshape(2, rows, -1)
    lead = table_product("cenm,fmx->cefnx", band[1], lead)
    lead = table_product("cenm,dfgmx->cdefgnx", band[2], lead)

    def last(child):
        b4 = pick(pick(band[3], child), zh)
        full = table_product("nm,cdefgmx->cdefgnx", b4, lead).astype(jnp.bfloat16)
        full = full.reshape(2, 2, 2, 2, 2, beams, own_rows, 2, FA)
        full = jnp.transpose(full, (2, 3, 5, 4, 7, 6, 0, 1, 8))
        return full.reshape(4 * beams * 2 * 2 * own_rows, 4 * FA)

    total = jnp.dot(last(zh), own, preferred_element_type=jnp.float32)
    total = total + jnp.dot(last(1 - zh), other, preferred_element_type=jnp.float32)
    result = total.astype(jnp.bfloat16).reshape(peers, 2 * 2 * own_rows, -1)
    arrived = lax.all_to_all(result, ("zl", "beam"), 0, 0, tiled=True)
    arrived = arrived.reshape(peers, 2, 2, own_rows, -1)
    return jnp.transpose(arrived, (1, 3, 2, 0, 4)).reshape(2, own_rows, 2, -1)


def solution(mesh):
    fine = Mesh(mesh.devices.reshape(4, 2, 4, 16), ("g", "zh", "zl", "beam"))
    sub = ("g", "zh", "zl")
    return jax.shard_map(
        local,
        mesh=fine,
        in_specs=(
            P(sub, "beam", None, None),
            P(),
            P(None, "beam", None),
            P(),
            P(),
            P(None, None, None, "beam"),
        ),
        out_specs=P(sub, "beam", None, None),
        check_vma=False,
    )
```

profile of v0, /device:TPU:1, one launch (start us, length us, event | category | flops | bytes accessed | tf_op | source)
XLA Modules:
  0.0 150.1 jit_solution(6426579035786599615)
XLA Ops:
  0.0 1.2 reshape.128
  1.2 1.1 fusion.34
  2.3 1.1 fusion.33
  3.4 1.1 convolution_add_fusion.4
  7.3 0.4 fusion.36
  8.2 0.9 slice_bitcast_fusion.2
  9.2 0.4 convolution_subtract_fusion
  9.7 0.4 convolution_add_fusion.1
  10.1 0.8 copy.172
  10.9 1.4 maximum_maximum_fusion
  12.3 1.0 fusion.59
  13.6 1.3 convolution_bitcast_fusion.3
  15.9 0.9 copy.175
  16.8 13.1 %all-to-all-start = ((bf16[64,8,256]{2,1,0:T(8,128)(2,1)}), bf16[64,8,256]{2,1,0:T(8,128)(2,1)S(1)}, u32[]{:S(2)}, u32[]{:S(2)}) async-start(bf16[64,8,256]{2,1,0:T(8,128)(2,1)} %copy.175), calls=%async_computation | async-start | bytes 524288 | tf_op jit(solution)/shard_map/all_to_all | solution.py:115
  30.1 24.7 %all_gather.3 = bf16[128,128]{1,0:T(8,128)(2,1)S(1)} all-gather(bf16[8,128]{1,0:T(8,128)(2,1)S(1)} %fusion.47), channel_id=1, replica_groups=mesh['g'=4,'zh'=2,'zl'=4,'beam'=16] {'beam'}, dimensions={0}, use_global_device_ids=true | all-gather | bytes 34816 | tf_op jit(solution)/shard_map/all_gather | solution.py:104
  55.3 0.6 select_add_fusion
  56.5 0.6 convolution_bitcast_fusion.1
  57.1 1.9 %convolution_bitcast_fusion = f32[2,2,2,2,2,128,256]{5,6,2,0,4,3,1:T(8,128)S(1)} fusion(f32[2,2,2,128,256,1,1]{3,4,6,5,2,1,0:T(8,128)S(1)} %convolution_bitcast_fusion.1, f32[4,2,2,128,128]{4,3,2,1,0:T(8,128)S(1)} %select_add_fusion), kind=kOutput, calls=%fused_computation.6 | convolution fusion | flops 805306368 | bytes 5505024 | tf_op jit(solution)/shard_map/cenm,dfgmx->cdefgnx/dot_general | solution.py:16
  59.0 1.9 %copy-done = f32[2,2,2,2,2,128,256]{5,6,2,0,4,3,1:T(8,128)} copy-done((f32[2,2,2,2,2,128,256]{5,6,2,0,4,3,1:T(8,128)}, f32[2,2,2,2,2,128,256]{5,6,2,0,4,3,1:T(8,128)S(1)}, u32[]{:S(2)}) %copy-start) | copy-done | bytes 4194328
  60.9 2.0 %convert_bitcast_fusion.1 = bf16[2,2,2,2,2,128,256]{5,6,4,3,2,1,0:T(8,128)(2,1)S(1)} fusion(f32[2,2,2,2,2,128,256]{5,6,2,0,4,3,1:T(8,128)S(1)} %convolution_bitcast_fusion, f32[1,2,2,128,128]{4,3,2,1,0:T(8,128)S(1)} %slice.94, s32[]{:T(128)S(6)} %select_n.32), kind=kOutput, calls=%fused_computation.9 | convolution fusion | flops 806354944 | bytes 6356996 | tf_op jit(solution)/shard_map/nm,cdefgmx->cdefgnx/dot_general | solution.py:16
  63.0 2.4 %copy.160 = bf16[2,2,2,2,2,128,256]{6,5,4,3,2,1,0:T(8,128)(2,1)} copy(bf16[2,2,2,2,2,128,256]{5,6,4,3,2,1,0:T(8,128)(2,1)S(1)} %convert_bitcast_fusion.1) | data formatting | bytes 4194304 | tf_op jit(solution)/shard_map/convert_element_type | solution.py:130
  65.3 2.2 %copy.161 = bf16[2,2,16,2,2,8,2,2,128]{8,5,7,6,4,3,2,1,0:T(8,128)(2,1)S(1)} copy(bf16[2,2,16,2,2,8,2,2,128]{8,5,4,2,3,1,0,7,6:T(8,128)(2,1)} %bitcast.206) | data formatting | bytes 4194304 | tf_op jit(solution)/shard_map/transpose | solution.py:132
  67.5 5.4 %convert_bitcast_fusion = bf16[2,2,2,2,2,128,256]{5,6,4,3,2,1,0:T(8,128)(2,1)} fusion(f32[2,2,2,2,2,128,256]{5,6,2,0,4,3,1:T(8,128)} %copy-done, f32[1,2,2,128,128]{4,3,2,1,0:T(8,128)S(1)} %slice.94, s32[]{:T(128)S(6)} %select_n.36, s32[]{:T(128)S(6)} %select_n.32), kind=kOutput, calls=%fused_computation.8 | convolution fusion | flops 806354944 | bytes 6357000 | tf_op jit(solution)/shard_map/nm,cdefgmx->cdefgnx/dot_general | solution.py:16
  72.9 4.1 %copy.177 = bf16[2,2,2,2,2,128,256]{6,5,4,3,2,1,0:T(8,128)(2,1)} copy(bf16[2,2,2,2,2,128,256]{5,6,4,3,2,1,0:T(8,128)(2,1)} %convert_bitcast_fusion) | data formatting | bytes 4194304 | tf_op jit(solution)/shard_map/convert_element_type | solution.py:130
  77.0 3.5 %copy.178 = bf16[2,2,16,2,2,8,2,2,128]{8,5,7,6,4,3,2,1,0:T(8,128)(2,1)} copy(bf16[2,2,16,2,2,8,2,2,128]{8,5,4,2,3,1,0,7,6:T(8,128)(2,1)} %bitcast.207) | data formatting | bytes 4194304 | tf_op jit(solution)/shard_map/transpose | solution.py:132
  80.5 8.8 %collective-permute-start = (bf16[512,256]{1,0:T(8,128)(2,1)S(1)}, bf16[512,256]{1,0:T(8,128)(2,1)S(1)}, u32[]{:S(2)}, u32[]{:S(2)}) collective-permute-start(bf16[512,256]{1,0:T(8,128)(2,1)S(1)} %bitcast.216), channel_id=1, source_target_pairs={{0,64},{64,0},{1,65},{65,1},{2,66},{66,2},{3,67},{67,3},{4,68},{68... | collective-permute-start | bytes 786440 | tf_op jit(solution)/shard_map/ppermute | solution.py:116
  89.3 0.7 fusion.54
  90.0 22.7 %collective-permute-done = bf16[512,256]{1,0:T(8,128)(2,1)S(1)} collective-permute-done((bf16[512,256]{1,0:T(8,128)(2,1)S(1)}, bf16[512,256]{1,0:T(8,128)(2,1)S(1)}, u32[]{:S(2)}, u32[]{:S(2)}) %collective-permute-start) | collective-permute-done | bytes 262176 | tf_op jit(solution)/shard_map/ppermute | solution.py:116
  112.8 0.7 fusion.4
  113.5 34.9 %all_to_all.10 = bf16[64,32,256]{2,1,0:T(8,128)(2,1)S(1)} all-to-all(bf16[64,32,256]{2,1,0:T(8,128)(2,1)S(1)} %bitcast.210), channel_id=1, replica_groups=mesh['g'=4,'zh'=2,'zl'=4,'beam'=16] {'zl','beam'}, dimensions={0} | all-to-all | bytes 2097152 | tf_op jit(solution)/shard_map/all_to_all | solution.py:138
  148.4 0.6 copy.221
  149.0 1.1 reshape.109
  (71 shorter events, 5.9 us)
Async XLA Ops:
  0.0 5.0 %copy-start.2 = (f32[128,128,1]{1,0,2:T(8,128)S(1)}, f32[128,128,1]{1,0,2:T(8,128)}, u32[]{:S(2)}) copy-start(f32[128,128,1]{1,0,2:T(8,128)} %constant.123) | copy-start | bytes 196612
  0.0 4.4 %copy-start.7 = (f32[128,128,1]{1,0,2:T(8,128)S(1)}, f32[128,128,1]{1,0,2:T(8,128)}, u32[]{:S(2)}) copy-start(f32[128,128,1]{1,0,2:T(8,128)} %constant.124) | copy-start | bytes 196612
  0.0 4.6 %copy-start.8 = (f32[128,128]{1,0:T(8,128)S(1)}, f32[128,128]{1,0:T(8,128)}, u32[]{:S(2)}) copy-start(f32[128,128]{1,0:T(8,128)} %constant.114.clone) | copy-start | bytes 196612
  0.0 4.7 %copy-start.9 = (f32[128,128]{1,0:T(8,128)S(1)}, f32[128,128]{1,0:T(8,128)}, u32[]{:S(2)}) copy-start(f32[128,128]{1,0:T(8,128)} %constant.115.clone) | copy-start | bytes 196612
  4.7 1.1 copy-start.11
  5.5 1.2 copy-start.4
  6.1 1.2 copy-start.5
  6.1 1.2 copy-start.6
  6.7 1.4 copy-start.10
  13.5 1.8 %copy-start.3 = (f32[2,2,1,128,128]{4,3,2,1,0:T(8,128)S(1)}, f32[2,2,1,128,128]{4,3,2,1,0:T(8,128)}, u32[]{:S(2)}) copy-start(f32[2,2,1,128,128]{4,3,2,1,0:T(8,128)} %copy.172) | copy-start | bytes 786436
  15.2 14.6 %copy-start.12 = (s32[4,2,2,8]{3,2,1,0:T(2,128)S(1)}, s32[4,2,2,8]{3,2,1,0:T(2,128)}, u32[]{:S(2)}) copy-start(s32[4,2,2,8]{3,2,1,0:T(2,128)} %param.19) | copy-start | bytes 1540
  15.2 14.7 %copy-start.13 = (bf16[2,8,32]{2,1,0:T(8,128)(2,1)S(1)}, bf16[2,8,32]{2,1,0:T(8,128)(2,1)}, u32[]{:S(2)}) copy-start(bf16[2,8,32]{2,1,0:T(8,128)(2,1)} %param.16) | copy-start | bytes 3076
  15.2 39.9 %copy-start.14 = (f32[4,2,2,2]{0,3,2,1:T(2,128)S(1)}, f32[4,2,2,2]{0,3,2,1:T(2,128)}, u32[]{:S(2)}) copy-start(f32[4,2,2,2]{0,3,2,1:T(2,128)} %param.18) | copy-start | bytes 388
  16.8 63.7 %all-to-all-start = ((bf16[64,8,256]{2,1,0:T(8,128)(2,1)}), bf16[64,8,256]{2,1,0:T(8,128)(2,1)S(1)}, u32[]{:S(2)}, u32[]{:S(2)}) async-start(bf16[64,8,256]{2,1,0:T(8,128)(2,1)} %copy.175), calls=%async_computation | async-start | bytes 524288 | tf_op jit(solution)/shard_map/all_to_all | solution.py:115
  59.0 1.9 %copy-start = (f32[2,2,2,2,2,128,256]{5,6,2,0,4,3,1:T(8,128)}, f32[2,2,2,2,2,128,256]{5,6,2,0,4,3,1:T(8,128)S(1)}, u32[]{:S(2)}) copy-start(f32[2,2,2,2,2,128,256]{5,6,2,0,4,3,1:T(8,128)S(1)} %convolution_bitcast_fusion) | copy-start | bytes 12582916
  80.5 32.3 %collective-permute-start = (bf16[512,256]{1,0:T(8,128)(2,1)S(1)}, bf16[512,256]{1,0:T(8,128)(2,1)S(1)}, u32[]{:S(2)}, u32[]{:S(2)}) collective-permute-start(bf16[512,256]{1,0:T(8,128)(2,1)S(1)} %bitcast.216), channel_id=1, source_target_pairs={{0,64},{64,0},{1,65},{65,1},{2,66},{66,2},{3,67},{67,3},{4,68},{68... | collective-permute-start | bytes 786440 | tf_op jit(solution)/shard_map/ppermute | solution.py:116
  89.3 23.4 %copy-start.1 = (bf16[2,2,16,2,2,8,2,2,128]{8,5,7,6,4,3,2,1,0:T(8,128)(2,1)S(1)}, bf16[2,2,16,2,2,8,2,2,128]{8,5,7,6,4,3,2,1,0:T(8,128)(2,1)}, u32[]{:S(2)}) copy-start(bf16[2,2,16,2,2,8,2,2,128]{8,5,7,6,4,3,2,1,0:T(8,128)(2,1)} %copy.178) | copy-start | bytes 6291460
where the time goes:
time: 151 us; the launch traced here: 150 us
  blocking collectives  59.6 us (39%)
  waiting for transfers between devices  22.7 us (15%)
  local copies, waits for them, and re-layouts  22.1 us (15%)
  starting transfers between devices  21.9 us (15%)
  matrix products  20.8 us (14%)
  other arithmetic  2.36 us (2%)
    all_to_all x1, blocking collectives, local(): arrived = lax.all_to_all(result, ('zl', 'beam'), 0, 0, tiled=True)  34.9 us
    all_gather x1, blocking collectives, local(): packed = lax.all_gather(packed, 'beam', axis=0, tiled=True)  24.7 us
    ppermute x1, waiting for transfers between devices, local(): other = lax.ppermute(own, 'zh', [(0, 1), (1, 0)])  22.7 us
    dot_general x24, matrix products, table_product(): return jnp.einsum(form, left, right, precision=HIGH)  19.1 us
    all_to_all x1, starting transfers between devices, local(): lax.all_to_all(message, ('zl', 'beam'), 0, 0, tiled=True)  13.1 us
    ppermute x1, starting transfers between devices, local(): other = lax.ppermute(own, 'zh', [(0, 1), (1, 0)])  8.81 us
    convert_element_type x2, local copies, waits for them, and re-layouts, last(): full = table_product('nm,cdefgmx->cdefgnx', b4, lead).astype(jnp.bfloat16)  6.51 us
    transpose x2, local copies, waits for them, and re-layouts, last(): full = jnp.transpose(full, (2, 3, 5, 4, 7, 6, 0, 1, 8))  5.65 us
  transfers between devices with their start and end apart: 2, of which 1 were waited for; matrix products, arithmetic and copies ran while one was open for 16% of the time, Pallas kernels for 0%

commit v1 on v0

v1 whole, which is shorter than its diff:
```python
import math

import jax
import jax.numpy as jnp
import ml_dtypes
import numpy as np
from jax import lax
from jax.experimental import pallas as pl
from jax.experimental.pallas import tpu as pltpu
from jax.sharding import Mesh
from jax.sharding import PartitionSpec as P

FA = 128
LEVELS = 4
BF16 = jnp.bfloat16
F32 = jnp.float32


def halves(table):
    high = table.astype(ml_dtypes.bfloat16)
    low = (table - high.astype(np.float64)).astype(ml_dtypes.bfloat16)
    return np.stack([high, low])


def dft_blocks():
    index = np.arange(FA)
    product = index[:, None] * index[None, :]
    angle = (product % FA) * (2.0 * math.pi / FA)
    c, s = np.cos(angle), np.sin(angle)
    turn = (product % (FA * FA)) * (2.0 * math.pi / (FA * FA))
    return (
        halves(np.block([[c, s], [-s, c]])),
        halves(np.block([[c, -s], [s, c]])),
        np.stack([np.cos(turn), np.sin(turn)]).astype(np.float32),
    )


def split(value):
    high = value.astype(BF16)
    return high, (value - high.astype(F32)).astype(BF16)


def dot(left, right):
    return jnp.dot(left, right, preferred_element_type=F32)


def dot_table(value, table):
    high, low = split(value)
    return dot(high, table[0]) + dot(low, table[0]) + dot(high, table[1])


def table_dot(table, value):
    high, low = split(value)
    return dot(table[0], high) + dot(table[0], low) + dot(table[1], high)


def complex_block(ref, *index):
    real_part, imag_part = ref[(*index, 0)], ref[(*index, 1)]
    top = jnp.concatenate([real_part, imag_part], axis=1)
    return jnp.concatenate([top, jnp.concatenate([-imag_part, real_part], axis=1)], axis=0)


def compress_kernel(bits, echo, matched, kern, packed, plus, minus, turn, out, rows):
    count = echo.shape[0]
    width = 2 * count
    c, s = turn[0], turn[1]

    chain = complex_block(kern, 3, bits[2]).astype(F32)
    for level in (2, 1):
        high, low = split(chain)
        block = complex_block(kern, level, bits[level - 1])
        chain = dot(block, high) + dot(block, low)
    high, low = split(chain)
    mats = []
    for child in range(2):
        block = complex_block(kern, 0, child)
        mats.append((dot(block, high) + dot(block, low)).astype(BF16))

    signal = jnp.concatenate([echo[q].reshape(2 * FA, FA) for q in range(count)], axis=1)
    first = dot(plus[0], signal) + dot(plus[1], signal)
    stacked = []
    for q in range(count):
        real_part = first[:FA, q * FA : (q + 1) * FA]
        imag_part = first[FA:, q * FA : (q + 1) * FA]
        stacked.append(
            jnp.concatenate([real_part * c + imag_part * s, imag_part * c - real_part * s], axis=1)
        )
    spectrum = dot_table(jnp.concatenate(stacked, axis=0), minus)

    scale = 1.0 / (FA * FA)
    filter_real = jnp.transpose(matched[0]) * scale
    filter_imag = jnp.transpose(matched[1]) * scale
    stacked = []
    for q in range(count):
        real_part = spectrum[q * FA : (q + 1) * FA, :FA]
        imag_part = spectrum[q * FA : (q + 1) * FA, FA:]
        stacked.append(
            jnp.concatenate(
                [
                    real_part * filter_real - imag_part * filter_imag,
                    real_part * filter_imag + imag_part * filter_real,
                ],
                axis=1,
            )
        )
    back = dot_table(jnp.concatenate(stacked, axis=0), plus)

    stacked = []
    for q in range(count):
        real_part = back[q * FA : (q + 1) * FA, :FA]
        imag_part = back[q * FA : (q + 1) * FA, FA:]
        stacked.append(
            jnp.concatenate([real_part * c - imag_part * s, imag_part * c + real_part * s], axis=0)
        )
    pulses = table_dot(minus, jnp.concatenate(stacked, axis=1)).astype(BF16)

    for q in range(count):
        lanes = slice(q * FA, (q + 1) * FA)
        pair = jnp.concatenate([pulses[:FA, lanes], pulses[FA:, lanes]], axis=1)
        turned = dot(pair, mats[q * 2 // count])
        rows[pl.ds(2 * q, FA, stride=width), :] = turned[:, :FA]
        rows[pl.ds(2 * q + 1, FA, stride=width), :] = turned[:, FA:]
    half = FA // 2
    for part in range(2):
        piece = rows[pl.ds(part * half * width, half * width), :]
        out[:, :, part * FA : (part + 1) * FA] = piece.reshape(half, width, FA).astype(BF16)
    out[:, :, 2 * FA :] = jnp.broadcast_to(packed[...][None], (half, width, FA))


def compress(bits, echo, matched, kern, packed):
    plus, minus, turn = dft_blocks()
    width = 2 * echo.shape[0]
    vmem = pl.BlockSpec(memory_space=pltpu.VMEM)
    return pl.pallas_call(
        compress_kernel,
        out_shape=jax.ShapeDtypeStruct((FA // 2, width, 3 * FA), BF16),
        in_specs=[pl.BlockSpec(memory_space=pltpu.SMEM)] + [vmem] * 7,
        out_specs=vmem,
        scratch_shapes=[pltpu.VMEM((FA * width, FA), F32)],
        compiler_params=pltpu.CompilerParams(vmem_limit_bytes=32 * 2**20),
        cost_estimate=pl.CostEstimate(flops=10**9, bytes_accessed=2 * 10**6, transcendentals=0),
    )(bits, echo, matched, kern, packed, jnp.asarray(plus), jnp.asarray(minus), jnp.asarray(turn))


def beam_kernel(steer_lanes, bits, gains, packed, mixing, out_own, out_other):
    e3 = pl.program_id(0) // 2
    e2 = pl.program_id(0) % 2
    e4 = bits[2]
    rows = packed.shape[0]
    data = packed[...]
    taps = data.astype(F32)
    row = lax.broadcasted_iota(jnp.int32, (rows, FA), 0)
    lane = lax.broadcasted_iota(jnp.int32, (rows, FA), 1)

    def weights(level, child, parity):
        at = steer_lanes + (level * 2 + child) * 2
        even, odd = taps[:, at : at + 1], taps[:, at + 1 : at + 2]
        if isinstance(parity, int):
            tap = odd if parity else even
        else:
            tap = jnp.where(parity == 1, odd, even)
        tap = jnp.broadcast_to(tap, (rows, FA))
        index = ((level * 2 + child) * 2 + parity) * 2
        g0, g1 = gains[index], gains[index + 1]
        backward = tap < 0
        before = jnp.where(backward & (row > 0), g0, 0.0)
        here = jnp.where(backward, g1, g0)
        after = jnp.where(jnp.logical_not(backward) & (row < rows - 1), g1, 0.0)
        return before, here, after

    def neighbours(value):
        return pltpu.roll(value, 1, 0), value, pltpu.roll(value, rows - 1, 0)

    def blend(near, weight):
        return near[0] * weight[0] + near[1] * weight[1] + near[2] * weight[2]

    second_child = (lane // 4) % 2 == 1
    levels = [[weights(level, child, parity) for child in range(2)] for level, parity in ((1, e2), (2, e3), (3, e4))]
    for e1 in range(2):
        pair = [weights(0, child, e1) for child in range(2)]
        lead = [jnp.where(second_child, odd, even) for even, odd in zip(*pair)]
        start = [blend(neighbours(dot(data, mixing[o])), lead) for o in range(2)]
        for c2 in range(2):
            mid = [blend(neighbours(v), levels[0][c2]) for v in start]
            for c3 in range(2):
                high = [neighbours(blend(neighbours(v), levels[1][c3])) for v in mid]
                lanes = slice((c3 * 2 + c2) * FA, (c3 * 2 + c2 + 1) * FA)
                for own, out in ((True, out_own), (False, out_other)):
                    weight = [
                        jnp.where((e4 == 0) == own, zero, one) for zero, one in zip(levels[2][0], levels[2][1])
                    ]
                    done = [blend(near, weight).reshape(rows // 8, 8, FA) for near in high]
                    out[0, :, e1, :, lanes] = jnp.concatenate(done, axis=1).astype(BF16)


def beam_factors(bits, gains, packed, beams, own_pulses):
    rows = packed.shape[0]
    pulses = beams * own_pulses
    mixing = np.zeros((2, FA, FA), ml_dtypes.bfloat16)
    for b in range(beams):
        for c1 in range(2):
            for p in range(own_pulses):
                for i in range(2):
                    lane = ((b * 2 + c1) * own_pulses + p) * 2 + i
                    pulse = b * own_pulses + p
                    mixing[0, i * pulses + pulse, lane] = -1 if i else 1
                    mixing[1, (1 - i) * pulses + pulse, lane] = 1
    shape = jax.ShapeDtypeStruct((4, rows // 8, 2, 16, 4 * FA), BF16)
    spec = pl.BlockSpec((1, rows // 8, 2, 16, 4 * FA), lambda g: (g, 0, 0, 0, 0))
    smem = pl.BlockSpec(memory_space=pltpu.SMEM)
    vmem = pl.BlockSpec(memory_space=pltpu.VMEM)

    def kernel(*refs):
        beam_kernel(2 * pulses, *refs)

    return pl.pallas_call(
        kernel,
        grid=(4,),
        out_shape=(shape, shape),
        in_specs=[smem, smem, vmem, vmem],
        out_specs=(spec, spec),
        compiler_params=pltpu.CompilerParams(vmem_limit_bytes=32 * 2**20),
        cost_estimate=pl.CostEstimate(flops=2 * 10**9, bytes_accessed=4 * 10**6, transcendentals=0),
    )(bits, gains, packed, jnp.asarray(mixing))


def local(echoes, matched_filter, steering, kernels, blend_gains, beam_taps):
    zh = lax.axis_index("zh")
    zl = lax.axis_index("zl")
    own_rows = steering.shape[1]
    pulses = steering.shape[2]
    own_pulses = echoes.shape[1]
    beams = pulses // own_pulses
    peers = 4 * beams
    bits = jnp.stack([zl & 1, zl >> 1, zh]).astype(jnp.int32)

    packed = jnp.concatenate(
        [
            jnp.moveaxis(steering, 1, 0).reshape(own_rows, 2 * pulses),
            jnp.moveaxis(beam_taps, 3, 0).reshape(own_rows, 4 * LEVELS).astype(BF16),
        ],
        axis=1,
    )
    packed = jnp.pad(packed, ((0, 0), (0, FA - packed.shape[1])))
    message = compress(
        bits, echoes.reshape(2 * own_pulses, 2, FA, FA), matched_filter.reshape(2, FA, FA), kernels, packed
    )
    arrived = lax.all_to_all(message, ("zl", "beam"), 0, 0, tiled=True)
    own = arrived[:, :, : 2 * FA].reshape(-1, 2 * FA)
    other = lax.ppermute(own, "zh", [(0, 1), (1, 0)])
    packed = arrived[:beams, :, 2 * FA :].reshape(-1, FA)
    near, far = beam_factors(bits, blend_gains.reshape(-1), packed, beams, own_pulses)

    total = dot(near.reshape(-1, 4 * FA), own)
    total = total + dot(far.reshape(-1, 4 * FA), other)
    result = total.astype(BF16).reshape(peers, 4 * own_rows, 2 * FA)
    arrived = lax.all_to_all(result, ("zl", "beam"), 0, 0, tiled=True)
    arrived = arrived.reshape(peers, 2, 2, own_rows, 2, FA)
    return jnp.transpose(arrived, (1, 3, 2, 4, 0, 5)).reshape(2, own_rows, 2, -1)


def solution(mesh):
    fine = Mesh(mesh.devices.reshape(4, 2, 4, 16), ("g", "zh", "zl", "beam"))
    sub = ("g", "zh", "zl")
    return jax.shard_map(
        local,
        mesh=fine,
        in_specs=(
            P(sub, "beam", None, None),
            P(),
            P(None, "beam", None),
            P(),
            P(),
            P(None, None, None, "beam"),
        ),
        out_specs=P(sub, "beam", None, None),
        check_vma=False,
    )
```

time: 151 us -> 109 us (0.72)
  blocking collectives: 59.6 us -> 34.3 us
  matrix products: 20.8 us -> 1.43 us
  local copies, waits for them, and re-layouts: 22.1 us -> 8.8 us
  Pallas kernels: 0 us -> 9.97 us
  waiting for transfers between devices: 22.7 us -> 31.5 us
    all_gather x1 -> x0, blocking collectives: 24.7 us -> none  [local(): packed = lax.all_gather(packed, 'beam', axis=0, tiled=True)]
    dot_general x27 -> x2, matrix products: 20.8 us -> 1.43 us  [dot(): return jnp.dot(left, right, preferred_element_type=F32)]
    all_to_all x1, waiting for transfers between devices: 0.01 us -> 16 us  [local(): arrived = lax.all_to_all(message, ('zl', 'beam'), 0, 0, tiled=True)]
    pallas_call x0 -> x2, Pallas kernels: none -> 9.97 us  [the longest x1 6.27 us: beam_factors(): pl.pallas_call(kernel, grid=(4,), out_shape=(shape, shape), in_specs=[sme...]
    ppermute x1, waiting for transfers between devices: 22.7 us -> 15.5 us  [local(): other = lax.ppermute(own, 'zh', [(0, 1), (1, 0)])]
    transpose x4 -> x0, local copies, waits for them, and re-layouts: 6.71 us -> none  [the longest x2 5.65 us: last(): full = jnp.transpose(full, (2, 3, 5, 4, 7, 6, 0, 1, 8))]
    convert_element_type x4 -> x1, local copies, waits for them, and re-layouts: 6.77 us -> 0.08 us  [local(): jnp.moveaxis(beam_taps, 3, 0).reshape(own_rows, 4 * LEVELS).astype(BF16)]
    unnamed x32 -> x14, local copies, waits for them, and re-layouts: 2.15 us -> 4.88 us
  transfers between devices with their start and end apart: 2 -> 2, of which waited for: 1 -> 2; matrix products, arithmetic and copies ran while one was open for 16% -> 1% of each run, Pallas kernels for 0% -> 6%
where the time goes in v1:
time: 109 us
  blocking collectives  34.3 us (31%)
  waiting for transfers between devices  31.5 us (29%)
  starting transfers between devices  21.9 us (20%)
  Pallas kernels  9.97 us (9%)
  local copies, waits for them, and re-layouts  8.8 us (8%)
  matrix products  1.43 us (1%)
    all_to_all x1, blocking collectives, local(): arrived = lax.all_to_all(result, ('zl', 'beam'), 0, 0, tiled=True)  34.3 us
    all_to_all x1, waiting for transfers between devices, local(): arrived = lax.all_to_all(message, ('zl', 'beam'), 0, 0, tiled=True)  16 us
    ppermute x1, waiting for transfers between devices, local(): other = lax.ppermute(own, 'zh', [(0, 1), (1, 0)])  15.5 us
    all_to_all x1, starting transfers between devices, local(): arrived = lax.all_to_all(message, ('zl', 'beam'), 0, 0, tiled=True)  13.1 us
    ppermute x1, starting transfers between devices, local(): other = lax.ppermute(own, 'zh', [(0, 1), (1, 0)])  8.82 us
    pallas_call x1, Pallas kernels, beam_factors(): pl.pallas_call(kernel, grid=(4,), out_shape=(shape, shape), in_specs=[sme...  6.27 us
    unnamed x14, local copies, waits for them, and re-layouts  4.88 us
    pallas_call x1, Pallas kernels, compress(): pl.pallas_call(compress_kernel, out_shape=jax.ShapeDtypeStruct((FA // 2,...  3.7 us
  transfers between devices with their start and end apart: 2, of which 2 were waited for; matrix products, arithmetic and copies ran while one was open for 1% of the time, Pallas kernels for 6%

profile of v1, /device:TPU:1, one launch (start us, length us, event | category | flops | bytes accessed | tf_op | source)
XLA Modules:
  0.0 108.8 jit_solution(2551736272717410532)
XLA Ops:
  0.0 1.2 %reshape.36.echo = bf16[4,2,128,128]{3,2,1,0:T(8,128)(2,1)S(1)} reshape(bf16[2,2,2,16384]{3,2,1,0:T(2,128)(2,1)} %param.10) | data formatting | bytes 524288 | tf_op jit(solution)/shard_map/reshape | solution.py:246
  1.2 0.9 copy.23
  2.1 0.7 convert_element_type.14
  2.8 0.1 copy.17
  2.9 0.7 copy.16
  3.6 0.1 reshape.38
  3.6 0.1 fusion.3.packed
  3.7 0.1 pad_add_fusion.bits.refs_0_
  3.8 0.0 copy-start
  3.8 1.0 copy-done
  4.8 0.0 copy-start.1
  4.8 0.9 copy-done.1
  5.8 0.0 copy-start.2
  5.8 0.9 copy-done.2
  6.7 0.9 copy-done.3
  7.6 0.0 copy-start.5
  7.7 0.0 copy-start.4
  7.7 3.7 %shard_map.100 = bf16[64,8,384]{2,1,0:T(8,128)(2,1)} custom-call(s32[3]{0:T(128)S(1)} %pad_add_fusion.bits.refs_0_, bf16[4,2,128,128]{3,2,1,0:T(8,128)(2,1)S(1)} %reshape.36.echo, f32[2,128,128]{2,1,0:T(8,128)S(1)} %bitcast.30, bf16[4,2,2,128,128]{4,3,2,1,0:T(8,128)(2,1)S(1)} %copy-done, bf16[8,128]{1,0:T(8,128)(2,1)S(1)} %fusion.3.packed, ...), custom_call_target="tpu_custom_call" | custom-call | flops 1000000000 | bytes 2000000 | tf_op jit(solution)/shard_map/pallas_call | solution.py:134
  11.4 13.1 %all-to-all-start = ((bf16[64,8,384]{2,1,0:T(8,128)(2,1)}), bf16[64,8,384]{2,1,0:T(8,128)(2,1)S(1)}, u32[]{:S(2)}, u32[]{:S(2)}) async-start(bf16[64,8,384]{2,1,0:T(8,128)(2,1)} %shard_map.100), calls=%async_computation | async-start | bytes 786432 | tf_op jit(solution)/shard_map/all_to_all | solution.py:248
  24.4 0.0 copy-done.5
  24.4 0.1 copy.15
  24.5 0.1 reshape.35.refs_1_
  24.6 16.0 %all-to-all-done = bf16[64,8,384]{2,1,0:T(8,128)(2,1)S(1)} async-done(((bf16[64,8,384]{2,1,0:T(8,128)(2,1)}), bf16[64,8,384]{2,1,0:T(8,128)(2,1)S(1)}, u32[]{:S(2)}, u32[]{:S(2)}) %all-to-all-start) | async-done | bytes 393248 | tf_op jit(solution)/shard_map/all_to_all | solution.py:248
  40.7 8.8 %collective-permute-start = (bf16[512,256]{1,0:T(8,128)(2,1)S(1)}, bf16[512,256]{1,0:T(8,128)(2,1)S(1)}, u32[]{:S(2)}, u32[]{:S(2)}) collective-permute-start(bf16[512,256]{1,0:T(8,128)(2,1)S(1)} %slice_bitcast_fusion), channel_id=1, source_target_pairs={{0,64},{64,0},{1,65},{65,1},{2,66},{66,2},{3,67},{67,3},{4,68},{68... | collective-permute-start | bytes 786440 | tf_op jit(solution)/shard_map/ppermute | solution.py:250
  49.5 0.0 copy-done.4
  49.5 6.3 %shard_map.101 = (bf16[4,16,2,16,512]{4,3,2,1,0:T(8,128)(2,1)S(1)}, bf16[4,16,2,16,512]{4,3,2,1,0:T(8,128)(2,1)S(1)}) custom-call(s32[3]{0:T(128)S(1)} %pad_add_fusion.bits.refs_0_, f32[32]{0:T(128)S(1)} %reshape.35.refs_1_, bf16[128,128]{1,0:T(8,128)(2,1)S(1)} %slice_bitcast_fusion.1.refs_2_, bf16[2,128,128]{2,1,0:T(8,128)(2,1)S(1)} %copy-done.4), custom_call_target="tpu_custom_call" | custom-call | flops 2000000000 | bytes 4000000 | tf_op jit(solution)/shard_map/pallas_call | solution.py:216
  55.8 0.7 fusion.4
  56.5 15.5 %collective-permute-done = bf16[512,256]{1,0:T(8,128)(2,1)S(1)} collective-permute-done((bf16[512,256]{1,0:T(8,128)(2,1)S(1)}, bf16[512,256]{1,0:T(8,128)(2,1)S(1)}, u32[]{:S(2)}, u32[]{:S(2)}) %collective-permute-start) | collective-permute-done | bytes 262176 | tf_op jit(solution)/shard_map/ppermute | solution.py:250
  72.0 0.7 fusion
  72.7 34.3 %all_to_all.10 = bf16[64,32,256]{2,1,0:T(8,128)(2,1)S(1)} all-to-all(bf16[64,32,256]{2,1,0:T(8,128)(2,1)S(1)} %bitcast.33), channel_id=1, replica_groups=mesh['g'=4,'zh'=2,'zl'=4,'beam'=16] {'zl','beam'}, dimensions={0} | all-to-all | bytes 2097152 | tf_op jit(solution)/shard_map/all_to_all | solution.py:257
  107.0 0.7 copy.22
  107.7 1.1 %reshape.45 = bf16[2,8,2,16384]{3,2,1,0:T(2,128)(2,1)} reshape(bf16[2,8,2,2,64,128]{5,4,3,2,1,0:T(8,128)(2,1)S(1)} %bitcast.32) | data formatting | bytes 2097152 | tf_op jit(solution)/shard_map/reshape | solution.py:259
  (3 shorter events, 0.0 us)
Async XLA Ops:
  3.8 1.0 copy-start
  4.8 0.9 copy-start.1
  5.8 0.9 copy-start.2
  6.7 0.9 copy-start.3
  7.6 16.8 %copy-start.5 = (f32[4,2,2,2]{0,3,2,1:T(2,128)S(1)}, f32[4,2,2,2]{0,3,2,1:T(2,128)}, u32[]{:S(2)}) copy-start(f32[4,2,2,2]{0,3,2,1:T(2,128)} %param.14) | copy-start | bytes 388
  7.7 41.9 %copy-start.4 = (bf16[2,128,128]{2,1,0:T(8,128)(2,1)S(1)}, bf16[2,128,128]{2,1,0:T(8,128)(2,1)}, u32[]{:S(2)}) copy-start(bf16[2,128,128]{2,1,0:T(8,128)(2,1)} %constant.28.clone.refs_3_) | copy-start | bytes 196612
  11.4 29.3 %all-to-all-start = ((bf16[64,8,384]{2,1,0:T(8,128)(2,1)}), bf16[64,8,384]{2,1,0:T(8,128)(2,1)S(1)}, u32[]{:S(2)}, u32[]{:S(2)}) async-start(bf16[64,8,384]{2,1,0:T(8,128)(2,1)} %shard_map.100), calls=%async_computation | async-start | bytes 786432 | tf_op jit(solution)/shard_map/all_to_all | solution.py:248
  40.7 31.3 %collective-permute-start = (bf16[512,256]{1,0:T(8,128)(2,1)S(1)}, bf16[512,256]{1,0:T(8,128)(2,1)S(1)}, u32[]{:S(2)}, u32[]{:S(2)}) collective-permute-start(bf16[512,256]{1,0:T(8,128)(2,1)S(1)} %slice_bitcast_fusion), channel_id=1, source_target_pairs={{0,64},{64,0},{1,65},{65,1},{2,66},{66,2},{3,67},{67,3},{4,68},{68... | collective-permute-start | bytes 786440 | tf_op jit(solution)/shard_map/ppermute | solution.py:250

commit v2 on v1

--- a/solution.py
+++ b/solution.py
@@ -60,11 +60,23 @@
     return jnp.concatenate([top, jnp.concatenate([-imag_part, real_part], axis=1)], axis=0)
 
 
-def compress_kernel(bits, echo, matched, kern, packed, plus, minus, turn, out, rows):
+def compress_kernel(children, carried, bits, echo, *refs):
+    if carried:
+        packed, refs = refs[0], refs[1:]
+    matched_hbm, kern_hbm, plus_hbm, minus_hbm, turn_hbm, out = refs[:6]
+    matched, kern, plus, minus, turn, rows, filters, sems = refs[6:]
+    loads = [
+        pltpu.make_async_copy(source, target, sems.at[at])
+        for at, (source, target) in enumerate(
+            ((kern_hbm, kern), (plus_hbm, plus), (turn_hbm, turn), (minus_hbm, minus), (matched_hbm, matched))
+        )
+    ]
+    for load in loads:
+        load.start()
     count = echo.shape[0]
     width = 2 * count
-    c, s = turn[0], turn[1]
-
+
+    loads[0].wait()
     chain = complex_block(kern, 3, bits[2]).astype(F32)
     for level in (2, 1):
         high, low = split(chain)
@@ -72,10 +84,13 @@
         chain = dot(block, high) + dot(block, low)
     high, low = split(chain)
     mats = []
-    for child in range(2):
+    for child in range(children):
         block = complex_block(kern, 0, child)
         mats.append((dot(block, high) + dot(block, low)).astype(BF16))
 
+    loads[1].wait()
+    loads[2].wait()
+    c, s = turn[0], turn[1]
     signal = jnp.concatenate([echo[q].reshape(2 * FA, FA) for q in range(count)], axis=1)
     first = dot(plus[0], signal) + dot(plus[1], signal)
     stacked = []
@@ -85,11 +100,16 @@
         stacked.append(
             jnp.concatenate([real_part * c + imag_part * s, imag_part * c - real_part * s], axis=1)
         )
+    loads[3].wait()
     spectrum = dot_table(jnp.concatenate(stacked, axis=0), minus)
 
+    loads[4].wait()
+    for j in range(FA):
+        filters[0, j : j + 1, :] = matched[0:1, j * FA : (j + 1) * FA]
+        filters[1, j : j + 1, :] = matched[1:2, j * FA : (j + 1) * FA]
     scale = 1.0 / (FA * FA)
-    filter_real = jnp.transpose(matched[0]) * scale
-    filter_imag = jnp.transpose(matched[1]) * scale
+    filter_real = jnp.transpose(filters[0]) * scale
+    filter_imag = jnp.transpose(filters[1]) * scale
     stacked = []
     for q in range(count):
         real_part = spectrum[q * FA : (q + 1) * FA, :FA]
@@ -117,29 +137,51 @@
     for q in range(count):
         lanes = slice(q * FA, (q + 1) * FA)
         pair = jnp.concatenate([pulses[:FA, lanes], pulses[FA:, lanes]], axis=1)
-        turned = dot(pair, mats[q * 2 // count])
+        turned = dot(pair, mats[q * children // count])
         rows[pl.ds(2 * q, FA, stride=width), :] = turned[:, :FA]
         rows[pl.ds(2 * q + 1, FA, stride=width), :] = turned[:, FA:]
     half = FA // 2
     for part in range(2):
         piece = rows[pl.ds(part * half * width, half * width), :]
-        out[:, :, part * FA : (part + 1) * FA] = piece.reshape(half, width, FA).astype(BF16)
-    out[:, :, 2 * FA :] = jnp.broadcast_to(packed[...][None], (half, width, FA))
-
-
-def compress(bits, echo, matched, kern, packed):
-    plus, minus, turn = dft_blocks()
-    width = 2 * echo.shape[0]
+        lanes = slice(part * FA, (part + 1) * FA)
+        if carried:
+            out[:, :, lanes] = piece.reshape(half, width, FA).astype(BF16)
+        else:
+            out[:, lanes] = piece.astype(BF16)
+    if carried:
+        out[:, :, 2 * FA :] = jnp.broadcast_to(packed[...][None], (half, width, FA))
+
+
+def compress(bits, echo, matched, kern, packed=None):
+    plus, minus, turn = (jnp.asarray(table) for table in dft_blocks())
+    count = echo.shape[0]
+    width = 2 * count
+    carried = packed is not None
     vmem = pl.BlockSpec(memory_space=pltpu.VMEM)
+    shape = (FA // 2, width, 3 * FA) if carried else (FA // 2 * width, 2 * FA)
+    large = [matched, kern, plus, minus, turn]
+
+    def kernel(*refs):
+        compress_kernel(count // 2, carried, *refs)
+
     return pl.pallas_call(
-        compress_kernel,
-        out_shape=jax.ShapeDtypeStruct((FA // 2, width, 3 * FA), BF16),
-        in_specs=[pl.BlockSpec(memory_space=pltpu.SMEM)] + [vmem] * 7,
+        kernel,
+        out_shape=jax.ShapeDtypeStruct(shape, BF16),
+        in_specs=[pl.BlockSpec(memory_space=pltpu.SMEM)]
+        + [vmem] * (1 + carried)
+        + [pl.BlockSpec(memory_space=pl.ANY)] * len(large),
         out_specs=vmem,
-        scratch_shapes=[pltpu.VMEM((FA * width, FA), F32)],
-        compiler_params=pltpu.CompilerParams(vmem_limit_bytes=32 * 2**20),
-        cost_estimate=pl.CostEstimate(flops=10**9, bytes_accessed=2 * 10**6, transcendentals=0),
-    )(bits, echo, matched, kern, packed, jnp.asarray(plus), jnp.asarray(minus), jnp.asarray(turn))
+        scratch_shapes=[pltpu.VMEM(table.shape, table.dtype) for table in large]
+        + [
+            pltpu.VMEM((FA * width, FA), F32),
+            pltpu.VMEM((2, FA, FA), F32),
+            pltpu.SemaphoreType.DMA((len(large),)),
+        ],
+        compiler_params=pltpu.CompilerParams(vmem_limit_bytes=60 * 2**20),
+        cost_estimate=pl.CostEstimate(
+            flops=10**9 if carried else 5 * 10**10, bytes_accessed=2 * 10**6, transcendentals=0
+        ),
+    )(bits, echo, *([packed] if carried else []), *large)
 
 
 def beam_kernel(steer_lanes, bits, gains, packed, mixing, out_own, out_other):
@@ -233,6 +275,7 @@
     beams = pulses // own_pulses
     peers = 4 * beams
     bits = jnp.stack([zl & 1, zl >> 1, zh]).astype(jnp.int32)
+    far_bits = jnp.stack([zl & 1, zl >> 1, 1 - zh]).astype(jnp.int32)
 
     packed = jnp.concatenate(
         [
@@ -242,12 +285,25 @@
         axis=1,
     )
     packed = jnp.pad(packed, ((0, 0), (0, FA - packed.shape[1])))
+    across = [(0, 1), (1, 0)]
+    far_echoes = lax.ppermute(echoes[:1], "zh", across)
     message = compress(
-        bits, echoes.reshape(2 * own_pulses, 2, FA, FA), matched_filter.reshape(2, FA, FA), kernels, packed
+        bits, echoes.reshape(2 * own_pulses, 2, FA, FA), matched_filter, kernels, packed
     )
     arrived = lax.all_to_all(message, ("zl", "beam"), 0, 0, tiled=True)
-    own = arrived[:, :, : 2 * FA].reshape(-1, 2 * FA)
-    other = lax.ppermute(own, "zh", [(0, 1), (1, 0)])
+    own = arrived[:, :, : 2 * FA]
+    width = own.shape[1]
+    far_second = lax.ppermute(own[:, width // 2 :].reshape(-1, 2 * FA), "zh", across)
+    far_message = compress(
+        far_bits, far_echoes.reshape(own_pulses, 2, FA, FA), matched_filter, kernels
+    )
+    far_first = lax.all_to_all(
+        far_message.reshape(peers, width // 2, 2 * FA), ("zl", "beam"), 0, 0, tiled=True
+    )
+    own = own.reshape(-1, 2 * FA)
+    other = jnp.concatenate(
+        [far_first, far_second.reshape(peers, width // 2, 2 * FA)], axis=1
+    ).reshape(-1, 2 * FA)
     packed = arrived[:beams, :, 2 * FA :].reshape(-1, FA)
     near, far = beam_factors(bits, blend_gains.reshape(-1), packed, beams, own_pulses)
 

time: 109 us -> 117 us (1.073)
  waiting for transfers between devices: 31.5 us -> 16.4 us
  Pallas kernels: 9.97 us -> 17 us
  starting transfers between devices: 21.9 us -> 28.6 us
  blocking collectives: 34.3 us -> 38.6 us
  matrix products: 1.43 us -> 4.47 us
  other arithmetic: 0.86 us -> 2.63 us
    all_to_all x1, waiting for transfers between devices: 16 us -> 7.91 us  [local(): arrived = lax.all_to_all(message, ('zl', 'beam'), 0, 0, tiled=True)]
    pallas_call x1 -> x2, Pallas kernels: 3.7 us -> 10.8 us  [compress(): pl.pallas_call(kernel, out_shape=jax.ShapeDtypeStruct(shape, BF16), in_sp...]
    ppermute x1 -> x2, waiting for transfers between devices: 15.5 us -> 8.52 us  [the longest x1 8.52 us: local(): lax.ppermute(own[:, width // 2:].reshape(-1, 2 * FA), 'zh', across)]
    unnamed x14 -> x7, local copies, waits for them, and re-layouts: 4.88 us -> 0.12 us
    all_to_all x0 -> x1, starting transfers between devices: none -> 4.53 us  [local(): lax.all_to_all(far_message.reshape(peers, width // 2, 2 * FA), ('zl', 'be...]
    all_to_all x1, blocking collectives: 34.3 us -> 38.6 us  [local(): arrived = lax.all_to_all(result, ('zl', 'beam'), 0, 0, tiled=True)]
    dot_general x2, matrix products: 1.43 us -> 4.47 us  [dot(): return jnp.dot(left, right, preferred_element_type=F32)]
    ppermute x1 -> x2, starting transfers between devices: 8.82 us -> 11.6 us  [the longest x1 9.65 us: local(): far_echoes = lax.ppermute(echoes[:1], 'zh', across)]
  transfers between devices with their start and end apart: 2 -> 4, of which waited for: 2 -> 2; matrix products, arithmetic and copies ran while one was open for 1% -> 9% of each run, Pallas kernels for 6% -> 15%
where the time goes in v2:
time: 117 us; the launch traced here: 116 us
  blocking collectives  38.6 us (33%)
  starting transfers between devices  28.6 us (24%)
  Pallas kernels  17 us (15%)
  waiting for transfers between devices  16.4 us (14%)
  local copies, waits for them, and re-layouts  8.22 us (7%)
  matrix products  4.47 us (4%)
  other arithmetic  2.63 us (2%)
    all_to_all x1, blocking collectives, local(): arrived = lax.all_to_all(result, ('zl', 'beam'), 0, 0, tiled=True)  38.6 us
    all_to_all x1, starting transfers between devices, local(): arrived = lax.all_to_all(message, ('zl', 'beam'), 0, 0, tiled=True)  12.5 us
    pallas_call x2, Pallas kernels, compress(): pl.pallas_call(kernel, out_shape=jax.ShapeDtypeStruct(shape, BF16), in_sp...  10.8 us
    ppermute x1, starting transfers between devices, local(): far_echoes = lax.ppermute(echoes[:1], 'zh', across)  9.65 us
    ppermute x1, waiting for transfers between devices, local(): lax.ppermute(own[:, width // 2:].reshape(-1, 2 * FA), 'zh', across)  8.52 us
    all_to_all x1, waiting for transfers between devices, local(): arrived = lax.all_to_all(message, ('zl', 'beam'), 0, 0, tiled=True)  7.91 us
    pallas_call x1, Pallas kernels, beam_factors(): pl.pallas_call(kernel, grid=(4,), out_shape=(shape, shape), in_specs=[sme...  6.27 us
    all_to_all x1, starting transfers between devices, local(): lax.all_to_all(far_message.reshape(peers, width // 2, 2 * FA), ('zl', 'be...  4.53 us
  transfers between devices with their start and end apart: 4, of which 2 were waited for; matrix products, arithmetic and copies ran while one was open for 9% of the time, Pallas kernels for 15%

profile of v2, /device:TPU:1, one launch (start us, length us, event | category | flops | bytes accessed | tf_op | source)
XLA Modules:
  0.0 116.2 jit_solution(3570163153815570192)
XLA Ops:
  0.0 1.0 slice.15
  1.0 9.6 %collective-permute-start = (bf16[1,2,2,16384]{3,2,1,0:T(2,128)(2,1)S(1)}, bf16[1,2,2,16384]{3,2,1,0:T(2,128)(2,1)S(1)}, u32[]{:S(2)}, u32[]{:S(2)}) collective-permute-start(bf16[1,2,2,16384]{3,2,1,0:T(2,128)(2,1)S(1)} %slice.15), channel_id=1, source_target_pairs={{0,64},{64,0},{1,65},{65,1},{2,66},{66,2},{3,67},{67,3},{4,68},{68... | collective-permute-start | bytes 393224 | tf_op jit(solution)/shard_map/ppermute | solution.py:289
  10.7 1.9 %reshape.48.refs_1_ = bf16[4,2,128,128]{3,2,1,0:T(8,128)(2,1)} reshape(bf16[2,2,2,16384]{3,2,1,0:T(2,128)(2,1)} %param.13) | data formatting | bytes 524288 | tf_op jit(solution)/shard_map/reshape | solution.py:291
  12.5 0.7 convert_element_type.14
  13.2 0.1 copy.20
  13.3 0.7 copy.19
  14.0 0.1 reshape.49
  14.1 0.7 fusion.6.refs_2_
  14.7 0.6 pad_add_fusion.refs_0_
  15.3 5.7 %shard_map.127 = bf16[64,8,384]{2,1,0:T(8,128)(2,1)} custom-call(s32[3]{0:T(128)} %pad_add_fusion.refs_0_, bf16[4,2,128,128]{3,2,1,0:T(8,128)(2,1)} %reshape.48.refs_1_, bf16[8,128]{1,0:T(8,128)(2,1)} %fusion.6.refs_2_, f32[2,16384]{1,0:T(2,128)} %refs_2_.1, bf16[4,2,2,128,128]{4,3,2,1,0:T(8,128)(2,1)} %refs_3_.4, ...), custom_call_target="tpu_custom_call" | custom-call | flops 1000000000 | bytes 2000000 | tf_op jit(solution)/shard_map/pallas_call | solution.py:167
  21.0 12.5 %all-to-all-start = ((bf16[64,8,384]{2,1,0:T(8,128)(2,1)}), bf16[64,8,384]{2,1,0:T(8,128)(2,1)S(1)}, u32[]{:S(2)}, u32[]{:S(2)}) async-start(bf16[64,8,384]{2,1,0:T(8,128)(2,1)} %shard_map.127), calls=%async_computation | async-start | bytes 786432 | tf_op jit(solution)/shard_map/all_to_all | solution.py:293
  33.6 0.0 copy-done.2
  33.6 0.1 copy.18
  33.7 0.1 reshape.47.refs_1_
  33.8 0.7 pad_add_fusion.2.refs_0_
  34.5 0.0 collective-permute-done
  34.5 0.8 reshape.54.refs_1_
  35.2 5.1 %shard_map.129 = bf16[256,256]{1,0:T(8,128)(2,1)} custom-call(s32[3]{0:T(128)} %pad_add_fusion.2.refs_0_, bf16[2,2,128,128]{3,2,1,0:T(8,128)(2,1)} %reshape.54.refs_1_, f32[2,16384]{1,0:T(2,128)} %refs_2_.1, bf16[4,2,2,128,128]{4,3,2,1,0:T(8,128)(2,1)} %refs_3_.4, bf16[2,256,256]{2,1,0:T(8,128)(2,1)} %constant.25.clone.refs_5_.refs_4_, ...), custom_call_target="tpu_custom_call" | custom-call | flops 49999998976 | bytes 2000000 | tf_op jit(solution)/shard_map/pallas_call | solution.py:167
  40.3 1.6 %reshape.55 = bf16[64,4,256]{2,1,0:T(4,128)(2,1)} reshape(bf16[256,256]{1,0:T(8,128)(2,1)} %shard_map.129) | data formatting | bytes 262144 | tf_op jit(solution)/shard_map/reshape | solution.py:301
  41.9 7.9 %all-to-all-done = bf16[64,8,384]{2,1,0:T(8,128)(2,1)S(1)} async-done(((bf16[64,8,384]{2,1,0:T(8,128)(2,1)}), bf16[64,8,384]{2,1,0:T(8,128)(2,1)S(1)}, u32[]{:S(2)}, u32[]{:S(2)}) %all-to-all-start) | async-done | bytes 393248 | tf_op jit(solution)/shard_map/all_to_all | solution.py:293
  49.8 4.5 %all-to-all-start.1 = ((bf16[64,4,256]{2,1,0:T(4,128)(2,1)}), bf16[64,4,256]{2,1,0:T(4,128)(2,1)S(1)}, u32[]{:S(2)}, u32[]{:S(2)}) async-start(bf16[64,4,256]{2,1,0:T(4,128)(2,1)} %reshape.55), calls=%async_computation.1 | async-start | bytes 262144 | tf_op jit(solution)/shard_map/all_to_all | solution.py:300
  54.3 0.1 slice.19
  54.5 1.9 %collective-permute-start.1 = (bf16[256,256]{1,0:T(8,128)(2,1)S(1)}, bf16[256,256]{1,0:T(8,128)(2,1)S(1)}, u32[]{:S(2)}, u32[]{:S(2)}) collective-permute-start(bf16[256,256]{1,0:T(8,128)(2,1)S(1)} %reshape.56), channel_id=1, source_target_pairs={{0,64},{64,0},{1,65},{65,1},{2,66},{66,2},{3,67},{67,3},{4,68},{68... | collective-permute-start | bytes 393224 | tf_op jit(solution)/shard_map/ppermute | solution.py:296
  56.4 0.0 copy-done
  56.4 6.3 %shard_map.128 = (bf16[4,16,2,16,512]{4,3,2,1,0:T(8,128)(2,1)S(1)}, bf16[4,16,2,16,512]{4,3,2,1,0:T(8,128)(2,1)S(1)}) custom-call(s32[3]{0:T(128)S(1)} %copy-done, f32[32]{0:T(128)S(1)} %reshape.47.refs_1_, bf16[128,128]{1,0:T(8,128)(2,1)S(1)} %slice_bitcast_fusion.2.refs_2_, bf16[2,128,128]{2,1,0:T(8,128)(2,1)S(1)} %copy-done.1), custom_call_target="tpu_custom_call" | custom-call | flops 2000000000 | bytes 4000000 | tf_op jit(solution)/shard_map/pallas_call | solution.py:258
  62.7 2.0 %fusion.1 = f32[2048,256]{1,0:T(8,128)} fusion(bf16[2048,512]{1,0:T(8,128)(2,1)S(1)} %bitcast.27, bf16[64,8,384]{2,1,0:T(8,128)(2,1)S(1)} %all-to-all-done), kind=kOutput, calls=%fused_computation.4 | convolution fusion | flops 536870912 | bytes 4456448 | tf_op jit(solution)/shard_map/dot_general | solution.py:44
  64.8 8.5 %collective-permute-done.1 = bf16[256,256]{1,0:T(8,128)(2,1)S(1)} collective-permute-done((bf16[256,256]{1,0:T(8,128)(2,1)S(1)}, bf16[256,256]{1,0:T(8,128)(2,1)S(1)}, u32[]{:S(2)}, u32[]{:S(2)}) %collective-permute-start.1) | collective-permute-done | bytes 131104 | tf_op jit(solution)/shard_map/ppermute | solution.py:296
  73.3 0.0 all-to-all-done.1
  73.3 2.4 %fusion = bf16[2048,256]{1,0:T(8,128)(2,1)S(1)} fusion(f32[2048,256]{1,0:T(8,128)} %fusion.1, bf16[2048,512]{1,0:T(8,128)(2,1)S(1)} %bitcast.28, bf16[64,4,256]{2,1,0:T(4,128)(2,1)S(1)} %reshape.57, bf16[64,4,256]{2,1,0:T(4,128)(2,1)S(1)} %all-to-all-done.1), kind=kOutput, calls=%fused_computation.1 | convolution fusion | flops 538443776 | bytes 5505024 | tf_op jit(solution)/shard_map/dot_general | solution.py:44
  75.8 38.6 %all_to_all.15 = bf16[64,32,256]{2,1,0:T(8,128)(2,1)S(1)} all-to-all(bf16[64,32,256]{2,1,0:T(8,128)(2,1)S(1)} %bitcast.31), channel_id=1, replica_groups=mesh['g'=4,'zh'=2,'zl'=4,'beam'=16] {'zl','beam'}, dimensions={0} | all-to-all | bytes 2097152 | tf_op jit(solution)/shard_map/all_to_all | solution.py:313
  114.4 0.7 copy.23
  115.1 1.1 reshape.61
  (7 shorter events, 0.1 us)
Async XLA Ops:
  1.0 33.5 %collective-permute-start = (bf16[1,2,2,16384]{3,2,1,0:T(2,128)(2,1)S(1)}, bf16[1,2,2,16384]{3,2,1,0:T(2,128)(2,1)S(1)}, u32[]{:S(2)}, u32[]{:S(2)}) collective-permute-start(bf16[1,2,2,16384]{3,2,1,0:T(2,128)(2,1)S(1)} %slice.15), channel_id=1, source_target_pairs={{0,64},{64,0},{1,65},{65,1},{2,66},{66,2},{3,67},{67,3},{4,68},{68... | collective-permute-start | bytes 393224 | tf_op jit(solution)/shard_map/ppermute | solution.py:289
  15.3 18.2 %copy-start.2 = (f32[4,2,2,2]{0,3,2,1:T(2,128)S(1)}, f32[4,2,2,2]{0,3,2,1:T(2,128)}, u32[]{:S(2)}) copy-start(f32[4,2,2,2]{0,3,2,1:T(2,128)} %param.17) | copy-start | bytes 388
  21.0 28.8 %all-to-all-start = ((bf16[64,8,384]{2,1,0:T(8,128)(2,1)}), bf16[64,8,384]{2,1,0:T(8,128)(2,1)S(1)}, u32[]{:S(2)}, u32[]{:S(2)}) async-start(bf16[64,8,384]{2,1,0:T(8,128)(2,1)} %shard_map.127), calls=%async_computation | async-start | bytes 786432 | tf_op jit(solution)/shard_map/all_to_all | solution.py:293
  35.2 21.2 %copy-start = (s32[3]{0:T(128)S(1)}, s32[3]{0:T(128)}, u32[]{:S(2)}) copy-start(s32[3]{0:T(128)} %pad_add_fusion.refs_0_) | copy-start | bytes 40
  35.2 21.2 %copy-start.1 = (bf16[2,128,128]{2,1,0:T(8,128)(2,1)S(1)}, bf16[2,128,128]{2,1,0:T(8,128)(2,1)}, u32[]{:S(2)}) copy-start(bf16[2,128,128]{2,1,0:T(8,128)(2,1)} %constant.28.clone.refs_3_) | copy-start | bytes 196612
  49.8 23.5 %all-to-all-start.1 = ((bf16[64,4,256]{2,1,0:T(4,128)(2,1)}), bf16[64,4,256]{2,1,0:T(4,128)(2,1)S(1)}, u32[]{:S(2)}, u32[]{:S(2)}) async-start(bf16[64,4,256]{2,1,0:T(4,128)(2,1)} %reshape.55), calls=%async_computation.1 | async-start | bytes 262144 | tf_op jit(solution)/shard_map/all_to_all | solution.py:300
  54.5 18.8 %collective-permute-start.1 = (bf16[256,256]{1,0:T(8,128)(2,1)S(1)}, bf16[256,256]{1,0:T(8,128)(2,1)S(1)}, u32[]{:S(2)}, u32[]{:S(2)}) collective-permute-start(bf16[256,256]{1,0:T(8,128)(2,1)S(1)} %reshape.56), channel_id=1, source_target_pairs={{0,64},{64,0},{1,65},{65,1},{2,66},{66,2},{3,67},{67,3},{4,68},{68... | collective-permute-start | bytes 393224 | tf_op jit(solution)/shard_map/ppermute | solution.py:296

commit v3 on v2

--- a/solution.py
+++ b/solution.py
@@ -60,9 +60,7 @@
     return jnp.concatenate([top, jnp.concatenate([-imag_part, real_part], axis=1)], axis=0)
 
 
-def compress_kernel(children, carried, bits, echo, *refs):
-    if carried:
-        packed, refs = refs[0], refs[1:]
+def compress_kernel(children, bits, echo, *refs):
     matched_hbm, kern_hbm, plus_hbm, minus_hbm, turn_hbm, out = refs[:6]
     matched, kern, plus, minus, turn, rows, filters, sems = refs[6:]
     loads = [
@@ -140,35 +138,28 @@
         turned = dot(pair, mats[q * children // count])
         rows[pl.ds(2 * q, FA, stride=width), :] = turned[:, :FA]
         rows[pl.ds(2 * q + 1, FA, stride=width), :] = turned[:, FA:]
-    half = FA // 2
-    for part in range(2):
-        piece = rows[pl.ds(part * half * width, half * width), :]
-        lanes = slice(part * FA, (part + 1) * FA)
-        if carried:
-            out[:, :, lanes] = piece.reshape(half, width, FA).astype(BF16)
-        else:
-            out[:, lanes] = piece.astype(BF16)
-    if carried:
-        out[:, :, 2 * FA :] = jnp.broadcast_to(packed[...][None], (half, width, FA))
-
-
-def compress(bits, echo, matched, kern, packed=None):
+    copies, slices = out.shape[:2]
+    for part in range(FA // slices):
+        piece = rows[pl.ds(part * slices * width, slices * width), :]
+        piece = piece.reshape(slices, width, FA).astype(BF16)
+        for copy in range(copies):
+            out[copy, :, :, part * FA : (part + 1) * FA] = piece
+
+
+def compress(bits, echo, matched, kern, copies, slices):
     plus, minus, turn = (jnp.asarray(table) for table in dft_blocks())
     count = echo.shape[0]
     width = 2 * count
-    carried = packed is not None
     vmem = pl.BlockSpec(memory_space=pltpu.VMEM)
-    shape = (FA // 2, width, 3 * FA) if carried else (FA // 2 * width, 2 * FA)
     large = [matched, kern, plus, minus, turn]
 
     def kernel(*refs):
-        compress_kernel(count // 2, carried, *refs)
+        compress_kernel(2, *refs)
 
     return pl.pallas_call(
         kernel,
-        out_shape=jax.ShapeDtypeStruct(shape, BF16),
-        in_specs=[pl.BlockSpec(memory_space=pltpu.SMEM)]
-        + [vmem] * (1 + carried)
+        out_shape=jax.ShapeDtypeStruct((copies, slices, width, FA * FA // slices), BF16),
+        in_specs=[pl.BlockSpec(memory_space=pltpu.SMEM), vmem]
         + [pl.BlockSpec(memory_space=pl.ANY)] * len(large),
         out_specs=vmem,
         scratch_shapes=[pltpu.VMEM(table.shape, table.dtype) for table in large]
@@ -178,16 +169,14 @@
             pltpu.SemaphoreType.DMA((len(large),)),
         ],
         compiler_params=pltpu.CompilerParams(vmem_limit_bytes=60 * 2**20),
-        cost_estimate=pl.CostEstimate(
-            flops=10**9 if carried else 5 * 10**10, bytes_accessed=2 * 10**6, transcendentals=0
-        ),
-    )(bits, echo, *([packed] if carried else []), *large)
+        cost_estimate=pl.CostEstimate(flops=5 * 10**10, bytes_accessed=2 * 10**6, transcendentals=0),
+    )(bits, echo, *large)
 
 
 def beam_kernel(steer_lanes, bits, gains, packed, mixing, out_own, out_other):
     e3 = pl.program_id(0) // 2
     e2 = pl.program_id(0) % 2
-    e4 = bits[2]
+    e4, core = bits[2], bits[3]
     rows = packed.shape[0]
     data = packed[...]
     taps = data.astype(F32)
@@ -210,45 +199,53 @@
         after = jnp.where(jnp.logical_not(backward) & (row < rows - 1), g1, 0.0)
         return before, here, after
 
+    def by_lane(level, parity, second):
+        pair = [weights(level, child, parity) for child in range(2)]
+        return [jnp.where(second, odd, even) for even, odd in zip(*pair)]
+
     def neighbours(value):
         return pltpu.roll(value, 1, 0), value, pltpu.roll(value, rows - 1, 0)
 
     def blend(near, weight):
         return near[0] * weight[0] + near[1] * weight[1] + near[2] * weight[2]
 
-    second_child = (lane // 4) % 2 == 1
-    levels = [[weights(level, child, parity) for child in range(2)] for level, parity in ((1, e2), (2, e3), (3, e4))]
+    def of_core(value):
+        tiles = value.reshape(rows // 16, 2, 8, FA)
+        return jnp.where(core == 0, tiles[:, 0], tiles[:, 1]).reshape(rows // 2, FA)
+
+    level2 = by_lane(1, e2, lane >= FA // 2)
+    level3 = [weights(2, child, e3) for child in range(2)]
+    level4 = [[of_core(w) for w in weights(3, child, e4)] for child in range(2)]
+    imaginary = lane[: rows // 2] % 2 == 1
     for e1 in range(2):
-        pair = [weights(0, child, e1) for child in range(2)]
-        lead = [jnp.where(second_child, odd, even) for even, odd in zip(*pair)]
-        start = [blend(neighbours(dot(data, mixing[o])), lead) for o in range(2)]
-        for c2 in range(2):
-            mid = [blend(neighbours(v), levels[0][c2]) for v in start]
+        level1 = by_lane(0, e1, (lane // 4) % 2 == 1)
+        for slot, out in ((0, out_own), (1, out_other)):
+            source = jnp.where(slot == 0, core, 1 - core)
+            steer = dot(data, mixing[source])
+            second = blend(neighbours(blend(neighbours(steer), level1)), level2)
+            second = neighbours(second)
             for c3 in range(2):
-                high = [neighbours(blend(neighbours(v), levels[1][c3])) for v in mid]
-                lanes = slice((c3 * 2 + c2) * FA, (c3 * 2 + c2 + 1) * FA)
-                for own, out in ((True, out_own), (False, out_other)):
-                    weight = [
-                        jnp.where((e4 == 0) == own, zero, one) for zero, one in zip(levels[2][0], levels[2][1])
-                    ]
-                    done = [blend(near, weight).reshape(rows // 8, 8, FA) for near in high]
-                    out[0, :, e1, :, lanes] = jnp.concatenate(done, axis=1).astype(BF16)
+                third = [of_core(v) for v in neighbours(blend(second, level3[c3]))]
+                for c4 in range(2):
+                    real_row = blend(third, level4[c4])
+                    imag_row = jnp.where(
+                        imaginary, pltpu.roll(real_row, 1, 1), -pltpu.roll(real_row, FA - 1, 1)
+                    )
+                    both = [v.reshape(rows // 16, 8, FA) for v in (real_row, imag_row)]
+                    at = (c4 * 2 + c3) * FA
+                    out[0, :, e1, :, at : at + FA] = jnp.concatenate(both, axis=1).astype(BF16)
 
 
 def beam_factors(bits, gains, packed, beams, own_pulses):
     rows = packed.shape[0]
     pulses = beams * own_pulses
+    chips = beams // 2
     mixing = np.zeros((2, FA, FA), ml_dtypes.bfloat16)
-    for b in range(beams):
-        for c1 in range(2):
-            for p in range(own_pulses):
-                for i in range(2):
-                    lane = ((b * 2 + c1) * own_pulses + p) * 2 + i
-                    pulse = b * own_pulses + p
-                    mixing[0, i * pulses + pulse, lane] = -1 if i else 1
-                    mixing[1, (1 - i) * pulses + pulse, lane] = 1
-    shape = jax.ShapeDtypeStruct((4, rows // 8, 2, 16, 4 * FA), BF16)
-    spec = pl.BlockSpec((1, rows // 8, 2, 16, 4 * FA), lambda g: (g, 0, 0, 0, 0))
+    for core, c2, chip, c1, p, i in np.ndindex(2, 2, chips, 2, own_pulses, 2):
+        lane = (((c2 * chips + chip) * 2 + c1) * own_pulses + p) * 2 + i
+        mixing[core, i * pulses + (chip * 2 + core) * own_pulses + p, lane] = -1 if i else 1
+    shape = jax.ShapeDtypeStruct((4, chips, 2, 16, 4 * FA), BF16)
+    spec = pl.BlockSpec((1, chips, 2, 16, 4 * FA), lambda g: (g, 0, 0, 0, 0))
     smem = pl.BlockSpec(memory_space=pltpu.SMEM)
     vmem = pl.BlockSpec(memory_space=pltpu.VMEM)
 
@@ -273,9 +270,8 @@
     pulses = steering.shape[2]
     own_pulses = echoes.shape[1]
     beams = pulses // own_pulses
-    peers = 4 * beams
-    bits = jnp.stack([zl & 1, zl >> 1, zh]).astype(jnp.int32)
-    far_bits = jnp.stack([zl & 1, zl >> 1, 1 - zh]).astype(jnp.int32)
+    slices = 4 * beams // 2
+    bits = jnp.stack([zl & 1, zl >> 1, zh, lax.axis_index("core")]).astype(jnp.int32)
 
     packed = jnp.concatenate(
         [
@@ -285,50 +281,42 @@
         axis=1,
     )
     packed = jnp.pad(packed, ((0, 0), (0, FA - packed.shape[1])))
-    across = [(0, 1), (1, 0)]
-    far_echoes = lax.ppermute(echoes[:1], "zh", across)
+    packed = jnp.broadcast_to(packed, (beams,) + packed.shape)
+    packed = lax.all_to_all(packed, ("chip", "core"), 0, 0, tiled=True).reshape(-1, FA)
     message = compress(
-        bits, echoes.reshape(2 * own_pulses, 2, FA, FA), matched_filter, kernels, packed
+        bits, echoes.reshape(2 * own_pulses, 2, FA, FA), matched_filter, kernels, 2, slices
     )
-    arrived = lax.all_to_all(message, ("zl", "beam"), 0, 0, tiled=True)
-    own = arrived[:, :, : 2 * FA]
-    width = own.shape[1]
-    far_second = lax.ppermute(own[:, width // 2 :].reshape(-1, 2 * FA), "zh", across)
-    far_message = compress(
-        far_bits, far_echoes.reshape(own_pulses, 2, FA, FA), matched_filter, kernels
-    )
-    far_first = lax.all_to_all(
-        far_message.reshape(peers, width // 2, 2 * FA), ("zl", "beam"), 0, 0, tiled=True
-    )
-    own = own.reshape(-1, 2 * FA)
-    other = jnp.concatenate(
-        [far_first, far_second.reshape(peers, width // 2, 2 * FA)], axis=1
-    ).reshape(-1, 2 * FA)
-    packed = arrived[:beams, :, 2 * FA :].reshape(-1, FA)
+    width = message.shape[2]
+    message, packed = lax.optimization_barrier((message, packed))
+    own = lax.all_to_all(
+        message.reshape(2 * slices, width, -1), ("zh", "zl", "chip"), 0, 0, tiled=True
+    ).reshape(2 * slices * width, -1)
     near, far = beam_factors(bits, blend_gains.reshape(-1), packed, beams, own_pulses)
+    other = lax.ppermute(own, "core", [(0, 1), (1, 0)])
 
     total = dot(near.reshape(-1, 4 * FA), own)
     total = total + dot(far.reshape(-1, 4 * FA), other)
-    result = total.astype(BF16).reshape(peers, 4 * own_rows, 2 * FA)
-    arrived = lax.all_to_all(result, ("zl", "beam"), 0, 0, tiled=True)
-    arrived = arrived.reshape(peers, 2, 2, own_rows, 2, FA)
+    result = total.astype(BF16).reshape(slices, 4 * own_rows, -1)
+    arrived = lax.all_to_all(result, ("zl", "chip"), 0, 0, tiled=True)
+    arrived = arrived.reshape(slices, 2, 2, own_rows, -1, FA)
     return jnp.transpose(arrived, (1, 3, 2, 4, 0, 5)).reshape(2, own_rows, 2, -1)
 
 
 def solution(mesh):
-    fine = Mesh(mesh.devices.reshape(4, 2, 4, 16), ("g", "zh", "zl", "beam"))
+    fine = Mesh(mesh.devices.reshape(4, 2, 4, 8, 2), ("g", "zh", "zl", "chip", "core"))
     sub = ("g", "zh", "zl")
+    beam = ("chip", "core")
     return jax.shard_map(
         local,
         mesh=fine,
         in_specs=(
-            P(sub, "beam", None, None),
+            P(sub, beam, None, None),
             P(),
-            P(None, "beam", None),
+            P(None, beam, None),
             P(),
             P(),
-            P(None, None, None, "beam"),
+            P(None, None, None, beam),
         ),
-        out_specs=P(sub, "beam", None, None),
+        out_specs=P(sub, beam, None, None),
         check_vma=False,
     )

time: 117 us -> 111 us (0.949)
  the two profiles are of different devices: /device:TPU:1 before, /device:TPU:32 now
where the time goes in v3:
time: 111 us; the launch traced here: 110 us
  blocking collectives  82.6 us (74%)
  Pallas kernels  10.5 us (9%)
  starting transfers between devices  8.94 us (8%)
  local copies, waits for them, and re-layouts  5.33 us (5%)
  matrix products  1.4 us (1%)
  other arithmetic  1.38 us (1%)
    all_to_all x1, blocking collectives, local(): lax.all_to_all(message.reshape(2 * slices, width, -1), ('zh', 'zl', 'chip...  47.7 us
    all_to_all x1, blocking collectives, local(): arrived = lax.all_to_all(result, ('zl', 'chip'), 0, 0, tiled=True)  34.9 us
    all_to_all x1, starting transfers between devices, local(): lax.all_to_all(packed, ('chip', 'core'), 0, 0, tiled=True).reshape(-1, FA)  7.03 us
    pallas_call x1, Pallas kernels, compress(): pl.pallas_call(kernel, out_shape=jax.ShapeDtypeStruct((copies, slices, wi...  5.81 us
    pallas_call x1, Pallas kernels, beam_factors(): pl.pallas_call(kernel, grid=(4,), out_shape=(shape, shape), in_specs=[sme...  4.64 us
  transfers between devices with their start and end apart: 2, of which 0 were waited for; matrix products, arithmetic and copies ran while one was open for 3% of the time, Pallas kernels for 9%

profile of v3, /device:TPU:32, one launch (start us, length us, event | category | flops | bytes accessed | tf_op | source)
XLA Modules:
  0.0 110.2 jit_solution(13592074894685708642)
XLA Ops:
  0.0 0.7 convert_element_type.14
  0.7 0.1 copy.16
  0.8 0.7 copy.15
  1.5 0.1 reshape.37
  1.6 0.1 fusion.2
  1.6 0.6 broadcast_in_dim.3
  2.3 7.0 %all-to-all-start = ((bf16[16,8,128]{2,1,0:T(8,128)(2,1)}), bf16[16,8,128]{2,1,0:T(8,128)(2,1)S(1)}, u32[]{:S(2)}, u32[]{:S(2)}) async-start(bf16[16,8,128]{2,1,0:T(8,128)(2,1)} %broadcast_in_dim.3), calls=%async_computation | async-start | bytes 65536 | tf_op jit(solution)/shard_map/all_to_all | solution.py:285
  9.3 1.9 %reshape.36.refs_1_ = bf16[4,2,128,128]{3,2,1,0:T(8,128)(2,1)} reshape(bf16[2,2,2,16384]{3,2,1,0:T(2,128)(2,1)} %param.10) | data formatting | bytes 524288 | tf_op jit(solution)/shard_map/reshape | solution.py:287
  11.2 0.6 pad_add_fusion.refs_0_
  11.8 0.0 copy-start.2
  11.8 0.0 copy-start
  11.8 0.0 copy-start.1
  11.8 5.8 %shard_map.100 = bf16[2,32,8,512]{3,2,1,0:T(8,128)(2,1)} custom-call(s32[4]{0:T(128)} %pad_add_fusion.refs_0_, bf16[4,2,128,128]{3,2,1,0:T(8,128)(2,1)} %reshape.36.refs_1_, f32[2,16384]{1,0:T(2,128)} %refs_2_.1, bf16[4,2,2,128,128]{4,3,2,1,0:T(8,128)(2,1)} %refs_3_.2, bf16[2,256,256]{2,1,0:T(8,128)(2,1)} %constant.27.clone.refs_4_, ...), custom_call_target="tpu_custom_call" | custom-call | flops 49999998976 | bytes 2000000 | tf_op jit(solution)/shard_map/pallas_call | solution.py:159
  17.6 0.0 all-to-all-done
  17.6 47.7 %all_to_all.15 = bf16[64,8,512]{2,1,0:T(8,128)(2,1)S(1)} all-to-all(bf16[64,8,512]{2,1,0:T(8,128)(2,1)} %bitcast.32), channel_id=1, replica_groups=mesh['g'=4,'zh'=2,'zl'=4,'chip'=8,'core'=2] {'zh','zl','chip'}, dimensions={0} | all-to-all | bytes 1048576 | tf_op jit(solution)/shard_map/all_to_all | solution.py:291
  65.3 1.9 %collective-permute-start = (bf16[512,512]{1,0:T(8,128)(2,1)S(1)}, bf16[512,512]{1,0:T(8,128)(2,1)S(1)}, u32[]{:S(2)}, u32[]{:S(2)}) collective-permute-start(bf16[512,512]{1,0:T(8,128)(2,1)S(1)} %bitcast.31), channel_id=1, source_target_pairs={{0,1},{1,0},{2,3},{3,2},{4,5},{5,4},{6,7},{7,6},{8,9},{9,8},{10,11... | collective-permute-start | bytes 1572872 | tf_op jit(solution)/shard_map/ppermute | solution.py:295
  67.3 0.0 copy-done.2
  67.3 0.1 copy.14
  67.4 0.1 reshape.35.refs_1_
  67.5 0.0 copy-done
  67.5 0.0 copy-done.1
  67.5 4.6 %shard_map.101 = (bf16[4,8,2,16,512]{4,3,2,1,0:T(8,128)(2,1)S(1)}, bf16[4,8,2,16,512]{4,3,2,1,0:T(8,128)(2,1)S(1)}) custom-call(s32[4]{0:T(128)S(1)} %copy-done, f32[32]{0:T(128)S(1)} %reshape.35.refs_1_, bf16[128,128]{1,0:T(8,128)(2,1)S(1)} %bitcast.27, bf16[2,128,128]{2,1,0:T(8,128)(2,1)S(1)} %copy-done.1), custom_call_target="tpu_custom_call" | custom-call | flops 2000000000 | bytes 4000000 | tf_op jit(solution)/shard_map/pallas_call | solution.py:255
  72.1 0.7 fusion.3
  72.8 0.0 collective-permute-done
  72.8 0.7 add_convert_fusion
  73.6 34.9 %all_to_all.16 = bf16[32,32,512]{2,1,0:T(8,128)(2,1)S(1)} all-to-all(bf16[32,32,512]{2,1,0:T(8,128)(2,1)S(1)} %bitcast.30), channel_id=1, replica_groups=mesh['g'=4,'zh'=2,'zl'=4,'chip'=8,'core'=2] {'zl','chip'}, dimensions={0} | all-to-all | bytes 2097152 | tf_op jit(solution)/shard_map/all_to_all | solution.py:300
  108.4 0.7 copy.19
  109.1 1.1 %reshape.45 = bf16[2,8,2,16384]{3,2,1,0:T(2,128)(2,1)} reshape(bf16[2,8,2,4,32,128]{5,4,3,2,1,0:T(8,128)(2,1)S(1)} %bitcast.29) | data formatting | bytes 2097152 | tf_op jit(solution)/shard_map/reshape | solution.py:302
Async XLA Ops:
  2.3 15.3 %all-to-all-start = ((bf16[16,8,128]{2,1,0:T(8,128)(2,1)}), bf16[16,8,128]{2,1,0:T(8,128)(2,1)S(1)}, u32[]{:S(2)}, u32[]{:S(2)}) async-start(bf16[16,8,128]{2,1,0:T(8,128)(2,1)} %broadcast_in_dim.3), calls=%async_computation | async-start | bytes 65536 | tf_op jit(solution)/shard_map/all_to_all | solution.py:285
  11.8 55.5 %copy-start.2 = (f32[4,2,2,2]{0,3,2,1:T(2,128)S(1)}, f32[4,2,2,2]{0,3,2,1:T(2,128)}, u32[]{:S(2)}) copy-start(f32[4,2,2,2]{0,3,2,1:T(2,128)} %param.14) | copy-start | bytes 388
  11.8 55.7 %copy-start = (s32[4]{0:T(128)S(1)}, s32[4]{0:T(128)}, u32[]{:S(2)}) copy-start(s32[4]{0:T(128)} %pad_add_fusion.refs_0_) | copy-start | bytes 52
  11.8 55.7 %copy-start.1 = (bf16[2,128,128]{2,1,0:T(8,128)(2,1)S(1)}, bf16[2,128,128]{2,1,0:T(8,128)(2,1)}, u32[]{:S(2)}) copy-start(bf16[2,128,128]{2,1,0:T(8,128)(2,1)} %constant.30.clone.refs_3_) | copy-start | bytes 196612
  65.3 7.5 %collective-permute-start = (bf16[512,512]{1,0:T(8,128)(2,1)S(1)}, bf16[512,512]{1,0:T(8,128)(2,1)S(1)}, u32[]{:S(2)}, u32[]{:S(2)}) collective-permute-start(bf16[512,512]{1,0:T(8,128)(2,1)S(1)} %bitcast.31), channel_id=1, source_target_pairs={{0,1},{1,0},{2,3},{3,2},{4,5},{5,4},{6,7},{7,6},{8,9},{9,8},{10,11... | collective-permute-start | bytes 1572872 | tf_op jit(solution)/shard_map/ppermute | solution.py:295

commit v4 on v3

v4 whole, which is shorter than its diff:
```python
import math

import jax
import jax.numpy as jnp
import ml_dtypes
import numpy as np
from jax import lax
from jax.experimental import pallas as pl
from jax.experimental.pallas import tpu as pltpu
from jax.sharding import Mesh
from jax.sharding import PartitionSpec as P

FA = 128
LEVELS = 4
BF16 = jnp.bfloat16
F32 = jnp.float32


def halves(table):
    high = table.astype(ml_dtypes.bfloat16)
    low = (table - high.astype(np.float64)).astype(ml_dtypes.bfloat16)
    return np.stack([high, low])


def dft_blocks():
    index = np.arange(FA)
    product = index[:, None] * index[None, :]
    angle = (product % FA) * (2.0 * math.pi / FA)
    c, s = np.cos(angle), np.sin(angle)
    turn = (product % (FA * FA)) * (2.0 * math.pi / (FA * FA))
    return (
        halves(np.block([[c, s], [-s, c]])),
        halves(np.block([[c, -s], [s, c]])),
        np.stack([np.cos(turn), np.sin(turn)]).astype(np.float32),
    )


def split(value):
    high = value.astype(BF16)
    return high, (value - high.astype(F32)).astype(BF16)


def dot(left, right):
    return jnp.dot(left, right, preferred_element_type=F32)


def dot_table(value, table):
    high, low = split(value)
    return dot(high, table[0]) + dot(low, table[0]) + dot(high, table[1])


def table_dot(table, value):
    high, low = split(value)
    return dot(table[0], high) + dot(table[0], low) + dot(table[1], high)


def complex_block(ref, *index):
    real_part, imag_part = ref[(*index, 0)], ref[(*index, 1)]
    top = jnp.concatenate([real_part, imag_part], axis=1)
    return jnp.concatenate([top, jnp.concatenate([-imag_part, real_part], axis=1)], axis=0)


def range_matrices(bits, kern):
    chain = complex_block(kern, 3, bits[2]).astype(F32)
    for level in (2, 1):
        high, low = split(chain)
        block = complex_block(kern, level, bits[level - 1])
        chain = dot(block, high) + dot(block, low)
    high, low = split(chain)
    mats = []
    for child in range(2):
        block = complex_block(kern, 0, child)
        mats.append((dot(block, high) + dot(block, low)).astype(BF16))
    return mats


def forward_left(echo, plus, turn):
    count = echo.shape[0]
    c, s = turn[0], turn[1]
    signal = jnp.concatenate([echo[q].reshape(2 * FA, FA) for q in range(count)], axis=1)
    first = dot(plus[0], signal) + dot(plus[1], signal)
    stacked = []
    for q in range(count):
        real_part = first[:FA, q * FA : (q + 1) * FA]
        imag_part = first[FA:, q * FA : (q + 1) * FA]
        stacked.append(
            jnp.concatenate([real_part * c + imag_part * s, imag_part * c - real_part * s], axis=1)
        )
    return jnp.concatenate(stacked, axis=0)


def filtered(spectrum, filters):
    stacked = []
    for q in range(spectrum.shape[0] // FA):
        real_part = spectrum[q * FA : (q + 1) * FA, :FA]
        imag_part = spectrum[q * FA : (q + 1) * FA, FA:]
        stacked.append(
            jnp.concatenate(
                [
                    real_part * filters[0] - imag_part * filters[1],
                    real_part * filters[1] + imag_part * filters[0],
                ],
                axis=1,
            )
        )
    return jnp.concatenate(stacked, axis=0)


def inverse_left(back, minus, turn):
    c, s = turn[0], turn[1]
    stacked = []
    for q in range(back.shape[0] // FA):
        real_part = back[q * FA : (q + 1) * FA, :FA]
        imag_part = back[q * FA : (q + 1) * FA, FA:]
        stacked.append(
            jnp.concatenate([real_part * c - imag_part * s, imag_part * c + real_part * s], axis=0)
        )
    return table_dot(minus, jnp.concatenate(stacked, axis=1)).astype(BF16)


def times_range(pulses, mats, rows):
    count = pulses.shape[1] // FA
    for q in range(count):
        lanes = slice(q * FA, (q + 1) * FA)
        pair = jnp.concatenate([pulses[:FA, lanes], pulses[FA:, lanes]], axis=1)
        turned = dot(pair, mats[q * 2 // count])
        rows[pl.ds(2 * q, FA, stride=2 * count), :] = turned[:, :FA]
        rows[pl.ds(2 * q + 1, FA, stride=2 * count), :] = turned[:, FA:]


def own_kernel(bits, echo, matched_hbm, kern_hbm, plus_hbm, minus_hbm, turn_hbm, rows, filters, *refs):
    matched, kern, plus, minus, turn, lines, sems = refs
    loads = [
        pltpu.make_async_copy(source, target, sems.at[at])
        for at, (source, target) in enumerate(
            ((kern_hbm, kern), (plus_hbm, plus), (turn_hbm, turn), (minus_hbm, minus), (matched_hbm, matched))
        )
    ]
    for load in loads:
        load.start()
    loads[0].wait()
    mats = range_matrices(bits, kern)
    loads[1].wait()
    loads[2].wait()
    turned = forward_left(echo, plus, turn)
    loads[3].wait()
    spectrum = dot_table(turned, minus)
    loads[4].wait()
    for j in range(FA):
        lines[0, j : j + 1, :] = matched[0:1, j * FA : (j + 1) * FA]
        lines[1, j : j + 1, :] = matched[1:2, j * FA : (j + 1) * FA]
    scale = 1.0 / (FA * FA)
    filters[0] = jnp.transpose(lines[0]) * scale
    filters[1] = jnp.transpose(lines[1]) * scale
    back = dot_table(filtered(spectrum, filters), plus)
    times_range(inverse_left(back, minus, turn), mats, rows)


def far_kernel(bits, echo, near_rows, filters, kern, plus, minus, turn, out, rows):
    mats = range_matrices(bits, kern)
    spectrum = dot_table(forward_left(echo, plus, turn), minus)
    back = dot_table(filtered(spectrum, filters), plus)
    times_range(inverse_left(back, minus, turn), mats, rows)
    slices = out.shape[0]
    width = rows.shape[0] // FA
    for part in range(FA // slices):
        at = pl.ds(part * slices * width, slices * width)
        pieces = [v[at, :].reshape(slices, width, FA) for v in (near_rows, rows)]
        out[:, :, part * FA : (part + 1) * FA] = jnp.concatenate(pieces, axis=1).astype(BF16)


SMEM = pl.BlockSpec(memory_space=pltpu.SMEM)
VMEM = pl.BlockSpec(memory_space=pltpu.VMEM)
ANY = pl.BlockSpec(memory_space=pl.ANY)


def compress_own(bits, echo, matched, kern, tables):
    large = [matched, kern, *tables]
    return pl.pallas_call(
        own_kernel,
        out_shape=(
            jax.ShapeDtypeStruct((FA * 2 * echo.shape[0], FA), F32),
            jax.ShapeDtypeStruct((2, FA, FA), F32),
        ),
        in_specs=[SMEM, VMEM] + [ANY] * len(large),
        out_specs=(VMEM, VMEM),
        scratch_shapes=[pltpu.VMEM(table.shape, table.dtype) for table in large]
        + [pltpu.VMEM((2, FA, FA), F32), pltpu.SemaphoreType.DMA((len(large),))],
        compiler_params=pltpu.CompilerParams(vmem_limit_bytes=32 * 2**20),
        cost_estimate=pl.CostEstimate(flops=10**9, bytes_accessed=2 * 10**6, transcendentals=0),
    )(bits, echo, *large)


def compress_far(bits, echo, near_rows, filters, kern, tables, slices):
    width = 2 * echo.shape[0]
    return pl.pallas_call(
        far_kernel,
        out_shape=jax.ShapeDtypeStruct((slices, 2 * width, FA * FA // slices), BF16),
        in_specs=[SMEM] + [VMEM] * (4 + len(tables)),
        out_specs=VMEM,
        scratch_shapes=[pltpu.VMEM((FA * width, FA), F32)],
        compiler_params=pltpu.CompilerParams(vmem_limit_bytes=32 * 2**20),
        cost_estimate=pl.CostEstimate(flops=10**9, bytes_accessed=2 * 10**6, transcendentals=0),
    )(bits, echo, near_rows, filters, kern, *tables)


def beam_kernel(steer_lanes, bits, gains, packed, mixing, out_own, out_other):
    e3 = pl.program_id(0) // 2
    e2 = pl.program_id(0) % 2
    e4, core = bits[2], bits[3]
    rows = packed.shape[0]
    data = packed[...]
    taps = data.astype(F32)
    row = lax.broadcasted_iota(jnp.int32, (rows, FA), 0)
    lane = lax.broadcasted_iota(jnp.int32, (rows, FA), 1)

    def weights(level, child, parity):
        at = steer_lanes + (level * 2 + child) * 2
        even, odd = taps[:, at : at + 1], taps[:, at + 1 : at + 2]
        if isinstance(parity, int):
            tap = odd if parity else even
        else:
            tap = jnp.where(parity == 1, odd, even)
        tap = jnp.broadcast_to(tap, (rows, FA))
        index = ((level * 2 + child) * 2 + parity) * 2
        g0, g1 = gains[index], gains[index + 1]
        backward = tap < 0
        before = jnp.where(backward & (row > 0), g0, 0.0)
        here = jnp.where(backward, g1, g0)
        after = jnp.where(jnp.logical_not(backward) & (row < rows - 1), g1, 0.0)
        return before, here, after

    def by_lane(level, parity, second):
        pair = [weights(level, child, parity) for child in range(2)]
        return [jnp.where(second, odd, even) for even, odd in zip(*pair)]

    def neighbours(value):
        return pltpu.roll(value, 1, 0), value, pltpu.roll(value, rows - 1, 0)

    def blend(near, weight):
        return near[0] * weight[0] + near[1] * weight[1] + near[2] * weight[2]

    def of_core(value):
        tiles = value.reshape(rows // 16, 2, 8, FA)
        return jnp.where(core == 0, tiles[:, 0], tiles[:, 1]).reshape(rows // 2, FA)

    level2 = [weights(1, child, e2) for child in range(2)]
    level3 = [weights(2, child, e3) for child in range(2)]
    near_child, far_child = ([jnp.where(e4 == at, *v) for v in zip(weights(3, 0, e4), weights(3, 1, e4))] for at in (0, 1))
    level4 = [of_core(jnp.where((lane // 8) % 2 == 0, *v)) for v in zip(near_child, far_child)]
    imaginary = lane[: rows // 2] % 2 == 1
    for e1 in range(2):
        level1 = by_lane(0, e1, (lane // 4) % 2 == 1)
        for slot, out in ((0, out_own), (1, out_other)):
            source = jnp.where(slot == 0, core, 1 - core)
            first = neighbours(blend(neighbours(dot(data, mixing[source])), level1))
            for c2 in range(2):
                second = neighbours(blend(first, level2[c2]))
                for c3 in range(2):
                    third = [of_core(v) for v in neighbours(blend(second, level3[c3]))]
                    real_row = blend(third, level4)
                    imag_row = jnp.where(
                        imaginary, pltpu.roll(real_row, 1, 1), -pltpu.roll(real_row, FA - 1, 1)
                    )
                    both = [v.reshape(rows // 16, 8, FA) for v in (real_row, imag_row)]
                    at = (c3 * 2 + c2) * FA
                    out[0, :, e1, :, at : at + FA] = jnp.concatenate(both, axis=1).astype(BF16)


def beam_factors(bits, gains, packed, beams, own_pulses):
    rows = packed.shape[0]
    pulses = beams * own_pulses
    chips = beams // 2
    mixing = np.zeros((2, FA, FA), ml_dtypes.bfloat16)
    for core, chip, half, c1, p, i in np.ndindex(2, chips, 2, 2, own_pulses, 2):
        lane = (((chip * 2 + half) * 2 + c1) * own_pulses + p) * 2 + i
        mixing[core, i * pulses + (chip * 2 + core) * own_pulses + p, lane] = -1 if i else 1
    shape = jax.ShapeDtypeStruct((4, chips, 2, 16, 4 * FA), BF16)
    spec = pl.BlockSpec((1, chips, 2, 16, 4 * FA), lambda g: (g, 0, 0, 0, 0))
    def kernel(*refs):
        beam_kernel(2 * pulses, *refs)

    return pl.pallas_call(
        kernel,
        grid=(4,),
        out_shape=(shape, shape),
        in_specs=[SMEM, SMEM, VMEM, VMEM],
        out_specs=(spec, spec),
        compiler_params=pltpu.CompilerParams(vmem_limit_bytes=32 * 2**20),
        cost_estimate=pl.CostEstimate(flops=3 * 10**10, bytes_accessed=4 * 10**6, transcendentals=0),
    )(bits, gains, packed, jnp.asarray(mixing))


def local(echoes, matched_filter, steering, kernels, blend_gains, beam_taps):
    zh = lax.axis_index("zh")
    zl = lax.axis_index("zl")
    own_rows = steering.shape[1]
    pulses = steering.shape[2]
    own_pulses = echoes.shape[1]
    beams = pulses // own_pulses
    slices = 4 * beams // 2
    core = lax.axis_index("core")
    bits = jnp.stack([zl & 1, zl >> 1, zh, core]).astype(jnp.int32)
    far_bits = jnp.stack([zl & 1, zl >> 1, 1 - zh, core]).astype(jnp.int32)
    swap = [(0, 1), (1, 0)]
    tables = [jnp.asarray(table) for table in dft_blocks()]
    blocks = (2 * own_pulses, 2, FA, FA)

    far_echoes = lax.ppermute(echoes, "zh", swap)
    packed = jnp.concatenate(
        [
            jnp.moveaxis(steering, 1, 0).reshape(own_rows, 2 * pulses),
            jnp.moveaxis(beam_taps, 3, 0).reshape(own_rows, 4 * LEVELS).astype(BF16),
        ],
        axis=1,
    )
    packed = jnp.pad(packed, ((0, 0), (0, FA - packed.shape[1])))
    packed = jnp.broadcast_to(packed, (beams,) + packed.shape)
    packed = lax.all_to_all(packed, ("chip", "core"), 0, 0, tiled=True).reshape(-1, FA)
    rows, filters = compress_own(bits, echoes.reshape(blocks), matched_filter, kernels, tables)
    message = compress_far(far_bits, far_echoes.reshape(blocks), rows, filters, kernels, tables, slices)
    message, packed = lax.optimization_barrier((message, packed))
    own = lax.all_to_all(message, ("zl", "chip"), 0, 0, tiled=True)
    own = own.reshape(slices * message.shape[1], -1)
    near, far = beam_factors(bits, blend_gains.reshape(-1), packed, beams, own_pulses)
    own, near, far = lax.optimization_barrier((own, near, far))
    other = lax.ppermute(own, "core", swap)

    total = dot(near.reshape(-1, 4 * FA), own)
    total = total + dot(far.reshape(-1, 4 * FA), other)
    result = total.astype(BF16).reshape(slices, 4 * own_rows, -1)
    arrived = lax.all_to_all(result, ("zl", "chip"), 0, 0, tiled=True)
    arrived = arrived.reshape(slices, 2, 2, own_rows, -1, FA)
    return jnp.transpose(arrived, (1, 3, 2, 4, 0, 5)).reshape(2, own_rows, 2, -1)


def solution(mesh):
    fine = Mesh(mesh.devices.reshape(4, 2, 4, 8, 2), ("g", "zh", "zl", "chip", "core"))
    sub = ("g", "zh", "zl")
    beam = ("chip", "core")
    return jax.shard_map(
        local,
        mesh=fine,
        in_specs=(
            P(sub, beam, None, None),
            P(),
            P(None, beam, None),
            P(),
            P(),
            P(None, None, None, beam),
        ),
        out_specs=P(sub, beam, None, None),
        check_vma=False,
    )
```

time: 111 us -> 103 us (0.928)
  blocking collectives: 82.6 us -> 32.9 us
  starting transfers between devices: 8.94 us -> 30.5 us
  waiting for transfers between devices: 0.01 us -> 12.8 us
  local copies, waits for them, and re-layouts: 5.33 us -> 10.3 us
  Pallas kernels: 10.5 us -> 13.4 us
    all_to_all x1 -> x0, blocking collectives: 47.7 us -> none  [local(): lax.all_to_all(message.reshape(2 * slices, width, -1), ('zh', 'zl', 'chip...]
    all_to_all x0 -> x1, starting transfers between devices: none -> 12.4 us  [local(): own = lax.all_to_all(message, ('zl', 'chip'), 0, 0, tiled=True)]
    all_to_all x0 -> x1, waiting for transfers between devices: none -> 11.6 us  [local(): own = lax.all_to_all(message, ('zl', 'chip'), 0, 0, tiled=True)]
    ppermute x1 -> x2, starting transfers between devices: 1.91 us -> 11 us  [the longest x1 9.09 us: local(): far_echoes = lax.ppermute(echoes, 'zh', swap)]
    unnamed x7 -> x21, local copies, waits for them, and re-layouts: 0.12 us -> 5.57 us
    pallas_call x2 -> x3, Pallas kernels: 10.5 us -> 13.4 us  [the longest x1 5.74 us: beam_factors(): pl.pallas_call(kernel, grid=(4,), out_shape=(shape, shape), in_specs=[SME...]
    all_to_all x1, blocking collectives: 34.9 us -> 32.9 us  [local(): arrived = lax.all_to_all(result, ('zl', 'chip'), 0, 0, tiled=True)]
    ppermute x1 -> x2, waiting for transfers between devices: 0.01 us -> 1.18 us  [the longest x1 1.17 us: local(): other = lax.ppermute(own, 'core', swap)]
  transfers between devices with their start and end apart: 2 -> 4, of which waited for: 0 -> 2; matrix products, arithmetic and copies ran while one was open for 3% -> 5% of each run, Pallas kernels for 9% -> 13%
where the time goes in v4:
time: 103 us; the launch traced here: 102 us
  blocking collectives  32.9 us (32%)
  starting transfers between devices  30.5 us (30%)
  Pallas kernels  13.4 us (13%)
  waiting for transfers between devices  12.8 us (12%)
  local copies, waits for them, and re-layouts  10.3 us (10%)
  matrix products  1.4 us (1%)
    all_to_all x1, blocking collectives, local(): arrived = lax.all_to_all(result, ('zl', 'chip'), 0, 0, tiled=True)  32.9 us
    all_to_all x1, starting transfers between devices, local(): own = lax.all_to_all(message, ('zl', 'chip'), 0, 0, tiled=True)  12.4 us
    all_to_all x1, waiting for transfers between devices, local(): own = lax.all_to_all(message, ('zl', 'chip'), 0, 0, tiled=True)  11.6 us
    ppermute x1, starting transfers between devices, local(): far_echoes = lax.ppermute(echoes, 'zh', swap)  9.09 us
    all_to_all x1, starting transfers between devices, local(): lax.all_to_all(packed, ('chip', 'core'), 0, 0, tiled=True).reshape(-1, FA)  7.03 us
    pallas_call x1, Pallas kernels, beam_factors(): pl.pallas_call(kernel, grid=(4,), out_shape=(shape, shape), in_specs=[SME...  5.74 us
    unnamed x21, local copies, waits for them, and re-layouts  5.57 us
    pallas_call x1, Pallas kernels, compress_own(): pl.pallas_call(own_kernel, out_shape=(jax.ShapeDtypeStruct((FA * 2 * echo...  3.88 us
  transfers between devices with their start and end apart: 4, of which 2 were waited for; matrix products, arithmetic and copies ran while one was open for 5% of the time, Pallas kernels for 13%

profile of v4, /device:TPU:32, one launch (start us, length us, event | category | flops | bytes accessed | tf_op | source)
XLA Modules:
  0.0 102.4 jit_solution(4518946432707955370)
XLA Ops:
  0.0 9.1 %collective-permute-start = (bf16[2,2,2,16384]{3,2,1,0:T(2,128)(2,1)}, bf16[2,2,2,16384]{3,2,1,0:T(2,128)(2,1)S(1)}, u32[]{:S(2)}, u32[]{:S(2)}) collective-permute-start(bf16[2,2,2,16384]{3,2,1,0:T(2,128)(2,1)} %param.10), channel_id=1, source_target_pairs={{0,64},{64,0},{1,65},{65,1},{2,66},{66,2},{3,67},{67,3},{4,68},{68... | collective-permute-start | bytes 786440 | tf_op jit(solution)/shard_map/ppermute | solution.py:309
  9.1 0.7 convert_element_type.14
  9.8 0.1 copy.15
  9.9 0.7 copy.14
  10.6 0.1 reshape.37
  10.7 0.1 fusion.2
  10.7 0.6 broadcast_in_dim.3
  11.4 7.0 %all-to-all-start = ((bf16[16,8,128]{2,1,0:T(8,128)(2,1)}), bf16[16,8,128]{2,1,0:T(8,128)(2,1)S(1)}, u32[]{:S(2)}, u32[]{:S(2)}) async-start(bf16[16,8,128]{2,1,0:T(8,128)(2,1)} %broadcast_in_dim.3), calls=%async_computation | async-start | bytes 65536 | tf_op jit(solution)/shard_map/all_to_all | solution.py:319
  18.4 1.2 %reshape.36.echo = bf16[4,2,128,128]{3,2,1,0:T(8,128)(2,1)S(1)} reshape(bf16[2,2,2,16384]{3,2,1,0:T(2,128)(2,1)} %param.10) | data formatting | bytes 524288 | tf_op jit(solution)/shard_map/reshape | solution.py:320
  19.6 0.8 copy.16
  20.4 0.1 reshape.40.refs_1_
  20.5 0.1 add_add_fusion.1.bits.refs_0_
  20.5 1.0 %copy-done = bf16[4,2,2,128,128]{4,3,2,1,0:T(8,128)(2,1)S(1)} copy-done((bf16[4,2,2,128,128]{4,3,2,1,0:T(8,128)(2,1)S(1)}, bf16[4,2,2,128,128]{4,3,2,1,0:T(8,128)(2,1)}, u32[]{:S(2)}) %copy-start) | copy-done | bytes 524312
  21.6 0.9 copy-done.2
  22.5 0.9 copy-done.3
  23.4 0.9 copy-done.5
  24.4 0.9 copy-done.7
  25.3 3.9 %shard_map.100 = (f32[1024,128]{1,0:T(8,128)S(1)}, f32[2,128,128]{2,1,0:T(8,128)S(1)}) custom-call(s32[4]{0:T(128)S(1)} %add_add_fusion.1.bits.refs_0_, bf16[4,2,128,128]{3,2,1,0:T(8,128)(2,1)S(1)} %reshape.36.echo, f32[2,16384]{1,0:T(2,128)S(1)} %copy-done.2, bf16[4,2,2,128,128]{4,3,2,1,0:T(8,128)(2,1)S(1)} %copy-done, bf16[2,256,256]{2,1,0:T(8,128)(2,1)S(1)} %copy-done.3, ...), custom_call_target="tpu_custom_call" | custom-call | flops 1000000000 | bytes 2000000 | tf_op jit(solution)/shard_map/pallas_call | solution.py:179
  29.2 0.1 add_add_fusion.bits
  29.3 0.2 reshape.35.echo
  29.5 0.0 copy-start.9
  29.5 3.8 %shard_map.101 = bf16[32,16,512]{2,1,0:T(8,128)(2,1)} custom-call(s32[4]{0:T(128)S(1)} %add_add_fusion.bits, bf16[4,2,128,128]{3,2,1,0:T(8,128)(2,1)S(1)} %reshape.35.echo, f32[1024,128]{1,0:T(8,128)S(1)} %get-tuple-element.14.near_rows, f32[2,128,128]{2,1,0:T(8,128)S(1)} %get-tuple-element.15.filters, bf16[4,2,2,128,128]{4,3,2,1,0:T(8,128)(2,1)S(1)} %copy-done.1, ...), custom_call_target="tpu_custom_call" | custom-call | flops 1000000000 | bytes 2000000 | tf_op jit(solution)/shard_map/pallas_call | solution.py:196
  33.3 12.4 %all-to-all-start.1 = ((bf16[32,16,512]{2,1,0:T(8,128)(2,1)}), bf16[32,16,512]{2,1,0:T(8,128)(2,1)S(1)}, u32[]{:S(2)}, u32[]{:S(2)}) async-start(bf16[32,16,512]{2,1,0:T(8,128)(2,1)} %shard_map.101), calls=%async_computation.1 | async-start | bytes 1048576 | tf_op jit(solution)/shard_map/all_to_all | solution.py:323
  45.8 5.7 %shard_map.102 = (bf16[4,8,2,16,512]{4,3,2,1,0:T(8,128)(2,1)S(1)}, bf16[4,8,2,16,512]{4,3,2,1,0:T(8,128)(2,1)S(1)}) custom-call(s32[4]{0:T(128)S(1)} %add_add_fusion.1.bits.refs_0_, f32[32]{0:T(128)S(1)} %reshape.40.refs_1_, bf16[128,128]{1,0:T(8,128)(2,1)S(1)} %bitcast.26, bf16[2,128,128]{2,1,0:T(8,128)(2,1)S(1)} %copy-done.9), custom_call_target="tpu_custom_call" | custom-call | flops 30000001024 | bytes 4000000 | tf_op jit(solution)/shard_map/pallas_call | solution.py:283
  51.5 11.6 %all-to-all-done.1 = bf16[32,16,512]{2,1,0:T(8,128)(2,1)S(1)} async-done(((bf16[32,16,512]{2,1,0:T(8,128)(2,1)}), bf16[32,16,512]{2,1,0:T(8,128)(2,1)S(1)}, u32[]{:S(2)}, u32[]{:S(2)}) %all-to-all-start.1) | async-done | bytes 524320 | tf_op jit(solution)/shard_map/all_to_all | solution.py:323
  63.2 1.9 %collective-permute-start.1 = (bf16[512,512]{1,0:T(8,128)(2,1)S(1)}, bf16[512,512]{1,0:T(8,128)(2,1)S(1)}, u32[]{:S(2)}, u32[]{:S(2)}) collective-permute-start(bf16[512,512]{1,0:T(8,128)(2,1)S(1)} %bitcast.30), channel_id=1, source_target_pairs={{0,1},{1,0},{2,3},{3,2},{4,5},{5,4},{6,7},{7,6},{8,9},{9,8},{10,11... | collective-permute-start | bytes 1572872 | tf_op jit(solution)/shard_map/ppermute | solution.py:327
  65.1 0.7 fusion.3
  65.8 1.2 %collective-permute-done.1 = bf16[512,512]{1,0:T(8,128)(2,1)S(1)} collective-permute-done((bf16[512,512]{1,0:T(8,128)(2,1)S(1)}, bf16[512,512]{1,0:T(8,128)(2,1)S(1)}, u32[]{:S(2)}, u32[]{:S(2)}) %collective-permute-start.1) | collective-permute-done | bytes 524320 | tf_op jit(solution)/shard_map/ppermute | solution.py:327
  67.0 0.7 add_convert_fusion
  67.7 32.9 %all_to_all.15 = bf16[32,32,512]{2,1,0:T(8,128)(2,1)S(1)} all-to-all(bf16[32,32,512]{2,1,0:T(8,128)(2,1)S(1)} %bitcast.29), channel_id=1, replica_groups=mesh['g'=4,'zh'=2,'zl'=4,'chip'=8,'core'=2] {'zl','chip'}, dimensions={0} | all-to-all | bytes 2097152 | tf_op jit(solution)/shard_map/all_to_all | solution.py:332
  100.6 0.7 copy.19
  101.2 1.1 %reshape.45 = bf16[2,8,2,16384]{3,2,1,0:T(2,128)(2,1)} reshape(bf16[2,8,2,4,32,128]{5,4,3,2,1,0:T(8,128)(2,1)S(1)} %bitcast.28) | data formatting | bytes 2097152 | tf_op jit(solution)/shard_map/reshape | solution.py:334
  (16 shorter events, 0.0 us)
Async XLA Ops:
  0.0 29.3 %collective-permute-start = (bf16[2,2,2,16384]{3,2,1,0:T(2,128)(2,1)}, bf16[2,2,2,16384]{3,2,1,0:T(2,128)(2,1)S(1)}, u32[]{:S(2)}, u32[]{:S(2)}) collective-permute-start(bf16[2,2,2,16384]{3,2,1,0:T(2,128)(2,1)} %param.10), channel_id=1, source_target_pairs={{0,64},{64,0},{1,65},{65,1},{2,66},{66,2},{3,67},{67,3},{4,68},{68... | collective-permute-start | bytes 786440 | tf_op jit(solution)/shard_map/ppermute | solution.py:309
  11.4 22.0 %all-to-all-start = ((bf16[16,8,128]{2,1,0:T(8,128)(2,1)}), bf16[16,8,128]{2,1,0:T(8,128)(2,1)S(1)}, u32[]{:S(2)}, u32[]{:S(2)}) async-start(bf16[16,8,128]{2,1,0:T(8,128)(2,1)} %broadcast_in_dim.3), calls=%async_computation | async-start | bytes 65536 | tf_op jit(solution)/shard_map/all_to_all | solution.py:319
  20.5 1.0 %copy-start = (bf16[4,2,2,128,128]{4,3,2,1,0:T(8,128)(2,1)S(1)}, bf16[4,2,2,128,128]{4,3,2,1,0:T(8,128)(2,1)}, u32[]{:S(2)}) copy-start(bf16[4,2,2,128,128]{4,3,2,1,0:T(8,128)(2,1)} %kern.1) | copy-start | bytes 1572868
  21.6 0.9 copy-start.2
  22.5 0.9 copy-start.3
  23.4 0.9 copy-start.5
  24.4 0.9 copy-start.7
  25.3 4.2 %copy-start.1 = (bf16[4,2,2,128,128]{4,3,2,1,0:T(8,128)(2,1)S(1)}, bf16[4,2,2,128,128]{4,3,2,1,0:T(8,128)(2,1)}, u32[]{:S(2)}) copy-start(bf16[4,2,2,128,128]{4,3,2,1,0:T(8,128)(2,1)} %kern.1) | copy-start | bytes 1572868
  25.3 4.2 %copy-start.4 = (bf16[2,256,256]{2,1,0:T(8,128)(2,1)S(1)}, bf16[2,256,256]{2,1,0:T(8,128)(2,1)}, u32[]{:S(2)}) copy-start(bf16[2,256,256]{2,1,0:T(8,128)(2,1)} %constant.27.clone.plus_hbm.plus) | copy-start | bytes 786436
  25.3 4.2 %copy-start.6 = (bf16[2,256,256]{2,1,0:T(8,128)(2,1)S(1)}, bf16[2,256,256]{2,1,0:T(8,128)(2,1)}, u32[]{:S(2)}) copy-start(bf16[2,256,256]{2,1,0:T(8,128)(2,1)} %constant.28.clone.minus_hbm.minus) | copy-start | bytes 786436
  25.3 4.2 %copy-start.8 = (f32[2,128,128]{2,1,0:T(8,128)S(1)}, f32[2,128,128]{2,1,0:T(8,128)}, u32[]{:S(2)}) copy-start(f32[2,128,128]{2,1,0:T(8,128)} %constant.29.clone.turn_hbm.turn) | copy-start | bytes 393220
  29.5 16.3 %copy-start.9 = (bf16[2,128,128]{2,1,0:T(8,128)(2,1)S(1)}, bf16[2,128,128]{2,1,0:T(8,128)(2,1)}, u32[]{:S(2)}) copy-start(bf16[2,128,128]{2,1,0:T(8,128)(2,1)} %constant.30.clone.refs_3_) | copy-start | bytes 196612
  33.3 29.8 %all-to-all-start.1 = ((bf16[32,16,512]{2,1,0:T(8,128)(2,1)}), bf16[32,16,512]{2,1,0:T(8,128)(2,1)S(1)}, u32[]{:S(2)}, u32[]{:S(2)}) async-start(bf16[32,16,512]{2,1,0:T(8,128)(2,1)} %shard_map.101), calls=%async_computation.1 | async-start | bytes 1048576 | tf_op jit(solution)/shard_map/all_to_all | solution.py:323
  63.2 3.8 %collective-permute-start.1 = (bf16[512,512]{1,0:T(8,128)(2,1)S(1)}, bf16[512,512]{1,0:T(8,128)(2,1)S(1)}, u32[]{:S(2)}, u32[]{:S(2)}) collective-permute-start(bf16[512,512]{1,0:T(8,128)(2,1)S(1)} %bitcast.30), channel_id=1, source_target_pairs={{0,1},{1,0},{2,3},{3,2},{4,5},{5,4},{6,7},{7,6},{8,9},{9,8},{10,11... | collective-permute-start | bytes 1572872 | tf_op jit(solution)/shard_map/ppermute | solution.py:327

commit v5 on v4

--- a/solution.py
+++ b/solution.py
@@ -128,8 +128,15 @@
         rows[pl.ds(2 * q + 1, FA, stride=2 * count), :] = turned[:, FA:]
 
 
-def own_kernel(bits, echo, matched_hbm, kern_hbm, plus_hbm, minus_hbm, turn_hbm, rows, filters, *refs):
-    matched, kern, plus, minus, turn, lines, sems = refs
+def send_order(rows, out):
+    slices, width = out.shape[:2]
+    for part in range(FA // slices):
+        piece = rows[pl.ds(part * slices * width, slices * width), :]
+        out[:, :, part * FA : (part + 1) * FA] = piece.reshape(slices, width, FA).astype(BF16)
+
+
+def own_kernel(bits, echo, packed, matched_hbm, kern_hbm, plus_hbm, minus_hbm, turn_hbm, out, filters, *refs):
+    matched, kern, plus, minus, turn, lines, rows, sems = refs
     loads = [
         pltpu.make_async_copy(source, target, sems.at[at])
         for at, (source, target) in enumerate(
@@ -154,19 +161,17 @@
     filters[1] = jnp.transpose(lines[1]) * scale
     back = dot_table(filtered(spectrum, filters), plus)
     times_range(inverse_left(back, minus, turn), mats, rows)
-
-
-def far_kernel(bits, echo, near_rows, filters, kern, plus, minus, turn, out, rows):
+    send_order(rows, out)
+    slices, width = out.shape[:2]
+    out[:, :, out.shape[2] - FA :] = jnp.broadcast_to(packed[...][None], (slices, width, FA))
+
+
+def far_kernel(bits, echo, filters, kern, plus, minus, turn, out, rows):
     mats = range_matrices(bits, kern)
     spectrum = dot_table(forward_left(echo, plus, turn), minus)
     back = dot_table(filtered(spectrum, filters), plus)
     times_range(inverse_left(back, minus, turn), mats, rows)
-    slices = out.shape[0]
-    width = rows.shape[0] // FA
-    for part in range(FA // slices):
-        at = pl.ds(part * slices * width, slices * width)
-        pieces = [v[at, :].reshape(slices, width, FA) for v in (near_rows, rows)]
-        out[:, :, part * FA : (part + 1) * FA] = jnp.concatenate(pieces, axis=1).astype(BF16)
+    send_order(rows, out)
 
 
 SMEM = pl.BlockSpec(memory_space=pltpu.SMEM)
@@ -174,37 +179,42 @@
 ANY = pl.BlockSpec(memory_space=pl.ANY)
 
 
-def compress_own(bits, echo, matched, kern, tables):
+def compress_own(bits, echo, packed, matched, kern, tables, slices):
     large = [matched, kern, *tables]
+    width = 2 * echo.shape[0]
     return pl.pallas_call(
         own_kernel,
         out_shape=(
-            jax.ShapeDtypeStruct((FA * 2 * echo.shape[0], FA), F32),
+            jax.ShapeDtypeStruct((slices, width, FA * FA // slices + FA), BF16),
             jax.ShapeDtypeStruct((2, FA, FA), F32),
         ),
-        in_specs=[SMEM, VMEM] + [ANY] * len(large),
+        in_specs=[SMEM, VMEM, VMEM] + [ANY] * len(large),
         out_specs=(VMEM, VMEM),
         scratch_shapes=[pltpu.VMEM(table.shape, table.dtype) for table in large]
-        + [pltpu.VMEM((2, FA, FA), F32), pltpu.SemaphoreType.DMA((len(large),))],
-        compiler_params=pltpu.CompilerParams(vmem_limit_bytes=32 * 2**20),
+        + [
+            pltpu.VMEM((2, FA, FA), F32),
+            pltpu.VMEM((FA * width, FA), F32),
+            pltpu.SemaphoreType.DMA((len(large),)),
+        ],
+        compiler_params=pltpu.CompilerParams(vmem_limit_bytes=60 * 2**20),
         cost_estimate=pl.CostEstimate(flops=10**9, bytes_accessed=2 * 10**6, transcendentals=0),
-    )(bits, echo, *large)
-
-
-def compress_far(bits, echo, near_rows, filters, kern, tables, slices):
+    )(bits, echo, packed, *large)
+
+
+def compress_far(bits, echo, filters, kern, tables, slices):
     width = 2 * echo.shape[0]
     return pl.pallas_call(
         far_kernel,
-        out_shape=jax.ShapeDtypeStruct((slices, 2 * width, FA * FA // slices), BF16),
-        in_specs=[SMEM] + [VMEM] * (4 + len(tables)),
+        out_shape=jax.ShapeDtypeStruct((slices, width, FA * FA // slices), BF16),
+        in_specs=[SMEM] + [VMEM] * (3 + len(tables)),
         out_specs=VMEM,
         scratch_shapes=[pltpu.VMEM((FA * width, FA), F32)],
         compiler_params=pltpu.CompilerParams(vmem_limit_bytes=32 * 2**20),
-        cost_estimate=pl.CostEstimate(flops=10**9, bytes_accessed=2 * 10**6, transcendentals=0),
-    )(bits, echo, near_rows, filters, kern, *tables)
-
-
-def beam_kernel(steer_lanes, bits, gains, packed, mixing, out_own, out_other):
+        cost_estimate=pl.CostEstimate(flops=6 * 10**10, bytes_accessed=2 * 10**6, transcendentals=0),
+    )(bits, echo, filters, kern, *tables)
+
+
+def beam_kernel(steer_lanes, bits, gains, packed, mixing, out_near, out_far):
     e3 = pl.program_id(0) // 2
     e2 = pl.program_id(0) % 2
     e4, core = bits[2], bits[3]
@@ -244,26 +254,26 @@
         tiles = value.reshape(rows // 16, 2, 8, FA)
         return jnp.where(core == 0, tiles[:, 0], tiles[:, 1]).reshape(rows // 2, FA)
 
-    level2 = [weights(1, child, e2) for child in range(2)]
+    level2 = by_lane(1, e2, lane >= FA // 2)
     level3 = [weights(2, child, e3) for child in range(2)]
-    near_child, far_child = ([jnp.where(e4 == at, *v) for v in zip(weights(3, 0, e4), weights(3, 1, e4))] for at in (0, 1))
-    level4 = [of_core(jnp.where((lane // 8) % 2 == 0, *v)) for v in zip(near_child, far_child)]
+    pair = [weights(3, child, e4) for child in range(2)]
+    level4 = [[of_core(jnp.where(e4 == at, *v)) for v in zip(pair[0], pair[1])] for at in (0, 1)]
     imaginary = lane[: rows // 2] % 2 == 1
     for e1 in range(2):
         level1 = by_lane(0, e1, (lane // 4) % 2 == 1)
-        for slot, out in ((0, out_own), (1, out_other)):
+        for slot in range(2):
             source = jnp.where(slot == 0, core, 1 - core)
-            first = neighbours(blend(neighbours(dot(data, mixing[source])), level1))
-            for c2 in range(2):
-                second = neighbours(blend(first, level2[c2]))
-                for c3 in range(2):
-                    third = [of_core(v) for v in neighbours(blend(second, level3[c3]))]
-                    real_row = blend(third, level4)
+            second = blend(neighbours(dot(data, mixing[source])), level1)
+            second = neighbours(blend(neighbours(second), level2))
+            for c3 in range(2):
+                third = [of_core(v) for v in neighbours(blend(second, level3[c3]))]
+                for half, out in ((0, out_near), (1, out_far)):
+                    real_row = blend(third, level4[half])
                     imag_row = jnp.where(
                         imaginary, pltpu.roll(real_row, 1, 1), -pltpu.roll(real_row, FA - 1, 1)
                     )
                     both = [v.reshape(rows // 16, 8, FA) for v in (real_row, imag_row)]
-                    at = (c3 * 2 + c2) * FA
+                    at = (slot * 2 + c3) * FA
                     out[0, :, e1, :, at : at + FA] = jnp.concatenate(both, axis=1).astype(BF16)
 
 
@@ -272,8 +282,8 @@
     pulses = beams * own_pulses
     chips = beams // 2
     mixing = np.zeros((2, FA, FA), ml_dtypes.bfloat16)
-    for core, chip, half, c1, p, i in np.ndindex(2, chips, 2, 2, own_pulses, 2):
-        lane = (((chip * 2 + half) * 2 + c1) * own_pulses + p) * 2 + i
+    for core, c2, chip, c1, p, i in np.ndindex(2, 2, chips, 2, own_pulses, 2):
+        lane = (((c2 * chips + chip) * 2 + c1) * own_pulses + p) * 2 + i
         mixing[core, i * pulses + (chip * 2 + core) * own_pulses + p, lane] = -1 if i else 1
     shape = jax.ShapeDtypeStruct((4, chips, 2, 16, 4 * FA), BF16)
     spec = pl.BlockSpec((1, chips, 2, 16, 4 * FA), lambda g: (g, 0, 0, 0, 0))
@@ -315,19 +325,30 @@
         axis=1,
     )
     packed = jnp.pad(packed, ((0, 0), (0, FA - packed.shape[1])))
-    packed = jnp.broadcast_to(packed, (beams,) + packed.shape)
-    packed = lax.all_to_all(packed, ("chip", "core"), 0, 0, tiled=True).reshape(-1, FA)
-    rows, filters = compress_own(bits, echoes.reshape(blocks), matched_filter, kernels, tables)
-    message = compress_far(far_bits, far_echoes.reshape(blocks), rows, filters, kernels, tables, slices)
-    message, packed = lax.optimization_barrier((message, packed))
-    own = lax.all_to_all(message, ("zl", "chip"), 0, 0, tiled=True)
-    own = own.reshape(slices * message.shape[1], -1)
-    near, far = beam_factors(bits, blend_gains.reshape(-1), packed, beams, own_pulses)
-    own, near, far = lax.optimization_barrier((own, near, far))
-    other = lax.ppermute(own, "core", swap)
-
-    total = dot(near.reshape(-1, 4 * FA), own)
-    total = total + dot(far.reshape(-1, 4 * FA), other)
+    message, filters = compress_own(
+        bits, echoes.reshape(blocks), packed, matched_filter, kernels, tables, slices
+    )
+    far_message = compress_far(far_bits, far_echoes.reshape(blocks), filters, kernels, tables, slices)
+    arrived = lax.all_to_all(message, ("zl", "chip"), 0, 0, tiled=True)
+    far_message, arrived = lax.optimization_barrier((far_message, arrived))
+    far_own = lax.all_to_all(far_message, ("zl", "chip"), 0, 0, tiled=True)
+
+    arrived = arrived.reshape(-1, arrived.shape[2])
+    swapped = lax.ppermute(arrived, "core", swap)
+    split_at = arrived.shape[1] - FA
+    chips = beams // 2
+    packed = [v[: chips * own_rows, split_at:].reshape(chips, own_rows, FA) for v in (arrived, swapped)]
+    packed = jnp.where(core == 0, jnp.stack(packed, axis=1), jnp.stack(packed[::-1], axis=1))
+    near, far = beam_factors(
+        bits, blend_gains.reshape(-1), packed.reshape(-1, FA), beams, own_pulses
+    )
+    near, far = (v.reshape(-1, 4 * FA) for v in (near, far))
+    total = dot(near[:, : 2 * FA], arrived[:, :split_at]) + dot(near[:, 2 * FA :], swapped[:, :split_at])
+
+    far_own, total, far = lax.optimization_barrier((far_own.reshape(-1, split_at), total, far))
+    far_swapped = lax.ppermute(far_own, "core", swap)
+    total = total + dot(far[:, : 2 * FA], far_own)
+    total = total + dot(far[:, 2 * FA :], far_swapped)
     result = total.astype(BF16).reshape(slices, 4 * own_rows, -1)
     arrived = lax.all_to_all(result, ("zl", "chip"), 0, 0, tiled=True)
     arrived = arrived.reshape(slices, 2, 2, own_rows, -1, FA)

time: 103 us -> 102 us (level)
  local copies, waits for them, and re-layouts: 10.3 us -> 6.39 us
  waiting for transfers between devices: 12.8 us -> 15.7 us
  starting transfers between devices: 30.5 us -> 29 us
  other arithmetic: 0.94 us -> 2.04 us
    unnamed x21, local copies, waits for them, and re-layouts: 5.57 us -> 1.58 us
    all_to_all x2, starting transfers between devices: 19.5 us -> 16.1 us  [the longest x1 11.3 us: local(): arrived = lax.all_to_all(message, ('zl', 'chip'), 0, 0, tiled=True)]
    all_to_all x2, waiting for transfers between devices: 11.7 us -> 14.6 us  [the longest x1 8.02 us: local(): arrived = lax.all_to_all(message, ('zl', 'chip'), 0, 0, tiled=True)]
    ppermute x1 -> x2, starting transfers between devices: 1.91 us -> 3.82 us  [the longest x1 1.91 us: local(): swapped = lax.ppermute(arrived, 'core', swap)]
    pallas_call x2, Pallas kernels: 7.67 us -> 9.43 us  [the longest x1 5.77 us: compress_own(): pl.pallas_call(own_kernel, out_shape=(jax.ShapeDtypeStruct((slices, width...]
  transfers between devices with their start and end apart: 4 -> 5, of which waited for: 2 -> 3; matrix products, arithmetic and copies ran while one was open for 5% -> 6% of each run, Pallas kernels for 13% -> 14%
where the time goes in v5:
time: 102 us
  blocking collectives  32.6 us (32%)
  starting transfers between devices  29 us (28%)
  waiting for transfers between devices  15.7 us (15%)
  Pallas kernels  14.2 us (14%)
  local copies, waits for them, and re-layouts  6.39 us (6%)
  other arithmetic  2.04 us (2%)
  matrix products  1.77 us (2%)
    all_to_all x1, blocking collectives, local(): arrived = lax.all_to_all(result, ('zl', 'chip'), 0, 0, tiled=True)  32.6 us
    all_to_all x1, starting transfers between devices, local(): arrived = lax.all_to_all(message, ('zl', 'chip'), 0, 0, tiled=True)  11.3 us
    ppermute x1, starting transfers between devices, local(): far_echoes = lax.ppermute(echoes, 'zh', swap)  9.09 us
    all_to_all x1, waiting for transfers between devices, local(): arrived = lax.all_to_all(message, ('zl', 'chip'), 0, 0, tiled=True)  8.02 us
    all_to_all x1, waiting for transfers between devices, local(): far_own = lax.all_to_all(far_message, ('zl', 'chip'), 0, 0, tiled=True)  6.62 us
    pallas_call x1, Pallas kernels, compress_own(): pl.pallas_call(own_kernel, out_shape=(jax.ShapeDtypeStruct((slices, width...  5.77 us
    all_to_all x1, starting transfers between devices, local(): far_own = lax.all_to_all(far_message, ('zl', 'chip'), 0, 0, tiled=True)  4.84 us
    pallas_call x1, Pallas kernels, beam_factors(): pl.pallas_call(kernel, grid=(4,), out_shape=(shape, shape), in_specs=[SME...  4.72 us
  transfers between devices with their start and end apart: 5, of which 3 were waited for; matrix products, arithmetic and copies ran while one was open for 6% of the time, Pallas kernels for 14%

profile of v5, /device:TPU:32, one launch (start us, length us, event | category | flops | bytes accessed | tf_op | source)
XLA Modules:
  0.0 101.9 jit_solution(5647463638245884448)
XLA Ops:
  0.0 9.1 %collective-permute-start = (bf16[2,2,2,16384]{3,2,1,0:T(2,128)(2,1)}, bf16[2,2,2,16384]{3,2,1,0:T(2,128)(2,1)S(1)}, u32[]{:S(2)}, u32[]{:S(2)}) collective-permute-start(bf16[2,2,2,16384]{3,2,1,0:T(2,128)(2,1)} %param.10), channel_id=1, source_target_pairs={{0,64},{64,0},{1,65},{65,1},{2,66},{66,2},{3,67},{67,3},{4,68},{68... | collective-permute-start | bytes 786440 | tf_op jit(solution)/shard_map/ppermute | solution.py:319
  9.1 0.7 copy.15
  9.8 0.1 reshape.42
  9.9 0.7 convert_element_type.14
  10.6 0.1 copy.16
  10.7 0.7 fusion.10.packed
  11.3 0.6 add_add_fusion.1.bits.refs_0_
  11.9 1.9 %reshape.41.echo = bf16[4,2,128,128]{3,2,1,0:T(8,128)(2,1)} reshape(bf16[2,2,2,16384]{3,2,1,0:T(2,128)(2,1)} %param.10) | data formatting | bytes 524288 | tf_op jit(solution)/shard_map/reshape | solution.py:329
  13.8 5.8 %shard_map.100 = (bf16[32,8,640]{2,1,0:T(8,128)(2,1)}, f32[2,128,128]{2,1,0:T(8,128)}) custom-call(s32[4]{0:T(128)} %add_add_fusion.1.bits.refs_0_, bf16[4,2,128,128]{3,2,1,0:T(8,128)(2,1)} %reshape.41.echo, bf16[8,128]{1,0:T(8,128)(2,1)} %fusion.10.packed, f32[2,16384]{1,0:T(2,128)} %matched_hbm.1, bf16[4,2,2,128,128]{4,3,2,1,0:T(8,128)(2,1)} %kern.1, ...), custom_call_target="tpu_custom_call" | custom-call | flops 1000000000 | bytes 2000000 | tf_op jit(solution)/shard_map/pallas_call | solution.py:185
  19.6 11.3 %all-to-all-start = ((bf16[32,8,640]{2,1,0:T(8,128)(2,1)}), bf16[32,8,640]{2,1,0:T(8,128)(2,1)S(1)}, u32[]{:S(2)}, u32[]{:S(2)}) async-start(bf16[32,8,640]{2,1,0:T(8,128)(2,1)} %get-tuple-element.15), calls=%async_computation | async-start | bytes 655360 | tf_op jit(solution)/shard_map/all_to_all | solution.py:332
  30.8 0.1 add_add_fusion.bits
  30.9 0.2 reshape.40.echo
  31.2 0.9 copy-done.6
  32.1 3.7 %shard_map.101 = bf16[32,8,512]{2,1,0:T(8,128)(2,1)} custom-call(s32[4]{0:T(128)S(1)} %add_add_fusion.bits, bf16[4,2,128,128]{3,2,1,0:T(8,128)(2,1)S(1)} %reshape.40.echo, f32[2,128,128]{2,1,0:T(8,128)S(1)} %copy-done.6, bf16[4,2,2,128,128]{4,3,2,1,0:T(8,128)(2,1)S(1)} %copy-done.1, bf16[2,256,256]{2,1,0:T(8,128)(2,1)S(1)} %copy-done.3, ...), custom_call_target="tpu_custom_call" | custom-call | flops 60000002048 | bytes 2000000 | tf_op jit(solution)/shard_map/pallas_call | solution.py:206
  35.8 8.0 %all-to-all-done = bf16[32,8,640]{2,1,0:T(8,128)(2,1)S(1)} async-done(((bf16[32,8,640]{2,1,0:T(8,128)(2,1)}), bf16[32,8,640]{2,1,0:T(8,128)(2,1)S(1)}, u32[]{:S(2)}, u32[]{:S(2)}) %all-to-all-start) | async-done | bytes 327712 | tf_op jit(solution)/shard_map/all_to_all | solution.py:332
  43.8 1.9 %collective-permute-start.1 = (bf16[256,640]{1,0:T(8,128)(2,1)S(1)}, bf16[256,640]{1,0:T(8,128)(2,1)S(1)}, u32[]{:S(2)}, u32[]{:S(2)}) collective-permute-start(bf16[256,640]{1,0:T(8,128)(2,1)S(1)} %bitcast.35), channel_id=1, source_target_pairs={{0,1},{1,0},{2,3},{3,2},{4,5},{5,4},{6,7},{7,6},{8,9},{9,8},{10,11... | collective-permute-start | bytes 983048 | tf_op jit(solution)/shard_map/ppermute | solution.py:337
  45.7 0.1 copy.17
  45.8 0.1 reshape.44.refs_1_
  45.9 4.8 %all-to-all-start.1 = ((bf16[32,8,512]{2,1,0:T(8,128)(2,1)}), bf16[32,8,512]{2,1,0:T(8,128)(2,1)S(1)}, u32[]{:S(2)}, u32[]{:S(2)}) async-start(bf16[32,8,512]{2,1,0:T(8,128)(2,1)} %shard_map.101), calls=%async_computation.1 | async-start | bytes 524288 | tf_op jit(solution)/shard_map/all_to_all | solution.py:334
  50.8 4.7 %shard_map.102 = (bf16[4,8,2,16,512]{4,3,2,1,0:T(8,128)(2,1)S(1)}, bf16[4,8,2,16,512]{4,3,2,1,0:T(8,128)(2,1)S(1)}) custom-call(s32[4]{0:T(128)S(1)} %copy-done, f32[32]{0:T(128)S(1)} %reshape.44.refs_1_, bf16[128,128]{1,0:T(8,128)(2,1)S(1)} %bitcast.31, bf16[2,128,128]{2,1,0:T(8,128)(2,1)S(1)} %copy-done.5), custom_call_target="tpu_custom_call" | custom-call | flops 30000001024 | bytes 4000000 | tf_op jit(solution)/shard_map/pallas_call | solution.py:293
  55.6 0.0 copy-start.8
  55.6 0.4 fusion.1
  56.0 0.5 copy-done.8
  56.6 0.4 convolution_add_fusion
  57.0 6.6 %all-to-all-done.1 = bf16[32,8,512]{2,1,0:T(8,128)(2,1)S(1)} async-done(((bf16[32,8,512]{2,1,0:T(8,128)(2,1)}), bf16[32,8,512]{2,1,0:T(8,128)(2,1)S(1)}, u32[]{:S(2)}, u32[]{:S(2)}) %all-to-all-start.1) | async-done | bytes 262176 | tf_op jit(solution)/shard_map/all_to_all | solution.py:334
  63.6 1.9 %collective-permute-start.2 = (bf16[256,512]{1,0:T(8,128)(2,1)S(1)}, bf16[256,512]{1,0:T(8,128)(2,1)S(1)}, u32[]{:S(2)}, u32[]{:S(2)}) collective-permute-start(bf16[256,512]{1,0:T(8,128)(2,1)S(1)} %bitcast.38), channel_id=1, source_target_pairs={{0,1},{1,0},{2,3},{3,2},{4,5},{5,4},{6,7},{7,6},{8,9},{9,8},{10,11... | collective-permute-start | bytes 786440 | tf_op jit(solution)/shard_map/ppermute | solution.py:349
  65.5 0.4 fusion.4
  66.0 1.1 %collective-permute-done.2 = bf16[256,512]{1,0:T(8,128)(2,1)S(1)} collective-permute-done((bf16[256,512]{1,0:T(8,128)(2,1)S(1)}, bf16[256,512]{1,0:T(8,128)(2,1)S(1)}, u32[]{:S(2)}, u32[]{:S(2)}) %collective-permute-start.2) | collective-permute-done | bytes 262176 | tf_op jit(solution)/shard_map/ppermute | solution.py:349
  67.0 0.5 add_convert_fusion
  67.5 32.6 %all_to_all.15 = bf16[32,32,512]{2,1,0:T(8,128)(2,1)S(1)} all-to-all(bf16[32,32,512]{2,1,0:T(8,128)(2,1)S(1)} %bitcast.34), channel_id=1, replica_groups=mesh['g'=4,'zh'=2,'zl'=4,'chip'=8,'core'=2] {'zl','chip'}, dimensions={0} | all-to-all | bytes 2097152 | tf_op jit(solution)/shard_map/all_to_all | solution.py:353
  100.1 0.7 copy.20
  100.8 1.1 %reshape.50 = bf16[2,8,2,16384]{3,2,1,0:T(2,128)(2,1)} reshape(bf16[2,8,2,4,32,128]{5,4,3,2,1,0:T(8,128)(2,1)S(1)} %bitcast.33) | data formatting | bytes 2097152 | tf_op jit(solution)/shard_map/reshape | solution.py:355
  (22 shorter events, 0.1 us)
Async XLA Ops:
  0.0 30.9 %collective-permute-start = (bf16[2,2,2,16384]{3,2,1,0:T(2,128)(2,1)}, bf16[2,2,2,16384]{3,2,1,0:T(2,128)(2,1)S(1)}, u32[]{:S(2)}, u32[]{:S(2)}) collective-permute-start(bf16[2,2,2,16384]{3,2,1,0:T(2,128)(2,1)} %param.10), channel_id=1, source_target_pairs={{0,64},{64,0},{1,65},{65,1},{2,66},{66,2},{3,67},{67,3},{4,68},{68... | collective-permute-start | bytes 786440 | tf_op jit(solution)/shard_map/ppermute | solution.py:319
  13.8 17.4 %copy-start.1 = (bf16[4,2,2,128,128]{4,3,2,1,0:T(8,128)(2,1)S(1)}, bf16[4,2,2,128,128]{4,3,2,1,0:T(8,128)(2,1)}, u32[]{:S(2)}) copy-start(bf16[4,2,2,128,128]{4,3,2,1,0:T(8,128)(2,1)} %kern.1) | copy-start | bytes 1572868
  13.8 17.4 %copy-start.2 = (bf16[2,256,256]{2,1,0:T(8,128)(2,1)S(1)}, bf16[2,256,256]{2,1,0:T(8,128)(2,1)}, u32[]{:S(2)}) copy-start(bf16[2,256,256]{2,1,0:T(8,128)(2,1)} %constant.29.clone.minus_hbm.minus) | copy-start | bytes 786436
  13.8 17.4 %copy-start.3 = (bf16[2,256,256]{2,1,0:T(8,128)(2,1)S(1)}, bf16[2,256,256]{2,1,0:T(8,128)(2,1)}, u32[]{:S(2)}) copy-start(bf16[2,256,256]{2,1,0:T(8,128)(2,1)} %constant.28.clone.plus_hbm.plus) | copy-start | bytes 786436
  13.8 17.4 %copy-start.4 = (f32[2,128,128]{2,1,0:T(8,128)S(1)}, f32[2,128,128]{2,1,0:T(8,128)}, u32[]{:S(2)}) copy-start(f32[2,128,128]{2,1,0:T(8,128)} %constant.30.clone.turn_hbm.turn) | copy-start | bytes 393220
  19.6 24.2 %all-to-all-start = ((bf16[32,8,640]{2,1,0:T(8,128)(2,1)}), bf16[32,8,640]{2,1,0:T(8,128)(2,1)S(1)}, u32[]{:S(2)}, u32[]{:S(2)}) async-start(bf16[32,8,640]{2,1,0:T(8,128)(2,1)} %get-tuple-element.15), calls=%async_computation | async-start | bytes 655360 | tf_op jit(solution)/shard_map/all_to_all | solution.py:332
  31.2 0.9 copy-start.6
  32.1 13.6 %copy-start.9 = (f32[4,2,2,2]{0,3,2,1:T(2,128)S(1)}, f32[4,2,2,2]{0,3,2,1:T(2,128)}, u32[]{:S(2)}) copy-start(f32[4,2,2,2]{0,3,2,1:T(2,128)} %param.14) | copy-start | bytes 388
  32.1 18.7 %copy-start = (s32[4]{0:T(128)S(1)}, s32[4]{0:T(128)}, u32[]{:S(2)}) copy-start(s32[4]{0:T(128)} %add_add_fusion.1.bits.refs_0_) | copy-start | bytes 52
  32.1 18.7 %copy-start.5 = (bf16[2,128,128]{2,1,0:T(8,128)(2,1)S(1)}, bf16[2,128,128]{2,1,0:T(8,128)(2,1)}, u32[]{:S(2)}) copy-start(bf16[2,128,128]{2,1,0:T(8,128)(2,1)} %constant.31.clone.refs_3_) | copy-start | bytes 196612
  43.8 7.0 %collective-permute-start.1 = (bf16[256,640]{1,0:T(8,128)(2,1)S(1)}, bf16[256,640]{1,0:T(8,128)(2,1)S(1)}, u32[]{:S(2)}, u32[]{:S(2)}) collective-permute-start(bf16[256,640]{1,0:T(8,128)(2,1)S(1)} %bitcast.35), channel_id=1, source_target_pairs={{0,1},{1,0},{2,3},{3,2},{4,5},{5,4},{6,7},{7,6},{8,9},{9,8},{10,11... | collective-permute-start | bytes 983048 | tf_op jit(solution)/shard_map/ppermute | solution.py:337
  45.9 17.7 %all-to-all-start.1 = ((bf16[32,8,512]{2,1,0:T(8,128)(2,1)}), bf16[32,8,512]{2,1,0:T(8,128)(2,1)S(1)}, u32[]{:S(2)}, u32[]{:S(2)}) async-start(bf16[32,8,512]{2,1,0:T(8,128)(2,1)} %shard_map.101), calls=%async_computation.1 | async-start | bytes 524288 | tf_op jit(solution)/shard_map/all_to_all | solution.py:334
  50.8 4.8 %copy-start.7 = (bf16[256,640]{1,0:T(8,128)(2,1)}, bf16[256,640]{1,0:T(8,128)(2,1)S(1)}, u32[]{:S(2)}) copy-start(bf16[256,640]{1,0:T(8,128)(2,1)S(1)} %collective-permute-done.1) | copy-start | bytes 983044
  55.6 1.0 copy-start.8
  63.6 3.4 %collective-permute-start.2 = (bf16[256,512]{1,0:T(8,128)(2,1)S(1)}, bf16[256,512]{1,0:T(8,128)(2,1)S(1)}, u32[]{:S(2)}, u32[]{:S(2)}) collective-permute-start(bf16[256,512]{1,0:T(8,128)(2,1)S(1)} %bitcast.38), channel_id=1, source_target_pairs={{0,1},{1,0},{2,3},{3,2},{4,5},{5,4},{6,7},{7,6},{8,9},{9,8},{10,11... | collective-permute-start | bytes 786440 | tf_op jit(solution)/shard_map/ppermute | solution.py:349

commit v6 on v5

--- a/solution.py
+++ b/solution.py
@@ -58,6 +58,11 @@
     real_part, imag_part = ref[(*index, 0)], ref[(*index, 1)]
     top = jnp.concatenate([real_part, imag_part], axis=1)
     return jnp.concatenate([top, jnp.concatenate([-imag_part, real_part], axis=1)], axis=0)
+
+
+def place_bits(place):
+    value = place[0]
+    return (value >> 1) & 1, (value >> 2) & 1, (value >> 3) & 1, value & 1
 
 
 def range_matrices(bits, kern):
@@ -135,24 +140,40 @@
         out[:, :, part * FA : (part + 1) * FA] = piece.reshape(slices, width, FA).astype(BF16)
 
 
-def own_kernel(bits, echo, packed, matched_hbm, kern_hbm, plus_hbm, minus_hbm, turn_hbm, out, filters, *refs):
-    matched, kern, plus, minus, turn, lines, rows, sems = refs
+def own_kernel(
+    place, steer, taps, echo_hbm, matched_hbm, kern_hbm, plus_hbm, minus_hbm, turn_hbm, out, filters, *refs
+):
+    echo, matched, kern, plus, minus, turn, lines, rows, packed, sems = refs
     loads = [
         pltpu.make_async_copy(source, target, sems.at[at])
         for at, (source, target) in enumerate(
-            ((kern_hbm, kern), (plus_hbm, plus), (turn_hbm, turn), (minus_hbm, minus), (matched_hbm, matched))
+            (
+                (kern_hbm, kern),
+                (plus_hbm, plus),
+                (echo_hbm, echo),
+                (turn_hbm, turn),
+                (minus_hbm, minus),
+                (matched_hbm, matched),
+            )
         )
     ]
     for load in loads:
         load.start()
+    packed[...] = jnp.zeros_like(packed)
+    count, span = steer.shape[1], steer.shape[2]
+    for i in range(2):
+        packed[:, i * span : (i + 1) * span] = steer[i].astype(F32)
+    for level, child, parity in np.ndindex(*taps.shape[:3]):
+        row, lane = level * 2 + child, 2 * span + parity * count
+        packed[row : row + 1, lane : lane + count] = taps[level, child, parity : parity + 1, :].astype(F32)
     loads[0].wait()
-    mats = range_matrices(bits, kern)
-    loads[1].wait()
-    loads[2].wait()
+    mats = range_matrices(place_bits(place), kern)
+    for load in loads[1:4]:
+        load.wait()
     turned = forward_left(echo, plus, turn)
-    loads[3].wait()
+    loads[4].wait()
     spectrum = dot_table(turned, minus)
-    loads[4].wait()
+    loads[5].wait()
     for j in range(FA):
         lines[0, j : j + 1, :] = matched[0:1, j * FA : (j + 1) * FA]
         lines[1, j : j + 1, :] = matched[1:2, j * FA : (j + 1) * FA]
@@ -163,12 +184,16 @@
     times_range(inverse_left(back, minus, turn), mats, rows)
     send_order(rows, out)
     slices, width = out.shape[:2]
-    out[:, :, out.shape[2] - FA :] = jnp.broadcast_to(packed[...][None], (slices, width, FA))
-
-
-def far_kernel(bits, echo, filters, kern, plus, minus, turn, out, rows):
-    mats = range_matrices(bits, kern)
+    out[:, :, out.shape[2] - FA :] = jnp.broadcast_to(packed[...].astype(BF16)[None], (slices, width, FA))
+
+
+def far_kernel(place, echo, filters_hbm, kern, plus, minus, turn, out, rows, filters, sem):
+    load = pltpu.make_async_copy(filters_hbm, filters, sem)
+    load.start()
+    low, middle, high, _ = place_bits(place)
+    mats = range_matrices((low, middle, 1 - high), kern)
     spectrum = dot_table(forward_left(echo, plus, turn), minus)
+    load.wait()
     back = dot_table(filtered(spectrum, filters), plus)
     times_range(inverse_left(back, minus, turn), mats, rows)
     send_order(rows, out)
@@ -179,8 +204,8 @@
 ANY = pl.BlockSpec(memory_space=pl.ANY)
 
 
-def compress_own(bits, echo, packed, matched, kern, tables, slices):
-    large = [matched, kern, *tables]
+def compress_own(place, steering, taps, echo, matched, kern, tables, slices):
+    large = [echo, matched, kern, *tables]
     width = 2 * echo.shape[0]
     return pl.pallas_call(
         own_kernel,
@@ -194,30 +219,35 @@
         + [
             pltpu.VMEM((2, FA, FA), F32),
             pltpu.VMEM((FA * width, FA), F32),
+            pltpu.VMEM((8, FA), F32),
             pltpu.SemaphoreType.DMA((len(large),)),
         ],
         compiler_params=pltpu.CompilerParams(vmem_limit_bytes=60 * 2**20),
         cost_estimate=pl.CostEstimate(flops=10**9, bytes_accessed=2 * 10**6, transcendentals=0),
-    )(bits, echo, packed, *large)
-
-
-def compress_far(bits, echo, filters, kern, tables, slices):
+    )(place, steering, taps, *large)
+
+
+def compress_far(place, echo, filters, kern, tables, slices):
     width = 2 * echo.shape[0]
     return pl.pallas_call(
         far_kernel,
         out_shape=jax.ShapeDtypeStruct((slices, width, FA * FA // slices), BF16),
-        in_specs=[SMEM] + [VMEM] * (3 + len(tables)),
+        in_specs=[SMEM, VMEM, ANY] + [VMEM] * (1 + len(tables)),
         out_specs=VMEM,
-        scratch_shapes=[pltpu.VMEM((FA * width, FA), F32)],
+        scratch_shapes=[
+            pltpu.VMEM((FA * width, FA), F32),
+            pltpu.VMEM(filters.shape, F32),
+            pltpu.SemaphoreType.DMA,
+        ],
         compiler_params=pltpu.CompilerParams(vmem_limit_bytes=32 * 2**20),
         cost_estimate=pl.CostEstimate(flops=6 * 10**10, bytes_accessed=2 * 10**6, transcendentals=0),
-    )(bits, echo, filters, kern, *tables)
-
-
-def beam_kernel(steer_lanes, bits, gains, packed, mixing, out_near, out_far):
+    )(place, echo, filters, kern, *tables)
+
+
+def beam_kernel(steer_lanes, place, gains, packed, mixing, out_near, out_far):
     e3 = pl.program_id(0) // 2
     e2 = pl.program_id(0) % 2
-    e4, core = bits[2], bits[3]
+    _, _, e4, core = place_bits(place)
     rows = packed.shape[0]
     data = packed[...]
     taps = data.astype(F32)
@@ -277,7 +307,7 @@
                     out[0, :, e1, :, at : at + FA] = jnp.concatenate(both, axis=1).astype(BF16)
 
 
-def beam_factors(bits, gains, packed, beams, own_pulses):
+def beam_factors(place, gains, packed, beams, own_pulses):
     rows = packed.shape[0]
     pulses = beams * own_pulses
     chips = beams // 2
@@ -297,8 +327,8 @@
         in_specs=[SMEM, SMEM, VMEM, VMEM],
         out_specs=(spec, spec),
         compiler_params=pltpu.CompilerParams(vmem_limit_bytes=32 * 2**20),
-        cost_estimate=pl.CostEstimate(flops=3 * 10**10, bytes_accessed=4 * 10**6, transcendentals=0),
-    )(bits, gains, packed, jnp.asarray(mixing))
+        cost_estimate=pl.CostEstimate(flops=10**6, bytes_accessed=10**5, transcendentals=0),
+    )(place, gains, packed, jnp.asarray(mixing))
 
 
 def local(echoes, matched_filter, steering, kernels, blend_gains, beam_taps):
@@ -310,25 +340,16 @@
     beams = pulses // own_pulses
     slices = 4 * beams // 2
     core = lax.axis_index("core")
-    bits = jnp.stack([zl & 1, zl >> 1, zh, core]).astype(jnp.int32)
-    far_bits = jnp.stack([zl & 1, zl >> 1, 1 - zh, core]).astype(jnp.int32)
+    place = ((zh * 4 + zl) * 2 + core).astype(jnp.int32).reshape(1)
     swap = [(0, 1), (1, 0)]
     tables = [jnp.asarray(table) for table in dft_blocks()]
     blocks = (2 * own_pulses, 2, FA, FA)
 
     far_echoes = lax.ppermute(echoes, "zh", swap)
-    packed = jnp.concatenate(
-        [
-            jnp.moveaxis(steering, 1, 0).reshape(own_rows, 2 * pulses),
-            jnp.moveaxis(beam_taps, 3, 0).reshape(own_rows, 4 * LEVELS).astype(BF16),
-        ],
-        axis=1,
+    message, filters = compress_own(
+        place, steering, beam_taps, echoes.reshape(blocks), matched_filter, kernels, tables, slices
     )
-    packed = jnp.pad(packed, ((0, 0), (0, FA - packed.shape[1])))
-    message, filters = compress_own(
-        bits, echoes.reshape(blocks), packed, matched_filter, kernels, tables, slices
-    )
-    far_message = compress_far(far_bits, far_echoes.reshape(blocks), filters, kernels, tables, slices)
+    far_message = compress_far(place, far_echoes.reshape(blocks), filters, kernels, tables, slices)
     arrived = lax.all_to_all(message, ("zl", "chip"), 0, 0, tiled=True)
     far_message, arrived = lax.optimization_barrier((far_message, arrived))
     far_own = lax.all_to_all(far_message, ("zl", "chip"), 0, 0, tiled=True)
@@ -337,10 +358,16 @@
     swapped = lax.ppermute(arrived, "core", swap)
     split_at = arrived.shape[1] - FA
     chips = beams // 2
-    packed = [v[: chips * own_rows, split_at:].reshape(chips, own_rows, FA) for v in (arrived, swapped)]
-    packed = jnp.where(core == 0, jnp.stack(packed, axis=1), jnp.stack(packed[::-1], axis=1))
+
+    lanes = [v[: chips * own_rows, split_at:].reshape(chips, own_rows, FA) for v in (arrived, swapped)]
+    lanes = jnp.where(core == 0, jnp.stack(lanes, axis=1), jnp.stack(lanes[::-1], axis=1))
+    lanes = lanes.reshape(beams, own_rows, FA)
+    taps = lanes[:, :, 2 * pulses : 2 * pulses + 2 * own_rows].reshape(beams, 2 * LEVELS, 2, own_rows)
+    taps = jnp.transpose(taps, (0, 3, 1, 2)).reshape(beams, own_rows, 4 * LEVELS)
+    packed = jnp.concatenate([lanes[:, :, : 2 * pulses], taps], axis=2)
+    packed = jnp.pad(packed, ((0, 0), (0, 0), (0, FA - packed.shape[2])))
     near, far = beam_factors(
-        bits, blend_gains.reshape(-1), packed.reshape(-1, FA), beams, own_pulses
+        place, blend_gains.reshape(-1), packed.reshape(-1, FA), beams, own_pulses
     )
     near, far = (v.reshape(-1, 4 * FA) for v in (near, far))
     total = dot(near[:, : 2 * FA], arrived[:, :split_at]) + dot(near[:, 2 * FA :], swapped[:, :split_at])

time: 102 us -> 101 us (level)
  the two profiles are of different devices: /device:TPU:32 before, /device:TPU:160 now
where the time goes in v6:
time: 101 us
  blocking collectives  32.8 us (32%)
  starting transfers between devices  25.7 us (25%)
  waiting for transfers between devices  20.7 us (20%)
  Pallas kernels  13.7 us (14%)
  local copies, waits for them, and re-layouts  5.99 us (6%)
  matrix products  1.75 us (2%)
    all_to_all x1, blocking collectives, local(): arrived = lax.all_to_all(result, ('zl', 'chip'), 0, 0, tiled=True)  32.8 us
    all_to_all x1, waiting for transfers between devices, local(): arrived = lax.all_to_all(message, ('zl', 'chip'), 0, 0, tiled=True)  13.9 us
    all_to_all x1, starting transfers between devices, local(): arrived = lax.all_to_all(message, ('zl', 'chip'), 0, 0, tiled=True)  11.3 us
    all_to_all x1, starting transfers between devices, local(): far_own = lax.all_to_all(far_message, ('zl', 'chip'), 0, 0, tiled=True)  8.73 us
    all_to_all x1, waiting for transfers between devices, local(): far_own = lax.all_to_all(far_message, ('zl', 'chip'), 0, 0, tiled=True)  5.76 us
    pallas_call x1, Pallas kernels, compress_own(): pl.pallas_call(own_kernel, out_shape=(jax.ShapeDtypeStruct((slices, width...  5.54 us
    pallas_call x1, Pallas kernels, beam_factors(): pl.pallas_call(kernel, grid=(4,), out_shape=(shape, shape), in_specs=[SME...  4.7 us
    pallas_call x1, Pallas kernels, compress_far(): pl.pallas_call(far_kernel, out_shape=jax.ShapeDtypeStruct((slices, width,...  3.42 us
  transfers between devices with their start and end apart: 5, of which 3 were waited for; matrix products, arithmetic and copies ran while one was open for 4% of the time, Pallas kernels for 14%

profile of v6, /device:TPU:160, one launch (start us, length us, event | category | flops | bytes accessed | tf_op | source)
XLA Modules:
  0.0 101.0 jit_solution(1636827641464711679)
XLA Ops:
  0.0 1.9 %collective-permute-start = (bf16[2,2,2,16384]{3,2,1,0:T(2,128)(2,1)}, bf16[2,2,2,16384]{3,2,1,0:T(2,128)(2,1)S(1)}, u32[]{:S(2)}, u32[]{:S(2)}) collective-permute-start(bf16[2,2,2,16384]{3,2,1,0:T(2,128)(2,1)} %param.10), channel_id=1, source_target_pairs={{0,64},{64,0},{1,65},{65,1},{2,66},{66,2},{3,67},{67,3},{4,68},{68... | collective-permute-start | bytes 786440 | tf_op jit(solution)/shard_map/ppermute | solution.py:348
  1.9 1.8 %reshape.49.echo_hbm = bf16[4,2,128,128]{3,2,1,0:T(8,128)(2,1)} reshape(bf16[2,2,2,16384]{3,2,1,0:T(2,128)(2,1)} %param.10) | data formatting | bytes 524288 | tf_op jit(solution)/shard_map/reshape | solution.py:350
  3.8 5.5 %shard_map.100 = (bf16[32,8,640]{2,1,0:T(8,128)(2,1)}, f32[2,128,128]{2,1,0:T(8,128)}) custom-call(s32[1]{0:T(128)} %bitcast.place.refs_0_, bf16[2,8,32]{2,1,0:T(8,128)(2,1)} %steer.1, s32[4,2,2,8]{3,2,1,0:T(2,128)} %taps.1, bf16[4,2,128,128]{3,2,1,0:T(8,128)(2,1)} %reshape.49.echo_hbm, f32[2,16384]{1,0:T(2,128)} %matched_hbm.1, ...), custom_call_target="tpu_custom_call" | custom-call | flops 1000000000 | bytes 2000000 | tf_op jit(solution)/shard_map/pallas_call | solution.py:210
  9.3 11.3 %all-to-all-start = ((bf16[32,8,640]{2,1,0:T(8,128)(2,1)}), bf16[32,8,640]{2,1,0:T(8,128)(2,1)S(1)}, u32[]{:S(2)}, u32[]{:S(2)}) async-start(bf16[32,8,640]{2,1,0:T(8,128)(2,1)} %get-tuple-element.15), calls=%async_computation | async-start | bytes 655360 | tf_op jit(solution)/shard_map/all_to_all | solution.py:353
  20.6 0.0 collective-permute-done
  20.6 0.2 reshape.48.echo
  20.9 0.9 copy-done.5
  21.8 3.4 %shard_map.101 = bf16[32,8,512]{2,1,0:T(8,128)(2,1)} custom-call(s32[1]{0:T(128)} %bitcast.place.refs_0_, bf16[4,2,128,128]{3,2,1,0:T(8,128)(2,1)S(1)} %reshape.48.echo, f32[2,128,128]{2,1,0:T(8,128)S(1)} %copy-done.5, bf16[4,2,2,128,128]{4,3,2,1,0:T(8,128)(2,1)S(1)} %copy-done.1, bf16[2,256,256]{2,1,0:T(8,128)(2,1)S(1)} %copy-done.3, ...), custom_call_target="tpu_custom_call" | custom-call | flops 60000002048 | bytes 2000000 | tf_op jit(solution)/shard_map/pallas_call | solution.py:232
  25.2 13.9 %all-to-all-done = bf16[32,8,640]{2,1,0:T(8,128)(2,1)S(1)} async-done(((bf16[32,8,640]{2,1,0:T(8,128)(2,1)}), bf16[32,8,640]{2,1,0:T(8,128)(2,1)S(1)}, u32[]{:S(2)}, u32[]{:S(2)}) %all-to-all-start) | async-done | bytes 327712 | tf_op jit(solution)/shard_map/all_to_all | solution.py:353
  39.1 1.9 %collective-permute-start.1 = (bf16[256,640]{1,0:T(8,128)(2,1)S(1)}, bf16[256,640]{1,0:T(8,128)(2,1)S(1)}, u32[]{:S(2)}, u32[]{:S(2)}) collective-permute-start(bf16[256,640]{1,0:T(8,128)(2,1)S(1)} %bitcast.34), channel_id=1, source_target_pairs={{0,1},{1,0},{2,3},{3,2},{4,5},{5,4},{6,7},{7,6},{8,9},{9,8},{10,11... | collective-permute-start | bytes 983048 | tf_op jit(solution)/shard_map/ppermute | solution.py:358
  41.0 0.1 copy.26
  41.1 0.1 reshape.51.refs_1_
  41.2 8.7 %all-to-all-start.1 = ((bf16[32,8,512]{2,1,0:T(8,128)(2,1)}), bf16[32,8,512]{2,1,0:T(8,128)(2,1)S(1)}, u32[]{:S(2)}, u32[]{:S(2)}) async-start(bf16[32,8,512]{2,1,0:T(8,128)(2,1)} %shard_map.101), calls=%async_computation.1 | async-start | bytes 524288 | tf_op jit(solution)/shard_map/all_to_all | solution.py:355
  50.0 0.0 collective-permute-done.1
  50.0 0.0 copy-start.6
  50.0 0.7 copy-done.6
  50.7 0.1 slice.43
  50.8 0.1 copy.27
  50.9 0.1 copy.28
  51.1 0.0 copy-start.7
  51.1 0.1 fusion.11.refs_2_
  51.2 4.7 %shard_map.102 = (bf16[4,8,2,16,512]{4,3,2,1,0:T(8,128)(2,1)S(1)}, bf16[4,8,2,16,512]{4,3,2,1,0:T(8,128)(2,1)S(1)}) custom-call(s32[1]{0:T(128)} %bitcast.place.refs_0_, f32[32]{0:T(128)S(1)} %reshape.51.refs_1_, bf16[128,128]{1,0:T(8,128)(2,1)S(1)} %fusion.11.refs_2_, bf16[2,128,128]{2,1,0:T(8,128)(2,1)S(1)} %copy-done), custom_call_target="tpu_custom_call" | custom-call | flops 1000000 | bytes 100000 | tf_op jit(solution)/shard_map/pallas_call | solution.py:323
  55.9 0.4 fusion.1
  56.3 0.4 convolution_add_fusion
  56.7 5.8 %all-to-all-done.1 = bf16[32,8,512]{2,1,0:T(8,128)(2,1)S(1)} async-done(((bf16[32,8,512]{2,1,0:T(8,128)(2,1)}), bf16[32,8,512]{2,1,0:T(8,128)(2,1)S(1)}, u32[]{:S(2)}, u32[]{:S(2)}) %all-to-all-start.1) | async-done | bytes 262176 | tf_op jit(solution)/shard_map/all_to_all | solution.py:355
  62.5 1.9 %collective-permute-start.2 = (bf16[256,512]{1,0:T(8,128)(2,1)S(1)}, bf16[256,512]{1,0:T(8,128)(2,1)S(1)}, u32[]{:S(2)}, u32[]{:S(2)}) collective-permute-start(bf16[256,512]{1,0:T(8,128)(2,1)S(1)} %bitcast.37), channel_id=1, source_target_pairs={{0,1},{1,0},{2,3},{3,2},{4,5},{5,4},{6,7},{7,6},{8,9},{9,8},{10,11... | collective-permute-start | bytes 786440 | tf_op jit(solution)/shard_map/ppermute | solution.py:376
  64.4 0.4 fusion.4
  64.8 1.1 %collective-permute-done.2 = bf16[256,512]{1,0:T(8,128)(2,1)S(1)} collective-permute-done((bf16[256,512]{1,0:T(8,128)(2,1)S(1)}, bf16[256,512]{1,0:T(8,128)(2,1)S(1)}, u32[]{:S(2)}, u32[]{:S(2)}) %collective-permute-start.2) | collective-permute-done | bytes 262176 | tf_op jit(solution)/shard_map/ppermute | solution.py:376
  65.9 0.5 add_convert_fusion
  66.4 32.8 %all_to_all.15 = bf16[32,32,512]{2,1,0:T(8,128)(2,1)S(1)} all-to-all(bf16[32,32,512]{2,1,0:T(8,128)(2,1)S(1)} %bitcast.33), channel_id=1, replica_groups=mesh['g'=4,'zh'=2,'zl'=4,'chip'=8,'core'=2] {'zl','chip'}, dimensions={0} | all-to-all | bytes 2097152 | tf_op jit(solution)/shard_map/all_to_all | solution.py:380
  99.2 0.7 copy.31
  99.9 1.1 %reshape.60 = bf16[2,8,2,16384]{3,2,1,0:T(2,128)(2,1)} reshape(bf16[2,8,2,4,32,128]{5,4,3,2,1,0:T(8,128)(2,1)S(1)} %bitcast.32) | data formatting | bytes 2097152 | tf_op jit(solution)/shard_map/reshape | solution.py:382
  (17 shorter events, 0.0 us)
Async XLA Ops:
  0.0 20.6 %collective-permute-start = (bf16[2,2,2,16384]{3,2,1,0:T(2,128)(2,1)}, bf16[2,2,2,16384]{3,2,1,0:T(2,128)(2,1)S(1)}, u32[]{:S(2)}, u32[]{:S(2)}) collective-permute-start(bf16[2,2,2,16384]{3,2,1,0:T(2,128)(2,1)} %param.10), channel_id=1, source_target_pairs={{0,64},{64,0},{1,65},{65,1},{2,66},{66,2},{3,67},{67,3},{4,68},{68... | collective-permute-start | bytes 786440 | tf_op jit(solution)/shard_map/ppermute | solution.py:348
  3.8 17.1 %copy-start.1 = (bf16[4,2,2,128,128]{4,3,2,1,0:T(8,128)(2,1)S(1)}, bf16[4,2,2,128,128]{4,3,2,1,0:T(8,128)(2,1)}, u32[]{:S(2)}) copy-start(bf16[4,2,2,128,128]{4,3,2,1,0:T(8,128)(2,1)} %kern.1) | copy-start | bytes 1572868
  3.8 17.1 %copy-start.2 = (bf16[2,256,256]{2,1,0:T(8,128)(2,1)S(1)}, bf16[2,256,256]{2,1,0:T(8,128)(2,1)}, u32[]{:S(2)}) copy-start(bf16[2,256,256]{2,1,0:T(8,128)(2,1)} %constant.31.clone.minus_hbm.minus) | copy-start | bytes 786436
  3.8 17.1 %copy-start.3 = (bf16[2,256,256]{2,1,0:T(8,128)(2,1)S(1)}, bf16[2,256,256]{2,1,0:T(8,128)(2,1)}, u32[]{:S(2)}) copy-start(bf16[2,256,256]{2,1,0:T(8,128)(2,1)} %constant.30.clone.plus_hbm.plus) | copy-start | bytes 786436
  3.8 17.1 %copy-start.4 = (f32[2,128,128]{2,1,0:T(8,128)S(1)}, f32[2,128,128]{2,1,0:T(8,128)}, u32[]{:S(2)}) copy-start(f32[2,128,128]{2,1,0:T(8,128)} %constant.32.clone.turn_hbm.turn) | copy-start | bytes 393220
  9.3 29.8 %all-to-all-start = ((bf16[32,8,640]{2,1,0:T(8,128)(2,1)}), bf16[32,8,640]{2,1,0:T(8,128)(2,1)S(1)}, u32[]{:S(2)}, u32[]{:S(2)}) async-start(bf16[32,8,640]{2,1,0:T(8,128)(2,1)} %get-tuple-element.15), calls=%async_computation | async-start | bytes 655360 | tf_op jit(solution)/shard_map/all_to_all | solution.py:353
  20.9 0.9 copy-start.5
  21.8 19.3 %copy-start.8 = (f32[4,2,2,2]{0,3,2,1:T(2,128)S(1)}, f32[4,2,2,2]{0,3,2,1:T(2,128)}, u32[]{:S(2)}) copy-start(f32[4,2,2,2]{0,3,2,1:T(2,128)} %param.14) | copy-start | bytes 388
  21.8 29.4 %copy-start = (bf16[2,128,128]{2,1,0:T(8,128)(2,1)S(1)}, bf16[2,128,128]{2,1,0:T(8,128)(2,1)}, u32[]{:S(2)}) copy-start(bf16[2,128,128]{2,1,0:T(8,128)(2,1)} %constant.33.clone.refs_3_) | copy-start | bytes 196612
  39.1 10.9 %collective-permute-start.1 = (bf16[256,640]{1,0:T(8,128)(2,1)S(1)}, bf16[256,640]{1,0:T(8,128)(2,1)S(1)}, u32[]{:S(2)}, u32[]{:S(2)}) collective-permute-start(bf16[256,640]{1,0:T(8,128)(2,1)S(1)} %bitcast.34), channel_id=1, source_target_pairs={{0,1},{1,0},{2,3},{3,2},{4,5},{5,4},{6,7},{7,6},{8,9},{9,8},{10,11... | collective-permute-start | bytes 983048 | tf_op jit(solution)/shard_map/ppermute | solution.py:358
  41.2 21.3 %all-to-all-start.1 = ((bf16[32,8,512]{2,1,0:T(8,128)(2,1)}), bf16[32,8,512]{2,1,0:T(8,128)(2,1)S(1)}, u32[]{:S(2)}, u32[]{:S(2)}) async-start(bf16[32,8,512]{2,1,0:T(8,128)(2,1)} %shard_map.101), calls=%async_computation.1 | async-start | bytes 524288 | tf_op jit(solution)/shard_map/all_to_all | solution.py:355
  50.0 0.7 copy-start.6
  51.1 5.3 %copy-start.7 = (bf16[256,640]{1,0:T(8,128)(2,1)S(1)}, bf16[256,640]{1,0:T(8,128)(2,1)}, u32[]{:S(2)}) copy-start(bf16[256,640]{1,0:T(8,128)(2,1)} %copy-done.6) | copy-start | bytes 983044
  62.5 3.4 %collective-permute-start.2 = (bf16[256,512]{1,0:T(8,128)(2,1)S(1)}, bf16[256,512]{1,0:T(8,128)(2,1)S(1)}, u32[]{:S(2)}, u32[]{:S(2)}) collective-permute-start(bf16[256,512]{1,0:T(8,128)(2,1)S(1)} %bitcast.37), channel_id=1, source_target_pairs={{0,1},{1,0},{2,3},{3,2},{4,5},{5,4},{6,7},{7,6},{8,9},{9,8},{10,11... | collective-permute-start | bytes 786440 | tf_op jit(solution)/shard_map/ppermute | solution.py:376

commit v7 on v6

--- a/solution.py
+++ b/solution.py
@@ -134,16 +134,16 @@
 
 
 def send_order(rows, out):
-    slices, width = out.shape[:2]
+    copies, slices, width = out.shape[:3]
     for part in range(FA // slices):
         piece = rows[pl.ds(part * slices * width, slices * width), :]
-        out[:, :, part * FA : (part + 1) * FA] = piece.reshape(slices, width, FA).astype(BF16)
-
-
-def own_kernel(
-    place, steer, taps, echo_hbm, matched_hbm, kern_hbm, plus_hbm, minus_hbm, turn_hbm, out, filters, *refs
-):
-    echo, matched, kern, plus, minus, turn, lines, rows, packed, sems = refs
+        piece = piece.reshape(slices, width, FA).astype(BF16)
+        for copy in range(copies):
+            out[copy, :, :, part * FA : (part + 1) * FA] = piece
+
+
+def own_kernel(place, echo_hbm, matched_hbm, kern_hbm, plus_hbm, minus_hbm, turn_hbm, out, *refs):
+    echo, matched, kern, plus, minus, turn, lines, rows, sems = refs
     loads = [
         pltpu.make_async_copy(source, target, sems.at[at])
         for at, (source, target) in enumerate(
@@ -159,13 +159,6 @@
     ]
     for load in loads:
         load.start()
-    packed[...] = jnp.zeros_like(packed)
-    count, span = steer.shape[1], steer.shape[2]
-    for i in range(2):
-        packed[:, i * span : (i + 1) * span] = steer[i].astype(F32)
-    for level, child, parity in np.ndindex(*taps.shape[:3]):
-        row, lane = level * 2 + child, 2 * span + parity * count
-        packed[row : row + 1, lane : lane + count] = taps[level, child, parity : parity + 1, :].astype(F32)
     loads[0].wait()
     mats = range_matrices(place_bits(place), kern)
     for load in loads[1:4]:
@@ -178,25 +171,10 @@
         lines[0, j : j + 1, :] = matched[0:1, j * FA : (j + 1) * FA]
         lines[1, j : j + 1, :] = matched[1:2, j * FA : (j + 1) * FA]
     scale = 1.0 / (FA * FA)
-    filters[0] = jnp.transpose(lines[0]) * scale
-    filters[1] = jnp.transpose(lines[1]) * scale
+    filters = [jnp.transpose(lines[part]) * scale for part in range(2)]
     back = dot_table(filtered(spectrum, filters), plus)
     times_range(inverse_left(back, minus, turn), mats, rows)
     send_order(rows, out)
-    slices, width = out.shape[:2]
-    out[:, :, out.shape[2] - FA :] = jnp.broadcast_to(packed[...].astype(BF16)[None], (slices, width, FA))
-
-
-def far_kernel(place, echo, filters_hbm, kern, plus, minus, turn, out, rows, filters, sem):
-    load = pltpu.make_async_copy(filters_hbm, filters, sem)
-    load.start()
-    low, middle, high, _ = place_bits(place)
-    mats = range_matrices((low, middle, 1 - high), kern)
-    spectrum = dot_table(forward_left(echo, plus, turn), minus)
-    load.wait()
-    back = dot_table(filtered(spectrum, filters), plus)
-    times_range(inverse_left(back, minus, turn), mats, rows)
-    send_order(rows, out)
 
 
 SMEM = pl.BlockSpec(memory_space=pltpu.SMEM)
@@ -204,47 +182,26 @@
 ANY = pl.BlockSpec(memory_space=pl.ANY)
 
 
-def compress_own(place, steering, taps, echo, matched, kern, tables, slices):
+def compress_own(place, echo, matched, kern, tables, copies, slices):
     large = [echo, matched, kern, *tables]
     width = 2 * echo.shape[0]
     return pl.pallas_call(
         own_kernel,
-        out_shape=(
-            jax.ShapeDtypeStruct((slices, width, FA * FA // slices + FA), BF16),
-            jax.ShapeDtypeStruct((2, FA, FA), F32),
-        ),
-        in_specs=[SMEM, VMEM, VMEM] + [ANY] * len(large),
-        out_specs=(VMEM, VMEM),
+        out_shape=jax.ShapeDtypeStruct((copies, slices, width, FA * FA // slices), BF16),
+        in_specs=[SMEM] + [ANY] * len(large),
+        out_specs=VMEM,
         scratch_shapes=[pltpu.VMEM(table.shape, table.dtype) for table in large]
         + [
             pltpu.VMEM((2, FA, FA), F32),
             pltpu.VMEM((FA * width, FA), F32),
-            pltpu.VMEM((8, FA), F32),
             pltpu.SemaphoreType.DMA((len(large),)),
         ],
         compiler_params=pltpu.CompilerParams(vmem_limit_bytes=60 * 2**20),
         cost_estimate=pl.CostEstimate(flops=10**9, bytes_accessed=2 * 10**6, transcendentals=0),
-    )(place, steering, taps, *large)
-
-
-def compress_far(place, echo, filters, kern, tables, slices):
-    width = 2 * echo.shape[0]
-    return pl.pallas_call(
-        far_kernel,
-        out_shape=jax.ShapeDtypeStruct((slices, width, FA * FA // slices), BF16),
-        in_specs=[SMEM, VMEM, ANY] + [VMEM] * (1 + len(tables)),
-        out_specs=VMEM,
-        scratch_shapes=[
-            pltpu.VMEM((FA * width, FA), F32),
-            pltpu.VMEM(filters.shape, F32),
-            pltpu.SemaphoreType.DMA,
-        ],
-        compiler_params=pltpu.CompilerParams(vmem_limit_bytes=32 * 2**20),
-        cost_estimate=pl.CostEstimate(flops=6 * 10**10, bytes_accessed=2 * 10**6, transcendentals=0),
-    )(place, echo, filters, kern, *tables)
-
-
-def beam_kernel(steer_lanes, place, gains, packed, mixing, out_near, out_far):
+    )(place, *large)
+
+
+def beam_kernel(steer_lanes, place, gains, packed, mixing, out_own, out_other):
     e3 = pl.program_id(0) // 2
     e2 = pl.program_id(0) % 2
     _, _, e4, core = place_bits(place)
@@ -286,24 +243,23 @@
 
     level2 = by_lane(1, e2, lane >= FA // 2)
     level3 = [weights(2, child, e3) for child in range(2)]
-    pair = [weights(3, child, e4) for child in range(2)]
-    level4 = [[of_core(jnp.where(e4 == at, *v)) for v in zip(pair[0], pair[1])] for at in (0, 1)]
+    level4 = [[of_core(w) for w in weights(3, child, e4)] for child in range(2)]
     imaginary = lane[: rows // 2] % 2 == 1
     for e1 in range(2):
         level1 = by_lane(0, e1, (lane // 4) % 2 == 1)
-        for slot in range(2):
+        for slot, out in ((0, out_own), (1, out_other)):
             source = jnp.where(slot == 0, core, 1 - core)
             second = blend(neighbours(dot(data, mixing[source])), level1)
             second = neighbours(blend(neighbours(second), level2))
             for c3 in range(2):
                 third = [of_core(v) for v in neighbours(blend(second, level3[c3]))]
-                for half, out in ((0, out_near), (1, out_far)):
-                    real_row = blend(third, level4[half])
+                for c4 in range(2):
+                    real_row = blend(third, level4[c4])
                     imag_row = jnp.where(
                         imaginary, pltpu.roll(real_row, 1, 1), -pltpu.roll(real_row, FA - 1, 1)
                     )
                     both = [v.reshape(rows // 16, 8, FA) for v in (real_row, imag_row)]
-                    at = (slot * 2 + c3) * FA
+                    at = (c4 * 2 + c3) * FA
                     out[0, :, e1, :, at : at + FA] = jnp.concatenate(both, axis=1).astype(BF16)
 
 
@@ -331,51 +287,52 @@
     )(place, gains, packed, jnp.asarray(mixing))
 
 
+def gather_rows(packed, core, chip):
+    steps = [("core", 1, core)] + [("chip", 1 << bit, (chip >> bit) & 1) for bit in range(3)]
+    for axis, apart, upper in steps:
+        size = lax.axis_size(axis)
+        got = lax.ppermute(packed, axis, [(i, i ^ apart) for i in range(size)])
+        low, high = jnp.where(upper == 0, packed, got), jnp.where(upper == 0, got, packed)
+        packed = jnp.concatenate([low, high], axis=0)
+    return packed
+
+
 def local(echoes, matched_filter, steering, kernels, blend_gains, beam_taps):
     zh = lax.axis_index("zh")
     zl = lax.axis_index("zl")
+    core = lax.axis_index("core")
     own_rows = steering.shape[1]
     pulses = steering.shape[2]
     own_pulses = echoes.shape[1]
     beams = pulses // own_pulses
     slices = 4 * beams // 2
-    core = lax.axis_index("core")
     place = ((zh * 4 + zl) * 2 + core).astype(jnp.int32).reshape(1)
-    swap = [(0, 1), (1, 0)]
     tables = [jnp.asarray(table) for table in dft_blocks()]
-    blocks = (2 * own_pulses, 2, FA, FA)
-
-    far_echoes = lax.ppermute(echoes, "zh", swap)
-    message, filters = compress_own(
-        place, steering, beam_taps, echoes.reshape(blocks), matched_filter, kernels, tables, slices
+
+    message = compress_own(
+        place, echoes.reshape(2 * own_pulses, 2, FA, FA), matched_filter, kernels, tables, 2, slices
     )
-    far_message = compress_far(place, far_echoes.reshape(blocks), filters, kernels, tables, slices)
-    arrived = lax.all_to_all(message, ("zl", "chip"), 0, 0, tiled=True)
-    far_message, arrived = lax.optimization_barrier((far_message, arrived))
-    far_own = lax.all_to_all(far_message, ("zl", "chip"), 0, 0, tiled=True)
-
-    arrived = arrived.reshape(-1, arrived.shape[2])
-    swapped = lax.ppermute(arrived, "core", swap)
-    split_at = arrived.shape[1] - FA
-    chips = beams // 2
-
-    lanes = [v[: chips * own_rows, split_at:].reshape(chips, own_rows, FA) for v in (arrived, swapped)]
-    lanes = jnp.where(core == 0, jnp.stack(lanes, axis=1), jnp.stack(lanes[::-1], axis=1))
-    lanes = lanes.reshape(beams, own_rows, FA)
-    taps = lanes[:, :, 2 * pulses : 2 * pulses + 2 * own_rows].reshape(beams, 2 * LEVELS, 2, own_rows)
-    taps = jnp.transpose(taps, (0, 3, 1, 2)).reshape(beams, own_rows, 4 * LEVELS)
-    packed = jnp.concatenate([lanes[:, :, : 2 * pulses], taps], axis=2)
-    packed = jnp.pad(packed, ((0, 0), (0, 0), (0, FA - packed.shape[2])))
-    near, far = beam_factors(
-        place, blend_gains.reshape(-1), packed.reshape(-1, FA), beams, own_pulses
+    message, steering, beam_taps = lax.optimization_barrier((message, steering, beam_taps))
+    width = message.shape[2]
+    own = lax.all_to_all(
+        message.reshape(2 * slices, width, -1), ("zh", "zl", "chip"), 0, 0, tiled=True
+    ).reshape(2 * slices * width, -1)
+
+    packed = jnp.concatenate(
+        [
+            jnp.moveaxis(steering, 1, 0).reshape(own_rows, 2 * pulses),
+            jnp.moveaxis(beam_taps, 3, 0).reshape(own_rows, 4 * LEVELS).astype(BF16),
+        ],
+        axis=1,
     )
-    near, far = (v.reshape(-1, 4 * FA) for v in (near, far))
-    total = dot(near[:, : 2 * FA], arrived[:, :split_at]) + dot(near[:, 2 * FA :], swapped[:, :split_at])
-
-    far_own, total, far = lax.optimization_barrier((far_own.reshape(-1, split_at), total, far))
-    far_swapped = lax.ppermute(far_own, "core", swap)
-    total = total + dot(far[:, : 2 * FA], far_own)
-    total = total + dot(far[:, 2 * FA :], far_swapped)
+    packed = jnp.pad(packed, ((0, 0), (0, FA - packed.shape[1])))
+    packed = gather_rows(packed, core, lax.axis_index("chip"))
+    near, far = beam_factors(place, blend_gains.reshape(-1), packed, beams, own_pulses)
+
+    own, near, far = lax.optimization_barrier((own, near, far))
+    other = lax.ppermute(own, "core", [(0, 1), (1, 0)])
+    total = dot(near.reshape(-1, 4 * FA), own)
+    total = total + dot(far.reshape(-1, 4 * FA), other)
     result = total.astype(BF16).reshape(slices, 4 * own_rows, -1)
     arrived = lax.all_to_all(result, ("zl", "chip"), 0, 0, tiled=True)
     arrived = arrived.reshape(slices, 2, 2, own_rows, -1, FA)

time: 101 us -> 97.8 us (0.968)
  the two profiles are of different devices: /device:TPU:160 before, /device:TPU:32 now
where the time goes in v7:
time: 97.8 us; the launch traced here: 97.4 us
  blocking collectives  37 us (38%)
  starting transfers between devices  35.3 us (36%)
  waiting for transfers between devices  9.77 us (10%)
  Pallas kernels  9.53 us (10%)
  local copies, waits for them, and re-layouts  4.03 us (4%)
  matrix products  1.4 us (1%)
    all_to_all x1, blocking collectives, local(): arrived = lax.all_to_all(result, ('zl', 'chip'), 0, 0, tiled=True)  37 us
    all_to_all x1, starting transfers between devices, local(): lax.all_to_all(message.reshape(2 * slices, width, -1), ('zh', 'zl', 'chip...  18.3 us
    ppermute x4, starting transfers between devices, gather_rows(): got = lax.ppermute(packed, axis, [(i, i ^ apart) for i in range(size)])  15.1 us
    ppermute x4, waiting for transfers between devices, gather_rows(): got = lax.ppermute(packed, axis, [(i, i ^ apart) for i in range(size)])  7.47 us
    pallas_call x1, Pallas kernels, compress_own(): pl.pallas_call(own_kernel, out_shape=jax.ShapeDtypeStruct((copies, slices...  4.9 us
    pallas_call x1, Pallas kernels, beam_factors(): pl.pallas_call(kernel, grid=(4,), out_shape=(shape, shape), in_specs=[SME...  4.63 us
  transfers between devices with their start and end apart: 6, of which 6 were waited for; matrix products, arithmetic and copies ran while one was open for 1% of the time, Pallas kernels for 5%

profile of v7, /device:TPU:32, one launch (start us, length us, event | category | flops | bytes accessed | tf_op | source)
XLA Modules:
  0.0 97.4 jit_solution(7055361238955840205)
XLA Ops:
  0.0 1.9 %reshape.36.echo_hbm = bf16[4,2,128,128]{3,2,1,0:T(8,128)(2,1)} reshape(bf16[2,2,2,16384]{3,2,1,0:T(2,128)(2,1)} %param.10) | data formatting | bytes 524288 | tf_op jit(solution)/shard_map/reshape | solution.py:313
  1.9 0.0 copy-start.1
  1.9 0.0 copy-start.3
  1.9 4.9 %shard_map.100 = bf16[2,32,8,512]{3,2,1,0:T(8,128)(2,1)} custom-call(s32[1]{0:T(128)} %bitcast.place.refs_0_, bf16[4,2,128,128]{3,2,1,0:T(8,128)(2,1)} %reshape.36.echo_hbm, f32[2,16384]{1,0:T(2,128)} %matched_hbm.1, bf16[4,2,2,128,128]{4,3,2,1,0:T(8,128)(2,1)} %kern_hbm.1, bf16[2,256,256]{2,1,0:T(8,128)(2,1)} %constant.36.clone.plus_hbm, ...), custom_call_target="tpu_custom_call" | custom-call | flops 1000000000 | bytes 2000000 | tf_op jit(solution)/shard_map/pallas_call | solution.py:188
  6.8 18.3 %all-to-all-start = ((bf16[64,8,512]{2,1,0:T(8,128)(2,1)}), bf16[64,8,512]{2,1,0:T(8,128)(2,1)S(1)}, u32[]{:S(2)}, u32[]{:S(2)}) async-start(bf16[64,8,512]{2,1,0:T(8,128)(2,1)} %bitcast.27), calls=%async_computation | async-start | bytes 1048576 | tf_op jit(solution)/shard_map/all_to_all | solution.py:317
  25.1 0.0 copy-done.1
  25.1 0.1 copy.17
  25.2 0.0 copy-done.3
  25.2 0.1 reshape.40
  25.3 0.1 fusion.2
  25.4 1.9 %collective-permute-start = (bf16[8,128]{1,0:T(8,128)(2,1)S(1)}, bf16[8,128]{1,0:T(8,128)(2,1)S(1)}, u32[]{:S(2)}, u32[]{:S(2)}) collective-permute-start(bf16[8,128]{1,0:T(8,128)(2,1)S(1)} %fusion.2), channel_id=1, source_target_pairs={{0,1},{1,0},{2,3},{3,2},{4,5},{5,4},{6,7},{7,6},{8,9},{9,8},{10,11... | collective-permute-start | bytes 6152 | tf_op jit(solution)/shard_map/ppermute | solution.py:294
  27.3 1.1 %collective-permute-done = bf16[8,128]{1,0:T(8,128)(2,1)S(1)} collective-permute-done((bf16[8,128]{1,0:T(8,128)(2,1)S(1)}, bf16[8,128]{1,0:T(8,128)(2,1)S(1)}, u32[]{:S(2)}, u32[]{:S(2)}) %collective-permute-start) | collective-permute-done | bytes 2080 | tf_op jit(solution)/shard_map/ppermute | solution.py:294
  28.4 0.1 broadcast_select_fusion.7
  28.5 3.4 %collective-permute-start.1 = (bf16[16,128]{1,0:T(8,128)(2,1)S(1)}, bf16[16,128]{1,0:T(8,128)(2,1)S(1)}, u32[]{:S(2)}, u32[]{:S(2)}) collective-permute-start(bf16[16,128]{1,0:T(8,128)(2,1)S(1)} %pad_maximum_fusion.3), channel_id=1, source_target_pairs={{0,2},{2,0},{4,6},{6,4},{8,10},{10,8},{12,14},{14,12},{1,3},{3,1},... | collective-permute-start | bytes 12296 | tf_op jit(solution)/shard_map/ppermute | solution.py:294
  31.9 2.1 %collective-permute-done.1 = bf16[16,128]{1,0:T(8,128)(2,1)S(1)} collective-permute-done((bf16[16,128]{1,0:T(8,128)(2,1)S(1)}, bf16[16,128]{1,0:T(8,128)(2,1)S(1)}, u32[]{:S(2)}, u32[]{:S(2)}) %collective-permute-start.1) | collective-permute-done | bytes 4128 | tf_op jit(solution)/shard_map/ppermute | solution.py:294
  34.0 4.9 %collective-permute-start.2 = (bf16[32,128]{1,0:T(8,128)(2,1)S(1)}, bf16[32,128]{1,0:T(8,128)(2,1)S(1)}, u32[]{:S(2)}, u32[]{:S(2)}) collective-permute-start(bf16[32,128]{1,0:T(8,128)(2,1)S(1)} %pad_maximum_fusion.2), channel_id=1, source_target_pairs={{0,4},{2,6},{4,0},{6,2},{8,12},{10,14},{12,8},{14,10},{1,5},{3,7},... | collective-permute-start | bytes 24584 | tf_op jit(solution)/shard_map/ppermute | solution.py:294
  38.9 2.2 %collective-permute-done.2 = bf16[32,128]{1,0:T(8,128)(2,1)S(1)} collective-permute-done((bf16[32,128]{1,0:T(8,128)(2,1)S(1)}, bf16[32,128]{1,0:T(8,128)(2,1)S(1)}, u32[]{:S(2)}, u32[]{:S(2)}) %collective-permute-start.2) | collective-permute-done | bytes 8224 | tf_op jit(solution)/shard_map/ppermute | solution.py:294
  41.1 4.9 %collective-permute-start.3 = (bf16[64,128]{1,0:T(8,128)(2,1)S(1)}, bf16[64,128]{1,0:T(8,128)(2,1)S(1)}, u32[]{:S(2)}, u32[]{:S(2)}) collective-permute-start(bf16[64,128]{1,0:T(8,128)(2,1)S(1)} %pad_maximum_fusion.1), channel_id=1, source_target_pairs={{0,8},{2,10},{4,12},{6,14},{8,0},{10,2},{12,4},{14,6},{1,9},{3,11}... | collective-permute-start | bytes 49160 | tf_op jit(solution)/shard_map/ppermute | solution.py:294
  46.0 0.0 copy-done.2
  46.0 0.1 copy.15
  46.2 0.1 reshape.39.refs_1_
  46.2 2.0 %collective-permute-done.3 = bf16[64,128]{1,0:T(8,128)(2,1)S(1)} collective-permute-done((bf16[64,128]{1,0:T(8,128)(2,1)S(1)}, bf16[64,128]{1,0:T(8,128)(2,1)S(1)}, u32[]{:S(2)}, u32[]{:S(2)}) %collective-permute-start.3) | collective-permute-done | bytes 16416 | tf_op jit(solution)/shard_map/ppermute | solution.py:294
  48.3 0.0 copy-done
  48.3 4.6 %shard_map.101 = (bf16[4,8,2,16,512]{4,3,2,1,0:T(8,128)(2,1)S(1)}, bf16[4,8,2,16,512]{4,3,2,1,0:T(8,128)(2,1)S(1)}) custom-call(s32[1]{0:T(128)} %bitcast.place.refs_0_, f32[32]{0:T(128)S(1)} %reshape.39.refs_1_, bf16[128,128]{1,0:T(8,128)(2,1)S(1)} %pad_maximum_fusion.refs_2_, bf16[2,128,128]{2,1,0:T(8,128)(2,1)S(1)} %copy-done), custom_call_target="tpu_custom_call" | custom-call | flops 1000000 | bytes 100000 | tf_op jit(solution)/shard_map/pallas_call | solution.py:279
  52.9 1.1 %all-to-all-done = bf16[64,8,512]{2,1,0:T(8,128)(2,1)S(1)} async-done(((bf16[64,8,512]{2,1,0:T(8,128)(2,1)}), bf16[64,8,512]{2,1,0:T(8,128)(2,1)S(1)}, u32[]{:S(2)}, u32[]{:S(2)}) %all-to-all-start) | async-done | bytes 524320 | tf_op jit(solution)/shard_map/all_to_all | solution.py:317
  54.1 1.9 %collective-permute-start.4 = (bf16[512,512]{1,0:T(8,128)(2,1)S(1)}, bf16[512,512]{1,0:T(8,128)(2,1)S(1)}, u32[]{:S(2)}, u32[]{:S(2)}) collective-permute-start(bf16[512,512]{1,0:T(8,128)(2,1)S(1)} %bitcast.25), channel_id=1, source_target_pairs={{0,1},{1,0},{2,3},{3,2},{4,5},{5,4},{6,7},{7,6},{8,9},{9,8},{10,11... | collective-permute-start | bytes 1572872 | tf_op jit(solution)/shard_map/ppermute | solution.py:333
  56.0 0.7 fusion.3
  56.7 1.2 %collective-permute-done.4 = bf16[512,512]{1,0:T(8,128)(2,1)S(1)} collective-permute-done((bf16[512,512]{1,0:T(8,128)(2,1)S(1)}, bf16[512,512]{1,0:T(8,128)(2,1)S(1)}, u32[]{:S(2)}, u32[]{:S(2)}) %collective-permute-start.4) | collective-permute-done | bytes 524320 | tf_op jit(solution)/shard_map/ppermute | solution.py:333
  57.9 0.7 add_convert_fusion
  58.6 37.0 %all_to_all.10 = bf16[32,32,512]{2,1,0:T(8,128)(2,1)S(1)} all-to-all(bf16[32,32,512]{2,1,0:T(8,128)(2,1)S(1)} %bitcast.24), channel_id=1, replica_groups=mesh['g'=4,'zh'=2,'zl'=4,'chip'=8,'core'=2] {'zl','chip'}, dimensions={0} | all-to-all | bytes 2097152 | tf_op jit(solution)/shard_map/all_to_all | solution.py:337
  95.6 0.7 copy.20
  96.3 1.1 %reshape.45 = bf16[2,8,2,16384]{3,2,1,0:T(2,128)(2,1)} reshape(bf16[2,8,2,4,32,128]{5,4,3,2,1,0:T(8,128)(2,1)S(1)} %bitcast.23) | data formatting | bytes 2097152 | tf_op jit(solution)/shard_map/reshape | solution.py:339
  (11 shorter events, 0.1 us)
Async XLA Ops:
  1.9 23.2 %copy-start.1 = (s32[4,2,2,8]{3,2,1,0:T(2,128)S(1)}, s32[4,2,2,8]{3,2,1,0:T(2,128)}, u32[]{:S(2)}) copy-start(s32[4,2,2,8]{3,2,1,0:T(2,128)} %param.15) | copy-start | bytes 1540
  1.9 23.3 %copy-start.3 = (bf16[2,8,32]{2,1,0:T(8,128)(2,1)S(1)}, bf16[2,8,32]{2,1,0:T(8,128)(2,1)}, u32[]{:S(2)}) copy-start(bf16[2,8,32]{2,1,0:T(8,128)(2,1)} %param.12) | copy-start | bytes 3076
  1.9 44.2 %copy-start.2 = (f32[4,2,2,2]{0,3,2,1:T(2,128)S(1)}, f32[4,2,2,2]{0,3,2,1:T(2,128)}, u32[]{:S(2)}) copy-start(f32[4,2,2,2]{0,3,2,1:T(2,128)} %param.14) | copy-start | bytes 388
  1.9 46.4 %copy-start = (bf16[2,128,128]{2,1,0:T(8,128)(2,1)S(1)}, bf16[2,128,128]{2,1,0:T(8,128)(2,1)}, u32[]{:S(2)}) copy-start(bf16[2,128,128]{2,1,0:T(8,128)(2,1)} %constant.39.clone.refs_3_) | copy-start | bytes 196612
  6.8 47.3 %all-to-all-start = ((bf16[64,8,512]{2,1,0:T(8,128)(2,1)}), bf16[64,8,512]{2,1,0:T(8,128)(2,1)S(1)}, u32[]{:S(2)}, u32[]{:S(2)}) async-start(bf16[64,8,512]{2,1,0:T(8,128)(2,1)} %bitcast.27), calls=%async_computation | async-start | bytes 1048576 | tf_op jit(solution)/shard_map/all_to_all | solution.py:317
  25.4 3.0 %collective-permute-start = (bf16[8,128]{1,0:T(8,128)(2,1)S(1)}, bf16[8,128]{1,0:T(8,128)(2,1)S(1)}, u32[]{:S(2)}, u32[]{:S(2)}) collective-permute-start(bf16[8,128]{1,0:T(8,128)(2,1)S(1)} %fusion.2), channel_id=1, source_target_pairs={{0,1},{1,0},{2,3},{3,2},{4,5},{5,4},{6,7},{7,6},{8,9},{9,8},{10,11... | collective-permute-start | bytes 6152 | tf_op jit(solution)/shard_map/ppermute | solution.py:294
  28.5 5.5 %collective-permute-start.1 = (bf16[16,128]{1,0:T(8,128)(2,1)S(1)}, bf16[16,128]{1,0:T(8,128)(2,1)S(1)}, u32[]{:S(2)}, u32[]{:S(2)}) collective-permute-start(bf16[16,128]{1,0:T(8,128)(2,1)S(1)} %pad_maximum_fusion.3), channel_id=1, source_target_pairs={{0,2},{2,0},{4,6},{6,4},{8,10},{10,8},{12,14},{14,12},{1,3},{3,1},... | collective-permute-start | bytes 12296 | tf_op jit(solution)/shard_map/ppermute | solution.py:294
  34.0 7.1 %collective-permute-start.2 = (bf16[32,128]{1,0:T(8,128)(2,1)S(1)}, bf16[32,128]{1,0:T(8,128)(2,1)S(1)}, u32[]{:S(2)}, u32[]{:S(2)}) collective-permute-start(bf16[32,128]{1,0:T(8,128)(2,1)S(1)} %pad_maximum_fusion.2), channel_id=1, source_target_pairs={{0,4},{2,6},{4,0},{6,2},{8,12},{10,14},{12,8},{14,10},{1,5},{3,7},... | collective-permute-start | bytes 24584 | tf_op jit(solution)/shard_map/ppermute | solution.py:294
  41.1 7.1 %collective-permute-start.3 = (bf16[64,128]{1,0:T(8,128)(2,1)S(1)}, bf16[64,128]{1,0:T(8,128)(2,1)S(1)}, u32[]{:S(2)}, u32[]{:S(2)}) collective-permute-start(bf16[64,128]{1,0:T(8,128)(2,1)S(1)} %pad_maximum_fusion.1), channel_id=1, source_target_pairs={{0,8},{2,10},{4,12},{6,14},{8,0},{10,2},{12,4},{14,6},{1,9},{3,11}... | collective-permute-start | bytes 49160 | tf_op jit(solution)/shard_map/ppermute | solution.py:294
  54.1 3.8 %collective-permute-start.4 = (bf16[512,512]{1,0:T(8,128)(2,1)S(1)}, bf16[512,512]{1,0:T(8,128)(2,1)S(1)}, u32[]{:S(2)}, u32[]{:S(2)}) collective-permute-start(bf16[512,512]{1,0:T(8,128)(2,1)S(1)} %bitcast.25), channel_id=1, source_target_pairs={{0,1},{1,0},{2,3},{3,2},{4,5},{5,4},{6,7},{7,6},{8,9},{9,8},{10,11... | collective-permute-start | bytes 1572872 | tf_op jit(solution)/shard_map/ppermute | solution.py:333

commit v8 on v7

--- a/solution.py
+++ b/solution.py
@@ -79,10 +79,9 @@
     return mats
 
 
-def forward_left(echo, plus, turn):
-    count = echo.shape[0]
+def forward_left(signal, plus, turn):
+    count = signal.shape[1] // FA
     c, s = turn[0], turn[1]
-    signal = jnp.concatenate([echo[q].reshape(2 * FA, FA) for q in range(count)], axis=1)
     first = dot(plus[0], signal) + dot(plus[1], signal)
     stacked = []
     for q in range(count):
@@ -134,24 +133,24 @@
 
 
 def send_order(rows, out):
-    copies, slices, width = out.shape[:3]
+    slices, copies, width = out.shape[:3]
     for part in range(FA // slices):
         piece = rows[pl.ds(part * slices * width, slices * width), :]
         piece = piece.reshape(slices, width, FA).astype(BF16)
         for copy in range(copies):
-            out[copy, :, :, part * FA : (part + 1) * FA] = piece
+            out[:, copy, :, part * FA : (part + 1) * FA] = piece
 
 
 def own_kernel(place, echo_hbm, matched_hbm, kern_hbm, plus_hbm, minus_hbm, turn_hbm, out, *refs):
-    echo, matched, kern, plus, minus, turn, lines, rows, sems = refs
+    echo, matched, kern, plus, minus, turn, signal, lines, rows, sems = refs
     loads = [
         pltpu.make_async_copy(source, target, sems.at[at])
         for at, (source, target) in enumerate(
             (
+                (echo_hbm, echo),
+                (plus_hbm, plus),
+                (turn_hbm, turn),
                 (kern_hbm, kern),
-                (plus_hbm, plus),
-                (echo_hbm, echo),
-                (turn_hbm, turn),
                 (minus_hbm, minus),
                 (matched_hbm, matched),
             )
@@ -160,13 +159,17 @@
     for load in loads:
         load.start()
     loads[0].wait()
+    pulses = echo.shape[1]
+    for n in range(FA):
+        for q in range(echo.shape[0] * pulses):
+            pair = echo[q // pulses, q % pulses, :, n * FA : (n + 1) * FA].astype(F32)
+            signal[n : n + 1, q * FA : (q + 1) * FA] = pair[0:1]
+            signal[FA + n : FA + n + 1, q * FA : (q + 1) * FA] = pair[1:2]
+    for load in loads[1:]:
+        load.wait()
     mats = range_matrices(place_bits(place), kern)
-    for load in loads[1:4]:
-        load.wait()
-    turned = forward_left(echo, plus, turn)
-    loads[4].wait()
+    turned = forward_left(signal[...].astype(BF16), plus, turn)
     spectrum = dot_table(turned, minus)
-    loads[5].wait()
     for j in range(FA):
         lines[0, j : j + 1, :] = matched[0:1, j * FA : (j + 1) * FA]
         lines[1, j : j + 1, :] = matched[1:2, j * FA : (j + 1) * FA]
@@ -184,14 +187,15 @@
 
 def compress_own(place, echo, matched, kern, tables, copies, slices):
     large = [echo, matched, kern, *tables]
-    width = 2 * echo.shape[0]
+    width = 2 * echo.shape[0] * echo.shape[1]
     return pl.pallas_call(
         own_kernel,
-        out_shape=jax.ShapeDtypeStruct((copies, slices, width, FA * FA // slices), BF16),
+        out_shape=jax.ShapeDtypeStruct((slices, copies, width, FA * FA // slices), BF16),
         in_specs=[SMEM] + [ANY] * len(large),
         out_specs=VMEM,
         scratch_shapes=[pltpu.VMEM(table.shape, table.dtype) for table in large]
         + [
+            pltpu.VMEM((2 * FA, width // 2 * FA), F32),
             pltpu.VMEM((2, FA, FA), F32),
             pltpu.VMEM((FA * width, FA), F32),
             pltpu.SemaphoreType.DMA((len(large),)),
@@ -241,25 +245,25 @@
         tiles = value.reshape(rows // 16, 2, 8, FA)
         return jnp.where(core == 0, tiles[:, 0], tiles[:, 1]).reshape(rows // 2, FA)
 
-    level2 = by_lane(1, e2, lane >= FA // 2)
+    level2 = [weights(1, child, e2) for child in range(2)]
     level3 = [weights(2, child, e3) for child in range(2)]
-    level4 = [[of_core(w) for w in weights(3, child, e4)] for child in range(2)]
+    level4 = [of_core(w) for w in by_lane(3, e4, (lane // 8) % 2 == 1)]
     imaginary = lane[: rows // 2] % 2 == 1
     for e1 in range(2):
         level1 = by_lane(0, e1, (lane // 4) % 2 == 1)
         for slot, out in ((0, out_own), (1, out_other)):
             source = jnp.where(slot == 0, core, 1 - core)
-            second = blend(neighbours(dot(data, mixing[source])), level1)
-            second = neighbours(blend(neighbours(second), level2))
-            for c3 in range(2):
-                third = [of_core(v) for v in neighbours(blend(second, level3[c3]))]
-                for c4 in range(2):
-                    real_row = blend(third, level4[c4])
+            first = neighbours(blend(neighbours(dot(data, mixing[source])), level1))
+            for c2 in range(2):
+                second = neighbours(blend(first, level2[c2]))
+                for c3 in range(2):
+                    third = [of_core(v) for v in neighbours(blend(second, level3[c3]))]
+                    real_row = blend(third, level4)
                     imag_row = jnp.where(
                         imaginary, pltpu.roll(real_row, 1, 1), -pltpu.roll(real_row, FA - 1, 1)
                     )
                     both = [v.reshape(rows // 16, 8, FA) for v in (real_row, imag_row)]
-                    at = (c4 * 2 + c3) * FA
+                    at = (c3 * 2 + c2) * FA
                     out[0, :, e1, :, at : at + FA] = jnp.concatenate(both, axis=1).astype(BF16)
 
 
@@ -268,8 +272,8 @@
     pulses = beams * own_pulses
     chips = beams // 2
     mixing = np.zeros((2, FA, FA), ml_dtypes.bfloat16)
-    for core, c2, chip, c1, p, i in np.ndindex(2, 2, chips, 2, own_pulses, 2):
-        lane = (((c2 * chips + chip) * 2 + c1) * own_pulses + p) * 2 + i
+    for core, chip, c4, c1, p, i in np.ndindex(2, chips, 2, 2, own_pulses, 2):
+        lane = (((chip * 2 + c4) * 2 + c1) * own_pulses + p) * 2 + i
         mixing[core, i * pulses + (chip * 2 + core) * own_pulses + p, lane] = -1 if i else 1
     shape = jax.ShapeDtypeStruct((4, chips, 2, 16, 4 * FA), BF16)
     spec = pl.BlockSpec((1, chips, 2, 16, 4 * FA), lambda g: (g, 0, 0, 0, 0))
@@ -310,12 +314,12 @@
     tables = [jnp.asarray(table) for table in dft_blocks()]
 
     message = compress_own(
-        place, echoes.reshape(2 * own_pulses, 2, FA, FA), matched_filter, kernels, tables, 2, slices
+        place, echoes, matched_filter, kernels, tables, 2, slices
     )
     message, steering, beam_taps = lax.optimization_barrier((message, steering, beam_taps))
     width = message.shape[2]
     own = lax.all_to_all(
-        message.reshape(2 * slices, width, -1), ("zh", "zl", "chip"), 0, 0, tiled=True
+        message.reshape(2 * slices, width, -1), ("zl", "chip", "zh"), 0, 0, tiled=True
     ).reshape(2 * slices * width, -1)
 
     packed = jnp.concatenate(

time: 97.8 us -> 97 us (level)
  local copies, waits for them, and re-layouts: 4.03 us -> 2.18 us
    reshape x1 -> x0, local copies, waits for them, and re-layouts: 1.85 us -> none  [local(): echoes.reshape(2 * own_pulses, 2, FA, FA)]
    pallas_call x1, Pallas kernels: 4.63 us -> 5.7 us  [beam_factors(): pl.pallas_call(kernel, grid=(4,), out_shape=(shape, shape), in_specs=[SME...]
  transfers between devices with their start and end apart: 6 -> 6, of which waited for: 6 -> 6; matrix products, arithmetic and copies ran while one was open for 1% -> 1% of each run, Pallas kernels for 5% -> 6%
where the time goes in v8:
time: 97 us; the launch traced here: 96.6 us
  blocking collectives  37.4 us (39%)
  starting transfers between devices  35.3 us (36%)
  Pallas kernels  10.4 us (11%)
  waiting for transfers between devices  9.52 us (10%)
  local copies, waits for them, and re-layouts  2.18 us (2%)
  matrix products  1.41 us (1%)
    all_to_all x1, blocking collectives, local(): arrived = lax.all_to_all(result, ('zl', 'chip'), 0, 0, tiled=True)  37.4 us
    all_to_all x1, starting transfers between devices, local(): lax.all_to_all(message.reshape(2 * slices, width, -1), ('zl', 'chip', 'zh...  18.3 us
    ppermute x4, starting transfers between devices, gather_rows(): got = lax.ppermute(packed, axis, [(i, i ^ apart) for i in range(size)])  15.1 us
    ppermute x4, waiting for transfers between devices, gather_rows(): got = lax.ppermute(packed, axis, [(i, i ^ apart) for i in range(size)])  7.43 us
    pallas_call x1, Pallas kernels, beam_factors(): pl.pallas_call(kernel, grid=(4,), out_shape=(shape, shape), in_specs=[SME...  5.7 us
    pallas_call x1, Pallas kernels, compress_own(): pl.pallas_call(own_kernel, out_shape=jax.ShapeDtypeStruct((slices, copies...  4.7 us
  transfers between devices with their start and end apart: 6, of which 6 were waited for; matrix products, arithmetic and copies ran while one was open for 1% of the time, Pallas kernels for 6%

profile of v8, /device:TPU:32, one launch (start us, length us, event | category | flops | bytes accessed | tf_op | source)
XLA Modules:
  0.0 96.6 jit_solution(2775934546990939630)
XLA Ops:
  0.0 0.0 copy-start.3
  0.0 0.0 copy-start.2
  0.0 0.0 copy-start
  0.0 4.7 %shard_map.100 = bf16[32,2,8,512]{3,2,1,0:T(8,128)(2,1)} custom-call(s32[1]{0:T(128)} %bitcast.place.refs_0_, bf16[2,2,2,16384]{3,2,1,0:T(2,128)(2,1)} %echo_hbm.1, f32[2,16384]{1,0:T(2,128)} %matched_hbm.1, bf16[4,2,2,128,128]{4,3,2,1,0:T(8,128)(2,1)} %kern_hbm.1, bf16[2,256,256]{2,1,0:T(8,128)(2,1)} %constant.36.clone.plus_hbm, ...), custom_call_target="tpu_custom_call" | custom-call | flops 1000000000 | bytes 2000000 | tf_op jit(solution)/shard_map/pallas_call | solution.py:191
  4.7 18.3 %all-to-all-start = ((bf16[64,8,512]{2,1,0:T(8,128)(2,1)}), bf16[64,8,512]{2,1,0:T(8,128)(2,1)S(1)}, u32[]{:S(2)}, u32[]{:S(2)}) async-start(bf16[64,8,512]{2,1,0:T(8,128)(2,1)} %bitcast.27), calls=%async_computation | async-start | bytes 1048576 | tf_op jit(solution)/shard_map/all_to_all | solution.py:321
  23.0 0.0 copy-done.1
  23.1 0.1 copy.17
  23.1 0.0 copy-done.3
  23.1 0.1 reshape.36
  23.2 0.1 fusion.2
  23.3 1.9 %collective-permute-start = (bf16[8,128]{1,0:T(8,128)(2,1)S(1)}, bf16[8,128]{1,0:T(8,128)(2,1)S(1)}, u32[]{:S(2)}, u32[]{:S(2)}) collective-permute-start(bf16[8,128]{1,0:T(8,128)(2,1)S(1)} %fusion.2), channel_id=1, source_target_pairs={{0,1},{1,0},{2,3},{3,2},{4,5},{5,4},{6,7},{7,6},{8,9},{9,8},{10,11... | collective-permute-start | bytes 6152 | tf_op jit(solution)/shard_map/ppermute | solution.py:298
  25.2 1.1 %collective-permute-done = bf16[8,128]{1,0:T(8,128)(2,1)S(1)} collective-permute-done((bf16[8,128]{1,0:T(8,128)(2,1)S(1)}, bf16[8,128]{1,0:T(8,128)(2,1)S(1)}, u32[]{:S(2)}, u32[]{:S(2)}) %collective-permute-start) | collective-permute-done | bytes 2080 | tf_op jit(solution)/shard_map/ppermute | solution.py:298
  26.4 0.1 broadcast_select_fusion.7
  26.4 3.4 %collective-permute-start.1 = (bf16[16,128]{1,0:T(8,128)(2,1)S(1)}, bf16[16,128]{1,0:T(8,128)(2,1)S(1)}, u32[]{:S(2)}, u32[]{:S(2)}) collective-permute-start(bf16[16,128]{1,0:T(8,128)(2,1)S(1)} %pad_maximum_fusion.3), channel_id=1, source_target_pairs={{0,2},{2,0},{4,6},{6,4},{8,10},{10,8},{12,14},{14,12},{1,3},{3,1},... | collective-permute-start | bytes 12296 | tf_op jit(solution)/shard_map/ppermute | solution.py:298
  29.8 2.1 %collective-permute-done.1 = bf16[16,128]{1,0:T(8,128)(2,1)S(1)} collective-permute-done((bf16[16,128]{1,0:T(8,128)(2,1)S(1)}, bf16[16,128]{1,0:T(8,128)(2,1)S(1)}, u32[]{:S(2)}, u32[]{:S(2)}) %collective-permute-start.1) | collective-permute-done | bytes 4128 | tf_op jit(solution)/shard_map/ppermute | solution.py:298
  31.9 4.9 %collective-permute-start.2 = (bf16[32,128]{1,0:T(8,128)(2,1)S(1)}, bf16[32,128]{1,0:T(8,128)(2,1)S(1)}, u32[]{:S(2)}, u32[]{:S(2)}) collective-permute-start(bf16[32,128]{1,0:T(8,128)(2,1)S(1)} %pad_maximum_fusion.2), channel_id=1, source_target_pairs={{0,4},{2,6},{4,0},{6,2},{8,12},{10,14},{12,8},{14,10},{1,5},{3,7},... | collective-permute-start | bytes 24584 | tf_op jit(solution)/shard_map/ppermute | solution.py:298
  36.9 2.1 %collective-permute-done.2 = bf16[32,128]{1,0:T(8,128)(2,1)S(1)} collective-permute-done((bf16[32,128]{1,0:T(8,128)(2,1)S(1)}, bf16[32,128]{1,0:T(8,128)(2,1)S(1)}, u32[]{:S(2)}, u32[]{:S(2)}) %collective-permute-start.2) | collective-permute-done | bytes 8224 | tf_op jit(solution)/shard_map/ppermute | solution.py:298
  39.0 4.9 %collective-permute-start.3 = (bf16[64,128]{1,0:T(8,128)(2,1)S(1)}, bf16[64,128]{1,0:T(8,128)(2,1)S(1)}, u32[]{:S(2)}, u32[]{:S(2)}) collective-permute-start(bf16[64,128]{1,0:T(8,128)(2,1)S(1)} %pad_maximum_fusion.1), channel_id=1, source_target_pairs={{0,8},{2,10},{4,12},{6,14},{8,0},{10,2},{12,4},{14,6},{1,9},{3,11}... | collective-permute-start | bytes 49160 | tf_op jit(solution)/shard_map/ppermute | solution.py:298
  44.0 0.0 copy-done.2
  44.0 0.1 copy.15
  44.1 0.1 reshape.35.refs_1_
  44.2 2.1 %collective-permute-done.3 = bf16[64,128]{1,0:T(8,128)(2,1)S(1)} collective-permute-done((bf16[64,128]{1,0:T(8,128)(2,1)S(1)}, bf16[64,128]{1,0:T(8,128)(2,1)S(1)}, u32[]{:S(2)}, u32[]{:S(2)}) %collective-permute-start.3) | collective-permute-done | bytes 16416 | tf_op jit(solution)/shard_map/ppermute | solution.py:298
  46.3 0.0 copy-done
  46.3 5.7 %shard_map.101 = (bf16[4,8,2,16,512]{4,3,2,1,0:T(8,128)(2,1)S(1)}, bf16[4,8,2,16,512]{4,3,2,1,0:T(8,128)(2,1)S(1)}) custom-call(s32[1]{0:T(128)} %bitcast.place.refs_0_, f32[32]{0:T(128)S(1)} %reshape.35.refs_1_, bf16[128,128]{1,0:T(8,128)(2,1)S(1)} %pad_maximum_fusion.refs_2_, bf16[2,128,128]{2,1,0:T(8,128)(2,1)S(1)} %copy-done), custom_call_target="tpu_custom_call" | custom-call | flops 1000000 | bytes 100000 | tf_op jit(solution)/shard_map/pallas_call | solution.py:283
  52.0 0.9 all-to-all-done
  52.9 1.9 %collective-permute-start.4 = (bf16[512,512]{1,0:T(8,128)(2,1)S(1)}, bf16[512,512]{1,0:T(8,128)(2,1)S(1)}, u32[]{:S(2)}, u32[]{:S(2)}) collective-permute-start(bf16[512,512]{1,0:T(8,128)(2,1)S(1)} %bitcast.25), channel_id=1, source_target_pairs={{0,1},{1,0},{2,3},{3,2},{4,5},{5,4},{6,7},{7,6},{8,9},{9,8},{10,11... | collective-permute-start | bytes 1572872 | tf_op jit(solution)/shard_map/ppermute | solution.py:337
  54.8 0.7 fusion.3
  55.5 1.2 %collective-permute-done.4 = bf16[512,512]{1,0:T(8,128)(2,1)S(1)} collective-permute-done((bf16[512,512]{1,0:T(8,128)(2,1)S(1)}, bf16[512,512]{1,0:T(8,128)(2,1)S(1)}, u32[]{:S(2)}, u32[]{:S(2)}) %collective-permute-start.4) | collective-permute-done | bytes 524320 | tf_op jit(solution)/shard_map/ppermute | solution.py:337
  56.7 0.7 add_convert_fusion
  57.4 37.4 %all_to_all.10 = bf16[32,32,512]{2,1,0:T(8,128)(2,1)S(1)} all-to-all(bf16[32,32,512]{2,1,0:T(8,128)(2,1)S(1)} %bitcast.24), channel_id=1, replica_groups=mesh['g'=4,'zh'=2,'zl'=4,'chip'=8,'core'=2] {'zl','chip'}, dimensions={0} | all-to-all | bytes 2097152 | tf_op jit(solution)/shard_map/all_to_all | solution.py:341
  94.8 0.7 copy.20
  95.5 1.1 %reshape.41 = bf16[2,8,2,16384]{3,2,1,0:T(2,128)(2,1)} reshape(bf16[2,8,2,4,32,128]{5,4,3,2,1,0:T(8,128)(2,1)S(1)} %bitcast.23) | data formatting | bytes 2097152 | tf_op jit(solution)/shard_map/reshape | solution.py:343
  (10 shorter events, 0.1 us)
Async XLA Ops:
  0.0 23.0 %copy-start.1 = (s32[4,2,2,8]{3,2,1,0:T(2,128)S(1)}, s32[4,2,2,8]{3,2,1,0:T(2,128)}, u32[]{:S(2)}) copy-start(s32[4,2,2,8]{3,2,1,0:T(2,128)} %param.15) | copy-start | bytes 1540
  0.0 23.1 %copy-start.3 = (bf16[2,8,32]{2,1,0:T(8,128)(2,1)S(1)}, bf16[2,8,32]{2,1,0:T(8,128)(2,1)}, u32[]{:S(2)}) copy-start(bf16[2,8,32]{2,1,0:T(8,128)(2,1)} %param.12) | copy-start | bytes 3076
  0.0 44.0 %copy-start.2 = (f32[4,2,2,2]{0,3,2,1:T(2,128)S(1)}, f32[4,2,2,2]{0,3,2,1:T(2,128)}, u32[]{:S(2)}) copy-start(f32[4,2,2,2]{0,3,2,1:T(2,128)} %param.14) | copy-start | bytes 388
  0.0 46.3 %copy-start = (bf16[2,128,128]{2,1,0:T(8,128)(2,1)S(1)}, bf16[2,128,128]{2,1,0:T(8,128)(2,1)}, u32[]{:S(2)}) copy-start(bf16[2,128,128]{2,1,0:T(8,128)(2,1)} %constant.39.clone.refs_3_) | copy-start | bytes 196612
  4.7 48.2 %all-to-all-start = ((bf16[64,8,512]{2,1,0:T(8,128)(2,1)}), bf16[64,8,512]{2,1,0:T(8,128)(2,1)S(1)}, u32[]{:S(2)}, u32[]{:S(2)}) async-start(bf16[64,8,512]{2,1,0:T(8,128)(2,1)} %bitcast.27), calls=%async_computation | async-start | bytes 1048576 | tf_op jit(solution)/shard_map/all_to_all | solution.py:321
  23.3 3.0 %collective-permute-start = (bf16[8,128]{1,0:T(8,128)(2,1)S(1)}, bf16[8,128]{1,0:T(8,128)(2,1)S(1)}, u32[]{:S(2)}, u32[]{:S(2)}) collective-permute-start(bf16[8,128]{1,0:T(8,128)(2,1)S(1)} %fusion.2), channel_id=1, source_target_pairs={{0,1},{1,0},{2,3},{3,2},{4,5},{5,4},{6,7},{7,6},{8,9},{9,8},{10,11... | collective-permute-start | bytes 6152 | tf_op jit(solution)/shard_map/ppermute | solution.py:298
  26.4 5.5 %collective-permute-start.1 = (bf16[16,128]{1,0:T(8,128)(2,1)S(1)}, bf16[16,128]{1,0:T(8,128)(2,1)S(1)}, u32[]{:S(2)}, u32[]{:S(2)}) collective-permute-start(bf16[16,128]{1,0:T(8,128)(2,1)S(1)} %pad_maximum_fusion.3), channel_id=1, source_target_pairs={{0,2},{2,0},{4,6},{6,4},{8,10},{10,8},{12,14},{14,12},{1,3},{3,1},... | collective-permute-start | bytes 12296 | tf_op jit(solution)/shard_map/ppermute | solution.py:298
  31.9 7.1 %collective-permute-start.2 = (bf16[32,128]{1,0:T(8,128)(2,1)S(1)}, bf16[32,128]{1,0:T(8,128)(2,1)S(1)}, u32[]{:S(2)}, u32[]{:S(2)}) collective-permute-start(bf16[32,128]{1,0:T(8,128)(2,1)S(1)} %pad_maximum_fusion.2), channel_id=1, source_target_pairs={{0,4},{2,6},{4,0},{6,2},{8,12},{10,14},{12,8},{14,10},{1,5},{3,7},... | collective-permute-start | bytes 24584 | tf_op jit(solution)/shard_map/ppermute | solution.py:298
  39.0 7.2 %collective-permute-start.3 = (bf16[64,128]{1,0:T(8,128)(2,1)S(1)}, bf16[64,128]{1,0:T(8,128)(2,1)S(1)}, u32[]{:S(2)}, u32[]{:S(2)}) collective-permute-start(bf16[64,128]{1,0:T(8,128)(2,1)S(1)} %pad_maximum_fusion.1), channel_id=1, source_target_pairs={{0,8},{2,10},{4,12},{6,14},{8,0},{10,2},{12,4},{14,6},{1,9},{3,11}... | collective-permute-start | bytes 49160 | tf_op jit(solution)/shard_map/ppermute | solution.py:298
  52.9 3.8 %collective-permute-start.4 = (bf16[512,512]{1,0:T(8,128)(2,1)S(1)}, bf16[512,512]{1,0:T(8,128)(2,1)S(1)}, u32[]{:S(2)}, u32[]{:S(2)}) collective-permute-start(bf16[512,512]{1,0:T(8,128)(2,1)S(1)} %bitcast.25), channel_id=1, source_target_pairs={{0,1},{1,0},{2,3},{3,2},{4,5},{5,4},{6,7},{7,6},{8,9},{9,8},{10,11... | collective-permute-start | bytes 1572872 | tf_op jit(solution)/shard_map/ppermute | solution.py:337

commit v9 on v8

--- a/solution.py
+++ b/solution.py
@@ -205,7 +205,7 @@
     )(place, *large)
 
 
-def beam_kernel(steer_lanes, place, gains, packed, mixing, out_own, out_other):
+def beam_kernel(steer_lanes, place, gains, packed, mixing, out_own, out_other, firsts, seconds):
     e3 = pl.program_id(0) // 2
     e2 = pl.program_id(0) % 2
     _, _, e4, core = place_bits(place)
@@ -249,13 +249,26 @@
     level3 = [weights(2, child, e3) for child in range(2)]
     level4 = [of_core(w) for w in by_lane(3, e4, (lane // 8) % 2 == 1)]
     imaginary = lane[: rows // 2] % 2 == 1
+
+    @pl.when(pl.program_id(0) == 0)
+    def _():
+        for e1 in range(2):
+            level1 = by_lane(0, e1, (lane // 4) % 2 == 1)
+            for slot in range(2):
+                source = jnp.where(slot == 0, core, 1 - core)
+                firsts[e1 * 2 + slot] = blend(neighbours(dot(data, mixing[source])), level1)
+
+    @pl.when(e3 == 0)
+    def _():
+        for at in range(4):
+            near = neighbours(firsts[at])
+            for c2 in range(2):
+                seconds[e2, at * 2 + c2] = blend(near, level2[c2])
+
     for e1 in range(2):
-        level1 = by_lane(0, e1, (lane // 4) % 2 == 1)
         for slot, out in ((0, out_own), (1, out_other)):
-            source = jnp.where(slot == 0, core, 1 - core)
-            first = neighbours(blend(neighbours(dot(data, mixing[source])), level1))
             for c2 in range(2):
-                second = neighbours(blend(first, level2[c2]))
+                second = neighbours(seconds[e2, (e1 * 2 + slot) * 2 + c2])
                 for c3 in range(2):
                     third = [of_core(v) for v in neighbours(blend(second, level3[c3]))]
                     real_row = blend(third, level4)
@@ -286,6 +299,10 @@
         out_shape=(shape, shape),
         in_specs=[SMEM, SMEM, VMEM, VMEM],
         out_specs=(spec, spec),
+        scratch_shapes=[
+            pltpu.VMEM((4, rows, FA), F32),
+            pltpu.VMEM((2, 8, rows, FA), F32),
+        ],
         compiler_params=pltpu.CompilerParams(vmem_limit_bytes=32 * 2**20),
         cost_estimate=pl.CostEstimate(flops=10**6, bytes_accessed=10**5, transcendentals=0),
     )(place, gains, packed, jnp.asarray(mixing))

time: 97 us -> 96.2 us (level)
  transfers between devices with their start and end apart: 6 -> 6, of which waited for: 6 -> 6; matrix products, arithmetic and copies ran while one was open for 1% -> 1% of each run, Pallas kernels for 6% -> 5%
where the time goes in v9:
time: 96.2 us; the launch traced here: 95.8 us
  blocking collectives  36.6 us (38%)
  starting transfers between devices  35.3 us (37%)
  waiting for transfers between devices  10.3 us (11%)
  Pallas kernels  9.63 us (10%)
  local copies, waits for them, and re-layouts  2.18 us (2%)
  matrix products  1.41 us (1%)
    all_to_all x1, blocking collectives, local(): arrived = lax.all_to_all(result, ('zl', 'chip'), 0, 0, tiled=True)  36.6 us
    all_to_all x1, starting transfers between devices, local(): lax.all_to_all(message.reshape(2 * slices, width, -1), ('zl', 'chip', 'zh...  18.3 us
    ppermute x4, starting transfers between devices, gather_rows(): got = lax.ppermute(packed, axis, [(i, i ^ apart) for i in range(size)])  15.1 us
    ppermute x4, waiting for transfers between devices, gather_rows(): got = lax.ppermute(packed, axis, [(i, i ^ apart) for i in range(size)])  7.43 us
    pallas_call x1, Pallas kernels, beam_factors(): pl.pallas_call(kernel, grid=(4,), out_shape=(shape, shape), in_specs=[SME...  4.93 us
    pallas_call x1, Pallas kernels, compress_own(): pl.pallas_call(own_kernel, out_shape=jax.ShapeDtypeStruct((slices, copies...  4.7 us
  transfers between devices with their start and end apart: 6, of which 6 were waited for; matrix products, arithmetic and copies ran while one was open for 1% of the time, Pallas kernels for 5%

profile of v9, /device:TPU:32, one launch (start us, length us, event | category | flops | bytes accessed | tf_op | source)
XLA Modules:
  0.0 95.8 jit_solution(18116137691014858125)
XLA Ops:
  0.0 0.0 copy-start.3
  0.0 0.0 copy-start.2
  0.0 0.0 copy-start
  0.0 4.7 %shard_map.100 = bf16[32,2,8,512]{3,2,1,0:T(8,128)(2,1)} custom-call(s32[1]{0:T(128)} %bitcast.place.refs_0_, bf16[2,2,2,16384]{3,2,1,0:T(2,128)(2,1)} %echo_hbm.1, f32[2,16384]{1,0:T(2,128)} %matched_hbm.1, bf16[4,2,2,128,128]{4,3,2,1,0:T(8,128)(2,1)} %kern_hbm.1, bf16[2,256,256]{2,1,0:T(8,128)(2,1)} %constant.36.clone.plus_hbm, ...), custom_call_target="tpu_custom_call" | custom-call | flops 1000000000 | bytes 2000000 | tf_op jit(solution)/shard_map/pallas_call | solution.py:191
  4.7 18.3 %all-to-all-start = ((bf16[64,8,512]{2,1,0:T(8,128)(2,1)}), bf16[64,8,512]{2,1,0:T(8,128)(2,1)S(1)}, u32[]{:S(2)}, u32[]{:S(2)}) async-start(bf16[64,8,512]{2,1,0:T(8,128)(2,1)} %bitcast.27), calls=%async_computation | async-start | bytes 1048576 | tf_op jit(solution)/shard_map/all_to_all | solution.py:338
  23.0 0.0 copy-done.1
  23.1 0.1 copy.17
  23.1 0.0 copy-done.3
  23.1 0.1 reshape.36
  23.2 0.1 fusion.2
  23.3 1.9 %collective-permute-start = (bf16[8,128]{1,0:T(8,128)(2,1)S(1)}, bf16[8,128]{1,0:T(8,128)(2,1)S(1)}, u32[]{:S(2)}, u32[]{:S(2)}) collective-permute-start(bf16[8,128]{1,0:T(8,128)(2,1)S(1)} %fusion.2), channel_id=1, source_target_pairs={{0,1},{1,0},{2,3},{3,2},{4,5},{5,4},{6,7},{7,6},{8,9},{9,8},{10,11... | collective-permute-start | bytes 6152 | tf_op jit(solution)/shard_map/ppermute | solution.py:315
  25.2 1.1 %collective-permute-done = bf16[8,128]{1,0:T(8,128)(2,1)S(1)} collective-permute-done((bf16[8,128]{1,0:T(8,128)(2,1)S(1)}, bf16[8,128]{1,0:T(8,128)(2,1)S(1)}, u32[]{:S(2)}, u32[]{:S(2)}) %collective-permute-start) | collective-permute-done | bytes 2080 | tf_op jit(solution)/shard_map/ppermute | solution.py:315
  26.4 0.1 broadcast_select_fusion.7
  26.4 3.4 %collective-permute-start.1 = (bf16[16,128]{1,0:T(8,128)(2,1)S(1)}, bf16[16,128]{1,0:T(8,128)(2,1)S(1)}, u32[]{:S(2)}, u32[]{:S(2)}) collective-permute-start(bf16[16,128]{1,0:T(8,128)(2,1)S(1)} %pad_maximum_fusion.3), channel_id=1, source_target_pairs={{0,2},{2,0},{4,6},{6,4},{8,10},{10,8},{12,14},{14,12},{1,3},{3,1},... | collective-permute-start | bytes 12296 | tf_op jit(solution)/shard_map/ppermute | solution.py:315
  29.8 2.1 %collective-permute-done.1 = bf16[16,128]{1,0:T(8,128)(2,1)S(1)} collective-permute-done((bf16[16,128]{1,0:T(8,128)(2,1)S(1)}, bf16[16,128]{1,0:T(8,128)(2,1)S(1)}, u32[]{:S(2)}, u32[]{:S(2)}) %collective-permute-start.1) | collective-permute-done | bytes 4128 | tf_op jit(solution)/shard_map/ppermute | solution.py:315
  31.9 4.9 %collective-permute-start.2 = (bf16[32,128]{1,0:T(8,128)(2,1)S(1)}, bf16[32,128]{1,0:T(8,128)(2,1)S(1)}, u32[]{:S(2)}, u32[]{:S(2)}) collective-permute-start(bf16[32,128]{1,0:T(8,128)(2,1)S(1)} %pad_maximum_fusion.2), channel_id=1, source_target_pairs={{0,4},{2,6},{4,0},{6,2},{8,12},{10,14},{12,8},{14,10},{1,5},{3,7},... | collective-permute-start | bytes 24584 | tf_op jit(solution)/shard_map/ppermute | solution.py:315
  36.9 2.1 %collective-permute-done.2 = bf16[32,128]{1,0:T(8,128)(2,1)S(1)} collective-permute-done((bf16[32,128]{1,0:T(8,128)(2,1)S(1)}, bf16[32,128]{1,0:T(8,128)(2,1)S(1)}, u32[]{:S(2)}, u32[]{:S(2)}) %collective-permute-start.2) | collective-permute-done | bytes 8224 | tf_op jit(solution)/shard_map/ppermute | solution.py:315
  39.0 4.9 %collective-permute-start.3 = (bf16[64,128]{1,0:T(8,128)(2,1)S(1)}, bf16[64,128]{1,0:T(8,128)(2,1)S(1)}, u32[]{:S(2)}, u32[]{:S(2)}) collective-permute-start(bf16[64,128]{1,0:T(8,128)(2,1)S(1)} %pad_maximum_fusion.1), channel_id=1, source_target_pairs={{0,8},{2,10},{4,12},{6,14},{8,0},{10,2},{12,4},{14,6},{1,9},{3,11}... | collective-permute-start | bytes 49160 | tf_op jit(solution)/shard_map/ppermute | solution.py:315
  44.0 0.0 copy-done.2
  44.0 0.1 copy.15
  44.1 0.1 reshape.35.refs_1_
  44.2 2.1 %collective-permute-done.3 = bf16[64,128]{1,0:T(8,128)(2,1)S(1)} collective-permute-done((bf16[64,128]{1,0:T(8,128)(2,1)S(1)}, bf16[64,128]{1,0:T(8,128)(2,1)S(1)}, u32[]{:S(2)}, u32[]{:S(2)}) %collective-permute-start.3) | collective-permute-done | bytes 16416 | tf_op jit(solution)/shard_map/ppermute | solution.py:315
  46.3 0.0 copy-done
  46.3 4.9 %shard_map.101 = (bf16[4,8,2,16,512]{4,3,2,1,0:T(8,128)(2,1)S(1)}, bf16[4,8,2,16,512]{4,3,2,1,0:T(8,128)(2,1)S(1)}) custom-call(s32[1]{0:T(128)} %bitcast.place.refs_0_, f32[32]{0:T(128)S(1)} %reshape.35.refs_1_, bf16[128,128]{1,0:T(8,128)(2,1)S(1)} %pad_maximum_fusion.refs_2_, bf16[2,128,128]{2,1,0:T(8,128)(2,1)S(1)} %copy-done), custom_call_target="tpu_custom_call" | custom-call | flops 1000000 | bytes 100000 | tf_op jit(solution)/shard_map/pallas_call | solution.py:296
  51.2 1.7 %all-to-all-done = bf16[64,8,512]{2,1,0:T(8,128)(2,1)S(1)} async-done(((bf16[64,8,512]{2,1,0:T(8,128)(2,1)}), bf16[64,8,512]{2,1,0:T(8,128)(2,1)S(1)}, u32[]{:S(2)}, u32[]{:S(2)}) %all-to-all-start) | async-done | bytes 524320 | tf_op jit(solution)/shard_map/all_to_all | solution.py:338
  52.9 1.9 %collective-permute-start.4 = (bf16[512,512]{1,0:T(8,128)(2,1)S(1)}, bf16[512,512]{1,0:T(8,128)(2,1)S(1)}, u32[]{:S(2)}, u32[]{:S(2)}) collective-permute-start(bf16[512,512]{1,0:T(8,128)(2,1)S(1)} %bitcast.25), channel_id=1, source_target_pairs={{0,1},{1,0},{2,3},{3,2},{4,5},{5,4},{6,7},{7,6},{8,9},{9,8},{10,11... | collective-permute-start | bytes 1572872 | tf_op jit(solution)/shard_map/ppermute | solution.py:354
  54.8 0.7 fusion.3
  55.5 1.2 %collective-permute-done.4 = bf16[512,512]{1,0:T(8,128)(2,1)S(1)} collective-permute-done((bf16[512,512]{1,0:T(8,128)(2,1)S(1)}, bf16[512,512]{1,0:T(8,128)(2,1)S(1)}, u32[]{:S(2)}, u32[]{:S(2)}) %collective-permute-start.4) | collective-permute-done | bytes 524320 | tf_op jit(solution)/shard_map/ppermute | solution.py:354
  56.7 0.7 add_convert_fusion
  57.4 36.6 %all_to_all.10 = bf16[32,32,512]{2,1,0:T(8,128)(2,1)S(1)} all-to-all(bf16[32,32,512]{2,1,0:T(8,128)(2,1)S(1)} %bitcast.24), channel_id=1, replica_groups=mesh['g'=4,'zh'=2,'zl'=4,'chip'=8,'core'=2] {'zl','chip'}, dimensions={0} | all-to-all | bytes 2097152 | tf_op jit(solution)/shard_map/all_to_all | solution.py:358
  94.0 0.7 copy.20
  94.7 1.1 %reshape.41 = bf16[2,8,2,16384]{3,2,1,0:T(2,128)(2,1)} reshape(bf16[2,8,2,4,32,128]{5,4,3,2,1,0:T(8,128)(2,1)S(1)} %bitcast.23) | data formatting | bytes 2097152 | tf_op jit(solution)/shard_map/reshape | solution.py:360
  (10 shorter events, 0.1 us)
Async XLA Ops:
  0.0 23.0 %copy-start.1 = (s32[4,2,2,8]{3,2,1,0:T(2,128)S(1)}, s32[4,2,2,8]{3,2,1,0:T(2,128)}, u32[]{:S(2)}) copy-start(s32[4,2,2,8]{3,2,1,0:T(2,128)} %param.15) | copy-start | bytes 1540
  0.0 23.1 %copy-start.3 = (bf16[2,8,32]{2,1,0:T(8,128)(2,1)S(1)}, bf16[2,8,32]{2,1,0:T(8,128)(2,1)}, u32[]{:S(2)}) copy-start(bf16[2,8,32]{2,1,0:T(8,128)(2,1)} %param.12) | copy-start | bytes 3076
  0.0 44.0 %copy-start.2 = (f32[4,2,2,2]{0,3,2,1:T(2,128)S(1)}, f32[4,2,2,2]{0,3,2,1:T(2,128)}, u32[]{:S(2)}) copy-start(f32[4,2,2,2]{0,3,2,1:T(2,128)} %param.14) | copy-start | bytes 388
  0.0 46.3 %copy-start = (bf16[2,128,128]{2,1,0:T(8,128)(2,1)S(1)}, bf16[2,128,128]{2,1,0:T(8,128)(2,1)}, u32[]{:S(2)}) copy-start(bf16[2,128,128]{2,1,0:T(8,128)(2,1)} %constant.39.clone.refs_3_) | copy-start | bytes 196612
  4.7 48.2 %all-to-all-start = ((bf16[64,8,512]{2,1,0:T(8,128)(2,1)}), bf16[64,8,512]{2,1,0:T(8,128)(2,1)S(1)}, u32[]{:S(2)}, u32[]{:S(2)}) async-start(bf16[64,8,512]{2,1,0:T(8,128)(2,1)} %bitcast.27), calls=%async_computation | async-start | bytes 1048576 | tf_op jit(solution)/shard_map/all_to_all | solution.py:338
  23.3 3.0 %collective-permute-start = (bf16[8,128]{1,0:T(8,128)(2,1)S(1)}, bf16[8,128]{1,0:T(8,128)(2,1)S(1)}, u32[]{:S(2)}, u32[]{:S(2)}) collective-permute-start(bf16[8,128]{1,0:T(8,128)(2,1)S(1)} %fusion.2), channel_id=1, source_target_pairs={{0,1},{1,0},{2,3},{3,2},{4,5},{5,4},{6,7},{7,6},{8,9},{9,8},{10,11... | collective-permute-start | bytes 6152 | tf_op jit(solution)/shard_map/ppermute | solution.py:315
  26.4 5.5 %collective-permute-start.1 = (bf16[16,128]{1,0:T(8,128)(2,1)S(1)}, bf16[16,128]{1,0:T(8,128)(2,1)S(1)}, u32[]{:S(2)}, u32[]{:S(2)}) collective-permute-start(bf16[16,128]{1,0:T(8,128)(2,1)S(1)} %pad_maximum_fusion.3), channel_id=1, source_target_pairs={{0,2},{2,0},{4,6},{6,4},{8,10},{10,8},{12,14},{14,12},{1,3},{3,1},... | collective-permute-start | bytes 12296 | tf_op jit(solution)/shard_map/ppermute | solution.py:315
  31.9 7.1 %collective-permute-start.2 = (bf16[32,128]{1,0:T(8,128)(2,1)S(1)}, bf16[32,128]{1,0:T(8,128)(2,1)S(1)}, u32[]{:S(2)}, u32[]{:S(2)}) collective-permute-start(bf16[32,128]{1,0:T(8,128)(2,1)S(1)} %pad_maximum_fusion.2), channel_id=1, source_target_pairs={{0,4},{2,6},{4,0},{6,2},{8,12},{10,14},{12,8},{14,10},{1,5},{3,7},... | collective-permute-start | bytes 24584 | tf_op jit(solution)/shard_map/ppermute | solution.py:315
  39.0 7.2 %collective-permute-start.3 = (bf16[64,128]{1,0:T(8,128)(2,1)S(1)}, bf16[64,128]{1,0:T(8,128)(2,1)S(1)}, u32[]{:S(2)}, u32[]{:S(2)}) collective-permute-start(bf16[64,128]{1,0:T(8,128)(2,1)S(1)} %pad_maximum_fusion.1), channel_id=1, source_target_pairs={{0,8},{2,10},{4,12},{6,14},{8,0},{10,2},{12,4},{14,6},{1,9},{3,11}... | collective-permute-start | bytes 49160 | tf_op jit(solution)/shard_map/ppermute | solution.py:315
  52.9 3.8 %collective-permute-start.4 = (bf16[512,512]{1,0:T(8,128)(2,1)S(1)}, bf16[512,512]{1,0:T(8,128)(2,1)S(1)}, u32[]{:S(2)}, u32[]{:S(2)}) collective-permute-start(bf16[512,512]{1,0:T(8,128)(2,1)S(1)} %bitcast.25), channel_id=1, source_target_pairs={{0,1},{1,0},{2,3},{3,2},{4,5},{5,4},{6,7},{7,6},{8,9},{9,8},{10,11... | collective-permute-start | bytes 1572872 | tf_op jit(solution)/shard_map/ppermute | solution.py:354

commit v10 on v9

--- a/solution.py
+++ b/solution.py
@@ -205,7 +205,7 @@
     )(place, *large)
 
 
-def beam_kernel(steer_lanes, place, gains, packed, mixing, out_own, out_other, firsts, seconds):
+def beam_kernel(steer_lanes, place, gains, packed, mixing, out_own, out_other, firsts, seconds, lasts):
     e3 = pl.program_id(0) // 2
     e2 = pl.program_id(0) % 2
     _, _, e4, core = place_bits(place)
@@ -245,13 +245,13 @@
         tiles = value.reshape(rows // 16, 2, 8, FA)
         return jnp.where(core == 0, tiles[:, 0], tiles[:, 1]).reshape(rows // 2, FA)
 
-    level2 = [weights(1, child, e2) for child in range(2)]
     level3 = [weights(2, child, e3) for child in range(2)]
-    level4 = [of_core(w) for w in by_lane(3, e4, (lane // 8) % 2 == 1)]
     imaginary = lane[: rows // 2] % 2 == 1
 
     @pl.when(pl.program_id(0) == 0)
     def _():
+        for at, weight in enumerate(by_lane(3, e4, (lane // 8) % 2 == 1)):
+            lasts[at] = of_core(weight)
         for e1 in range(2):
             level1 = by_lane(0, e1, (lane // 4) % 2 == 1)
             for slot in range(2):
@@ -260,11 +260,13 @@
 
     @pl.when(e3 == 0)
     def _():
+        level2 = [weights(1, child, e2) for child in range(2)]
         for at in range(4):
             near = neighbours(firsts[at])
             for c2 in range(2):
                 seconds[e2, at * 2 + c2] = blend(near, level2[c2])
 
+    level4 = [lasts[at] for at in range(3)]
     for e1 in range(2):
         for slot, out in ((0, out_own), (1, out_other)):
             for c2 in range(2):
@@ -302,6 +304,7 @@
         scratch_shapes=[
             pltpu.VMEM((4, rows, FA), F32),
             pltpu.VMEM((2, 8, rows, FA), F32),
+            pltpu.VMEM((3, rows // 2, FA), F32),
         ],
         compiler_params=pltpu.CompilerParams(vmem_limit_bytes=32 * 2**20),
         cost_estimate=pl.CostEstimate(flops=10**6, bytes_accessed=10**5, transcendentals=0),

time: 96.2 us -> 96.1 us (level)
  no operation moved by 1% of the time
where the time goes in v10:
time: 96.1 us; the launch traced here: 95.7 us
  blocking collectives  36.5 us (38%)
  starting transfers between devices  35.3 us (37%)
  waiting for transfers between devices  10.4 us (11%)
  Pallas kernels  9.5 us (10%)
  local copies, waits for them, and re-layouts  2.18 us (2%)
  matrix products  1.41 us (1%)
    all_to_all x1, blocking collectives, local(): arrived = lax.all_to_all(result, ('zl', 'chip'), 0, 0, tiled=True)  36.5 us
    all_to_all x1, starting transfers between devices, local(): lax.all_to_all(message.reshape(2 * slices, width, -1), ('zl', 'chip', 'zh...  18.3 us
    ppermute x4, starting transfers between devices, gather_rows(): got = lax.ppermute(packed, axis, [(i, i ^ apart) for i in range(size)])  15.1 us
    ppermute x4, waiting for transfers between devices, gather_rows(): got = lax.ppermute(packed, axis, [(i, i ^ apart) for i in range(size)])  7.43 us
    pallas_call x1, Pallas kernels, beam_factors(): pl.pallas_call(kernel, grid=(4,), out_shape=(shape, shape), in_specs=[SME...  4.8 us
    pallas_call x1, Pallas kernels, compress_own(): pl.pallas_call(own_kernel, out_shape=jax.ShapeDtypeStruct((slices, copies...  4.7 us
  transfers between devices with their start and end apart: 6, of which 6 were waited for; matrix products, arithmetic and copies ran while one was open for 1% of the time, Pallas kernels for 5%

profile of v10, /device:TPU:32, one launch (start us, length us, event | category | flops | bytes accessed | tf_op | source)
XLA Modules:
  0.0 95.7 jit_solution(3216778759733112057)
XLA Ops:
  0.0 0.0 copy-start.3
  0.0 0.0 copy-start.2
  0.0 0.0 copy-start
  0.0 4.7 %shard_map.100 = bf16[32,2,8,512]{3,2,1,0:T(8,128)(2,1)} custom-call(s32[1]{0:T(128)} %bitcast.place.refs_0_, bf16[2,2,2,16384]{3,2,1,0:T(2,128)(2,1)} %echo_hbm.1, f32[2,16384]{1,0:T(2,128)} %matched_hbm.1, bf16[4,2,2,128,128]{4,3,2,1,0:T(8,128)(2,1)} %kern_hbm.1, bf16[2,256,256]{2,1,0:T(8,128)(2,1)} %constant.36.clone.plus_hbm, ...), custom_call_target="tpu_custom_call" | custom-call | flops 1000000000 | bytes 2000000 | tf_op jit(solution)/shard_map/pallas_call | solution.py:191
  4.7 18.3 %all-to-all-start = ((bf16[64,8,512]{2,1,0:T(8,128)(2,1)}), bf16[64,8,512]{2,1,0:T(8,128)(2,1)S(1)}, u32[]{:S(2)}, u32[]{:S(2)}) async-start(bf16[64,8,512]{2,1,0:T(8,128)(2,1)} %bitcast.27), calls=%async_computation | async-start | bytes 1048576 | tf_op jit(solution)/shard_map/all_to_all | solution.py:341
  23.0 0.0 copy-done.1
  23.1 0.1 copy.17
  23.1 0.0 copy-done.3
  23.1 0.1 reshape.36
  23.2 0.1 fusion.2
  23.3 1.9 %collective-permute-start = (bf16[8,128]{1,0:T(8,128)(2,1)S(1)}, bf16[8,128]{1,0:T(8,128)(2,1)S(1)}, u32[]{:S(2)}, u32[]{:S(2)}) collective-permute-start(bf16[8,128]{1,0:T(8,128)(2,1)S(1)} %fusion.2), channel_id=1, source_target_pairs={{0,1},{1,0},{2,3},{3,2},{4,5},{5,4},{6,7},{7,6},{8,9},{9,8},{10,11... | collective-permute-start | bytes 6152 | tf_op jit(solution)/shard_map/ppermute | solution.py:318
  25.2 1.1 %collective-permute-done = bf16[8,128]{1,0:T(8,128)(2,1)S(1)} collective-permute-done((bf16[8,128]{1,0:T(8,128)(2,1)S(1)}, bf16[8,128]{1,0:T(8,128)(2,1)S(1)}, u32[]{:S(2)}, u32[]{:S(2)}) %collective-permute-start) | collective-permute-done | bytes 2080 | tf_op jit(solution)/shard_map/ppermute | solution.py:318
  26.4 0.1 broadcast_select_fusion.7
  26.4 3.4 %collective-permute-start.1 = (bf16[16,128]{1,0:T(8,128)(2,1)S(1)}, bf16[16,128]{1,0:T(8,128)(2,1)S(1)}, u32[]{:S(2)}, u32[]{:S(2)}) collective-permute-start(bf16[16,128]{1,0:T(8,128)(2,1)S(1)} %pad_maximum_fusion.3), channel_id=1, source_target_pairs={{0,2},{2,0},{4,6},{6,4},{8,10},{10,8},{12,14},{14,12},{1,3},{3,1},... | collective-permute-start | bytes 12296 | tf_op jit(solution)/shard_map/ppermute | solution.py:318
  29.8 2.1 %collective-permute-done.1 = bf16[16,128]{1,0:T(8,128)(2,1)S(1)} collective-permute-done((bf16[16,128]{1,0:T(8,128)(2,1)S(1)}, bf16[16,128]{1,0:T(8,128)(2,1)S(1)}, u32[]{:S(2)}, u32[]{:S(2)}) %collective-permute-start.1) | collective-permute-done | bytes 4128 | tf_op jit(solution)/shard_map/ppermute | solution.py:318
  31.9 4.9 %collective-permute-start.2 = (bf16[32,128]{1,0:T(8,128)(2,1)S(1)}, bf16[32,128]{1,0:T(8,128)(2,1)S(1)}, u32[]{:S(2)}, u32[]{:S(2)}) collective-permute-start(bf16[32,128]{1,0:T(8,128)(2,1)S(1)} %pad_maximum_fusion.2), channel_id=1, source_target_pairs={{0,4},{2,6},{4,0},{6,2},{8,12},{10,14},{12,8},{14,10},{1,5},{3,7},... | collective-permute-start | bytes 24584 | tf_op jit(solution)/shard_map/ppermute | solution.py:318
  36.9 2.1 %collective-permute-done.2 = bf16[32,128]{1,0:T(8,128)(2,1)S(1)} collective-permute-done((bf16[32,128]{1,0:T(8,128)(2,1)S(1)}, bf16[32,128]{1,0:T(8,128)(2,1)S(1)}, u32[]{:S(2)}, u32[]{:S(2)}) %collective-permute-start.2) | collective-permute-done | bytes 8224 | tf_op jit(solution)/shard_map/ppermute | solution.py:318
  39.0 4.9 %collective-permute-start.3 = (bf16[64,128]{1,0:T(8,128)(2,1)S(1)}, bf16[64,128]{1,0:T(8,128)(2,1)S(1)}, u32[]{:S(2)}, u32[]{:S(2)}) collective-permute-start(bf16[64,128]{1,0:T(8,128)(2,1)S(1)} %pad_maximum_fusion.1), channel_id=1, source_target_pairs={{0,8},{2,10},{4,12},{6,14},{8,0},{10,2},{12,4},{14,6},{1,9},{3,11}... | collective-permute-start | bytes 49160 | tf_op jit(solution)/shard_map/ppermute | solution.py:318
  44.0 0.0 copy-done.2
  44.0 0.1 copy.15
  44.1 0.1 reshape.35.refs_1_
  44.2 2.1 %collective-permute-done.3 = bf16[64,128]{1,0:T(8,128)(2,1)S(1)} collective-permute-done((bf16[64,128]{1,0:T(8,128)(2,1)S(1)}, bf16[64,128]{1,0:T(8,128)(2,1)S(1)}, u32[]{:S(2)}, u32[]{:S(2)}) %collective-permute-start.3) | collective-permute-done | bytes 16416 | tf_op jit(solution)/shard_map/ppermute | solution.py:318
  46.3 0.0 copy-done
  46.3 4.8 %shard_map.101 = (bf16[4,8,2,16,512]{4,3,2,1,0:T(8,128)(2,1)S(1)}, bf16[4,8,2,16,512]{4,3,2,1,0:T(8,128)(2,1)S(1)}) custom-call(s32[1]{0:T(128)} %bitcast.place.refs_0_, f32[32]{0:T(128)S(1)} %reshape.35.refs_1_, bf16[128,128]{1,0:T(8,128)(2,1)S(1)} %pad_maximum_fusion.refs_2_, bf16[2,128,128]{2,1,0:T(8,128)(2,1)S(1)} %copy-done), custom_call_target="tpu_custom_call" | custom-call | flops 1000000 | bytes 100000 | tf_op jit(solution)/shard_map/pallas_call | solution.py:298
  51.1 1.8 %all-to-all-done = bf16[64,8,512]{2,1,0:T(8,128)(2,1)S(1)} async-done(((bf16[64,8,512]{2,1,0:T(8,128)(2,1)}), bf16[64,8,512]{2,1,0:T(8,128)(2,1)S(1)}, u32[]{:S(2)}, u32[]{:S(2)}) %all-to-all-start) | async-done | bytes 524320 | tf_op jit(solution)/shard_map/all_to_all | solution.py:341
  52.9 1.9 %collective-permute-start.4 = (bf16[512,512]{1,0:T(8,128)(2,1)S(1)}, bf16[512,512]{1,0:T(8,128)(2,1)S(1)}, u32[]{:S(2)}, u32[]{:S(2)}) collective-permute-start(bf16[512,512]{1,0:T(8,128)(2,1)S(1)} %bitcast.25), channel_id=1, source_target_pairs={{0,1},{1,0},{2,3},{3,2},{4,5},{5,4},{6,7},{7,6},{8,9},{9,8},{10,11... | collective-permute-start | bytes 1572872 | tf_op jit(solution)/shard_map/ppermute | solution.py:357
  54.8 0.7 fusion.3
  55.5 1.2 %collective-permute-done.4 = bf16[512,512]{1,0:T(8,128)(2,1)S(1)} collective-permute-done((bf16[512,512]{1,0:T(8,128)(2,1)S(1)}, bf16[512,512]{1,0:T(8,128)(2,1)S(1)}, u32[]{:S(2)}, u32[]{:S(2)}) %collective-permute-start.4) | collective-permute-done | bytes 524320 | tf_op jit(solution)/shard_map/ppermute | solution.py:357
  56.7 0.7 add_convert_fusion
  57.4 36.5 %all_to_all.10 = bf16[32,32,512]{2,1,0:T(8,128)(2,1)S(1)} all-to-all(bf16[32,32,512]{2,1,0:T(8,128)(2,1)S(1)} %bitcast.24), channel_id=1, replica_groups=mesh['g'=4,'zh'=2,'zl'=4,'chip'=8,'core'=2] {'zl','chip'}, dimensions={0} | all-to-all | bytes 2097152 | tf_op jit(solution)/shard_map/all_to_all | solution.py:361
  93.9 0.7 copy.20
  94.6 1.1 %reshape.41 = bf16[2,8,2,16384]{3,2,1,0:T(2,128)(2,1)} reshape(bf16[2,8,2,4,32,128]{5,4,3,2,1,0:T(8,128)(2,1)S(1)} %bitcast.23) | data formatting | bytes 2097152 | tf_op jit(solution)/shard_map/reshape | solution.py:363
  (10 shorter events, 0.1 us)
Async XLA Ops:
  0.0 23.0 %copy-start.1 = (s32[4,2,2,8]{3,2,1,0:T(2,128)S(1)}, s32[4,2,2,8]{3,2,1,0:T(2,128)}, u32[]{:S(2)}) copy-start(s32[4,2,2,8]{3,2,1,0:T(2,128)} %param.15) | copy-start | bytes 1540
  0.0 23.1 %copy-start.3 = (bf16[2,8,32]{2,1,0:T(8,128)(2,1)S(1)}, bf16[2,8,32]{2,1,0:T(8,128)(2,1)}, u32[]{:S(2)}) copy-start(bf16[2,8,32]{2,1,0:T(8,128)(2,1)} %param.12) | copy-start | bytes 3076
  0.0 44.0 %copy-start.2 = (f32[4,2,2,2]{0,3,2,1:T(2,128)S(1)}, f32[4,2,2,2]{0,3,2,1:T(2,128)}, u32[]{:S(2)}) copy-start(f32[4,2,2,2]{0,3,2,1:T(2,128)} %param.14) | copy-start | bytes 388
  0.0 46.3 %copy-start = (bf16[2,128,128]{2,1,0:T(8,128)(2,1)S(1)}, bf16[2,128,128]{2,1,0:T(8,128)(2,1)}, u32[]{:S(2)}) copy-start(bf16[2,128,128]{2,1,0:T(8,128)(2,1)} %constant.39.clone.refs_3_) | copy-start | bytes 196612
  4.7 48.2 %all-to-all-start = ((bf16[64,8,512]{2,1,0:T(8,128)(2,1)}), bf16[64,8,512]{2,1,0:T(8,128)(2,1)S(1)}, u32[]{:S(2)}, u32[]{:S(2)}) async-start(bf16[64,8,512]{2,1,0:T(8,128)(2,1)} %bitcast.27), calls=%async_computation | async-start | bytes 1048576 | tf_op jit(solution)/shard_map/all_to_all | solution.py:341
  23.3 3.0 %collective-permute-start = (bf16[8,128]{1,0:T(8,128)(2,1)S(1)}, bf16[8,128]{1,0:T(8,128)(2,1)S(1)}, u32[]{:S(2)}, u32[]{:S(2)}) collective-permute-start(bf16[8,128]{1,0:T(8,128)(2,1)S(1)} %fusion.2), channel_id=1, source_target_pairs={{0,1},{1,0},{2,3},{3,2},{4,5},{5,4},{6,7},{7,6},{8,9},{9,8},{10,11... | collective-permute-start | bytes 6152 | tf_op jit(solution)/shard_map/ppermute | solution.py:318
  26.4 5.5 %collective-permute-start.1 = (bf16[16,128]{1,0:T(8,128)(2,1)S(1)}, bf16[16,128]{1,0:T(8,128)(2,1)S(1)}, u32[]{:S(2)}, u32[]{:S(2)}) collective-permute-start(bf16[16,128]{1,0:T(8,128)(2,1)S(1)} %pad_maximum_fusion.3), channel_id=1, source_target_pairs={{0,2},{2,0},{4,6},{6,4},{8,10},{10,8},{12,14},{14,12},{1,3},{3,1},... | collective-permute-start | bytes 12296 | tf_op jit(solution)/shard_map/ppermute | solution.py:318
  31.9 7.1 %collective-permute-start.2 = (bf16[32,128]{1,0:T(8,128)(2,1)S(1)}, bf16[32,128]{1,0:T(8,128)(2,1)S(1)}, u32[]{:S(2)}, u32[]{:S(2)}) collective-permute-start(bf16[32,128]{1,0:T(8,128)(2,1)S(1)} %pad_maximum_fusion.2), channel_id=1, source_target_pairs={{0,4},{2,6},{4,0},{6,2},{8,12},{10,14},{12,8},{14,10},{1,5},{3,7},... | collective-permute-start | bytes 24584 | tf_op jit(solution)/shard_map/ppermute | solution.py:318
  39.0 7.2 %collective-permute-start.3 = (bf16[64,128]{1,0:T(8,128)(2,1)S(1)}, bf16[64,128]{1,0:T(8,128)(2,1)S(1)}, u32[]{:S(2)}, u32[]{:S(2)}) collective-permute-start(bf16[64,128]{1,0:T(8,128)(2,1)S(1)} %pad_maximum_fusion.1), channel_id=1, source_target_pairs={{0,8},{2,10},{4,12},{6,14},{8,0},{10,2},{12,4},{14,6},{1,9},{3,11}... | collective-permute-start | bytes 49160 | tf_op jit(solution)/shard_map/ppermute | solution.py:318
  52.9 3.8 %collective-permute-start.4 = (bf16[512,512]{1,0:T(8,128)(2,1)S(1)}, bf16[512,512]{1,0:T(8,128)(2,1)S(1)}, u32[]{:S(2)}, u32[]{:S(2)}) collective-permute-start(bf16[512,512]{1,0:T(8,128)(2,1)S(1)} %bitcast.25), channel_id=1, source_target_pairs={{0,1},{1,0},{2,3},{3,2},{4,5},{5,4},{6,7},{7,6},{8,9},{9,8},{10,11... | collective-permute-start | bytes 1572872 | tf_op jit(solution)/shard_map/ppermute | solution.py:357

commit v11 on v10

--- a/solution.py
+++ b/solution.py
@@ -205,7 +205,7 @@
     )(place, *large)
 
 
-def beam_kernel(steer_lanes, place, gains, packed, mixing, out_own, out_other, firsts, seconds, lasts):
+def beam_kernel(steer_lanes, place, gains, packed, mixing, out_own, out_other, firsts, seconds, lasts, thirds):
     e3 = pl.program_id(0) // 2
     e2 = pl.program_id(0) % 2
     _, _, e4, core = place_bits(place)
@@ -245,7 +245,13 @@
         tiles = value.reshape(rows // 16, 2, 8, FA)
         return jnp.where(core == 0, tiles[:, 0], tiles[:, 1]).reshape(rows // 2, FA)
 
-    level3 = [weights(2, child, e3) for child in range(2)]
+
+    @pl.when(e2 == 0)
+    def _():
+        for child in range(2):
+            for at, weight in enumerate(weights(2, child, e3)):
+                thirds[child, at] = weight
+
     imaginary = lane[: rows // 2] % 2 == 1
 
     @pl.when(pl.program_id(0) == 0)
@@ -266,6 +272,7 @@
             for c2 in range(2):
                 seconds[e2, at * 2 + c2] = blend(near, level2[c2])
 
+    level3 = [[thirds[child, at] for at in range(3)] for child in range(2)]
     level4 = [lasts[at] for at in range(3)]
     for e1 in range(2):
         for slot, out in ((0, out_own), (1, out_other)):
@@ -305,6 +312,7 @@
             pltpu.VMEM((4, rows, FA), F32),
             pltpu.VMEM((2, 8, rows, FA), F32),
             pltpu.VMEM((3, rows // 2, FA), F32),
+            pltpu.VMEM((2, 3, rows, FA), F32),
         ],
         compiler_params=pltpu.CompilerParams(vmem_limit_bytes=32 * 2**20),
         cost_estimate=pl.CostEstimate(flops=10**6, bytes_accessed=10**5, transcendentals=0),

time: 96.1 us -> 95.9 us (level)
  no operation moved by 1% of the time
where the time goes in v11:
time: 95.9 us; the launch traced here: 95.5 us
  blocking collectives  36.3 us (38%)
  starting transfers between devices  35.3 us (37%)
  waiting for transfers between devices  10.6 us (11%)
  Pallas kernels  9.31 us (10%)
  local copies, waits for them, and re-layouts  2.18 us (2%)
  matrix products  1.41 us (1%)
    all_to_all x1, blocking collectives, local(): arrived = lax.all_to_all(result, ('zl', 'chip'), 0, 0, tiled=True)  36.3 us
    all_to_all x1, starting transfers between devices, local(): lax.all_to_all(message.reshape(2 * slices, width, -1), ('zl', 'chip', 'zh...  18.3 us
    ppermute x4, starting transfers between devices, gather_rows(): got = lax.ppermute(packed, axis, [(i, i ^ apart) for i in range(size)])  15.1 us
    ppermute x4, waiting for transfers between devices, gather_rows(): got = lax.ppermute(packed, axis, [(i, i ^ apart) for i in range(size)])  7.43 us
    pallas_call x1, Pallas kernels, compress_own(): pl.pallas_call(own_kernel, out_shape=jax.ShapeDtypeStruct((slices, copies...  4.7 us
    pallas_call x1, Pallas kernels, beam_factors(): pl.pallas_call(kernel, grid=(4,), out_shape=(shape, shape), in_specs=[SME...  4.61 us
    all_to_all x1, waiting for transfers between devices, local(): lax.all_to_all(message.reshape(2 * slices, width, -1), ('zl', 'chip', 'zh...  2.01 us
  transfers between devices with their start and end apart: 6, of which 6 were waited for; matrix products, arithmetic and copies ran while one was open for 1% of the time, Pallas kernels for 5%

profile of v11, /device:TPU:32, one launch (start us, length us, event | category | flops | bytes accessed | tf_op | source)
XLA Modules:
  0.0 95.5 jit_solution(18384601067880637448)
XLA Ops:
  0.0 0.0 copy-start.3
  0.0 0.0 copy-start.2
  0.0 0.0 copy-start
  0.0 4.7 %shard_map.100 = bf16[32,2,8,512]{3,2,1,0:T(8,128)(2,1)} custom-call(s32[1]{0:T(128)} %bitcast.place.refs_0_, bf16[2,2,2,16384]{3,2,1,0:T(2,128)(2,1)} %echo_hbm.1, f32[2,16384]{1,0:T(2,128)} %matched_hbm.1, bf16[4,2,2,128,128]{4,3,2,1,0:T(8,128)(2,1)} %kern_hbm.1, bf16[2,256,256]{2,1,0:T(8,128)(2,1)} %constant.36.clone.plus_hbm, ...), custom_call_target="tpu_custom_call" | custom-call | flops 1000000000 | bytes 2000000 | tf_op jit(solution)/shard_map/pallas_call | solution.py:191
  4.7 18.3 %all-to-all-start = ((bf16[64,8,512]{2,1,0:T(8,128)(2,1)}), bf16[64,8,512]{2,1,0:T(8,128)(2,1)S(1)}, u32[]{:S(2)}, u32[]{:S(2)}) async-start(bf16[64,8,512]{2,1,0:T(8,128)(2,1)} %bitcast.27), calls=%async_computation | async-start | bytes 1048576 | tf_op jit(solution)/shard_map/all_to_all | solution.py:349
  23.0 0.0 copy-done.1
  23.1 0.1 copy.17
  23.1 0.0 copy-done.3
  23.1 0.1 reshape.36
  23.2 0.1 fusion.2
  23.3 1.9 %collective-permute-start = (bf16[8,128]{1,0:T(8,128)(2,1)S(1)}, bf16[8,128]{1,0:T(8,128)(2,1)S(1)}, u32[]{:S(2)}, u32[]{:S(2)}) collective-permute-start(bf16[8,128]{1,0:T(8,128)(2,1)S(1)} %fusion.2), channel_id=1, source_target_pairs={{0,1},{1,0},{2,3},{3,2},{4,5},{5,4},{6,7},{7,6},{8,9},{9,8},{10,11... | collective-permute-start | bytes 6152 | tf_op jit(solution)/shard_map/ppermute | solution.py:326
  25.2 1.1 %collective-permute-done = bf16[8,128]{1,0:T(8,128)(2,1)S(1)} collective-permute-done((bf16[8,128]{1,0:T(8,128)(2,1)S(1)}, bf16[8,128]{1,0:T(8,128)(2,1)S(1)}, u32[]{:S(2)}, u32[]{:S(2)}) %collective-permute-start) | collective-permute-done | bytes 2080 | tf_op jit(solution)/shard_map/ppermute | solution.py:326
  26.4 0.1 broadcast_select_fusion.7
  26.4 3.4 %collective-permute-start.1 = (bf16[16,128]{1,0:T(8,128)(2,1)S(1)}, bf16[16,128]{1,0:T(8,128)(2,1)S(1)}, u32[]{:S(2)}, u32[]{:S(2)}) collective-permute-start(bf16[16,128]{1,0:T(8,128)(2,1)S(1)} %pad_maximum_fusion.3), channel_id=1, source_target_pairs={{0,2},{2,0},{4,6},{6,4},{8,10},{10,8},{12,14},{14,12},{1,3},{3,1},... | collective-permute-start | bytes 12296 | tf_op jit(solution)/shard_map/ppermute | solution.py:326
  29.8 2.1 %collective-permute-done.1 = bf16[16,128]{1,0:T(8,128)(2,1)S(1)} collective-permute-done((bf16[16,128]{1,0:T(8,128)(2,1)S(1)}, bf16[16,128]{1,0:T(8,128)(2,1)S(1)}, u32[]{:S(2)}, u32[]{:S(2)}) %collective-permute-start.1) | collective-permute-done | bytes 4128 | tf_op jit(solution)/shard_map/ppermute | solution.py:326
  31.9 4.9 %collective-permute-start.2 = (bf16[32,128]{1,0:T(8,128)(2,1)S(1)}, bf16[32,128]{1,0:T(8,128)(2,1)S(1)}, u32[]{:S(2)}, u32[]{:S(2)}) collective-permute-start(bf16[32,128]{1,0:T(8,128)(2,1)S(1)} %pad_maximum_fusion.2), channel_id=1, source_target_pairs={{0,4},{2,6},{4,0},{6,2},{8,12},{10,14},{12,8},{14,10},{1,5},{3,7},... | collective-permute-start | bytes 24584 | tf_op jit(solution)/shard_map/ppermute | solution.py:326
  36.9 2.1 %collective-permute-done.2 = bf16[32,128]{1,0:T(8,128)(2,1)S(1)} collective-permute-done((bf16[32,128]{1,0:T(8,128)(2,1)S(1)}, bf16[32,128]{1,0:T(8,128)(2,1)S(1)}, u32[]{:S(2)}, u32[]{:S(2)}) %collective-permute-start.2) | collective-permute-done | bytes 8224 | tf_op jit(solution)/shard_map/ppermute | solution.py:326
  39.0 4.9 %collective-permute-start.3 = (bf16[64,128]{1,0:T(8,128)(2,1)S(1)}, bf16[64,128]{1,0:T(8,128)(2,1)S(1)}, u32[]{:S(2)}, u32[]{:S(2)}) collective-permute-start(bf16[64,128]{1,0:T(8,128)(2,1)S(1)} %pad_maximum_fusion.1), channel_id=1, source_target_pairs={{0,8},{2,10},{4,12},{6,14},{8,0},{10,2},{12,4},{14,6},{1,9},{3,11}... | collective-permute-start | bytes 49160 | tf_op jit(solution)/shard_map/ppermute | solution.py:326
  44.0 0.0 copy-done.2
  44.0 0.1 copy.15
  44.1 0.1 reshape.35.refs_1_
  44.2 2.1 %collective-permute-done.3 = bf16[64,128]{1,0:T(8,128)(2,1)S(1)} collective-permute-done((bf16[64,128]{1,0:T(8,128)(2,1)S(1)}, bf16[64,128]{1,0:T(8,128)(2,1)S(1)}, u32[]{:S(2)}, u32[]{:S(2)}) %collective-permute-start.3) | collective-permute-done | bytes 16416 | tf_op jit(solution)/shard_map/ppermute | solution.py:326
  46.3 0.0 copy-done
  46.3 4.6 %shard_map.101 = (bf16[4,8,2,16,512]{4,3,2,1,0:T(8,128)(2,1)S(1)}, bf16[4,8,2,16,512]{4,3,2,1,0:T(8,128)(2,1)S(1)}) custom-call(s32[1]{0:T(128)} %bitcast.place.refs_0_, f32[32]{0:T(128)S(1)} %reshape.35.refs_1_, bf16[128,128]{1,0:T(8,128)(2,1)S(1)} %pad_maximum_fusion.refs_2_, bf16[2,128,128]{2,1,0:T(8,128)(2,1)S(1)} %copy-done), custom_call_target="tpu_custom_call" | custom-call | flops 1000000 | bytes 100000 | tf_op jit(solution)/shard_map/pallas_call | solution.py:305
  50.9 2.0 %all-to-all-done = bf16[64,8,512]{2,1,0:T(8,128)(2,1)S(1)} async-done(((bf16[64,8,512]{2,1,0:T(8,128)(2,1)}), bf16[64,8,512]{2,1,0:T(8,128)(2,1)S(1)}, u32[]{:S(2)}, u32[]{:S(2)}) %all-to-all-start) | async-done | bytes 524320 | tf_op jit(solution)/shard_map/all_to_all | solution.py:349
  52.9 1.9 %collective-permute-start.4 = (bf16[512,512]{1,0:T(8,128)(2,1)S(1)}, bf16[512,512]{1,0:T(8,128)(2,1)S(1)}, u32[]{:S(2)}, u32[]{:S(2)}) collective-permute-start(bf16[512,512]{1,0:T(8,128)(2,1)S(1)} %bitcast.25), channel_id=1, source_target_pairs={{0,1},{1,0},{2,3},{3,2},{4,5},{5,4},{6,7},{7,6},{8,9},{9,8},{10,11... | collective-permute-start | bytes 1572872 | tf_op jit(solution)/shard_map/ppermute | solution.py:365
  54.8 0.7 fusion.3
  55.5 1.2 %collective-permute-done.4 = bf16[512,512]{1,0:T(8,128)(2,1)S(1)} collective-permute-done((bf16[512,512]{1,0:T(8,128)(2,1)S(1)}, bf16[512,512]{1,0:T(8,128)(2,1)S(1)}, u32[]{:S(2)}, u32[]{:S(2)}) %collective-permute-start.4) | collective-permute-done | bytes 524320 | tf_op jit(solution)/shard_map/ppermute | solution.py:365
  56.7 0.7 add_convert_fusion
  57.4 36.3 %all_to_all.10 = bf16[32,32,512]{2,1,0:T(8,128)(2,1)S(1)} all-to-all(bf16[32,32,512]{2,1,0:T(8,128)(2,1)S(1)} %bitcast.24), channel_id=1, replica_groups=mesh['g'=4,'zh'=2,'zl'=4,'chip'=8,'core'=2] {'zl','chip'}, dimensions={0} | all-to-all | bytes 2097152 | tf_op jit(solution)/shard_map/all_to_all | solution.py:369
  93.7 0.7 copy.20
  94.4 1.1 %reshape.41 = bf16[2,8,2,16384]{3,2,1,0:T(2,128)(2,1)} reshape(bf16[2,8,2,4,32,128]{5,4,3,2,1,0:T(8,128)(2,1)S(1)} %bitcast.23) | data formatting | bytes 2097152 | tf_op jit(solution)/shard_map/reshape | solution.py:371
  (10 shorter events, 0.1 us)
Async XLA Ops:
  0.0 23.0 %copy-start.1 = (s32[4,2,2,8]{3,2,1,0:T(2,128)S(1)}, s32[4,2,2,8]{3,2,1,0:T(2,128)}, u32[]{:S(2)}) copy-start(s32[4,2,2,8]{3,2,1,0:T(2,128)} %param.15) | copy-start | bytes 1540
  0.0 23.1 %copy-start.3 = (bf16[2,8,32]{2,1,0:T(8,128)(2,1)S(1)}, bf16[2,8,32]{2,1,0:T(8,128)(2,1)}, u32[]{:S(2)}) copy-start(bf16[2,8,32]{2,1,0:T(8,128)(2,1)} %param.12) | copy-start | bytes 3076
  0.0 44.0 %copy-start.2 = (f32[4,2,2,2]{0,3,2,1:T(2,128)S(1)}, f32[4,2,2,2]{0,3,2,1:T(2,128)}, u32[]{:S(2)}) copy-start(f32[4,2,2,2]{0,3,2,1:T(2,128)} %param.14) | copy-start | bytes 388
  0.0 46.3 %copy-start = (bf16[2,128,128]{2,1,0:T(8,128)(2,1)S(1)}, bf16[2,128,128]{2,1,0:T(8,128)(2,1)}, u32[]{:S(2)}) copy-start(bf16[2,128,128]{2,1,0:T(8,128)(2,1)} %constant.39.clone.refs_3_) | copy-start | bytes 196612
  4.7 48.2 %all-to-all-start = ((bf16[64,8,512]{2,1,0:T(8,128)(2,1)}), bf16[64,8,512]{2,1,0:T(8,128)(2,1)S(1)}, u32[]{:S(2)}, u32[]{:S(2)}) async-start(bf16[64,8,512]{2,1,0:T(8,128)(2,1)} %bitcast.27), calls=%async_computation | async-start | bytes 1048576 | tf_op jit(solution)/shard_map/all_to_all | solution.py:349
  23.3 3.0 %collective-permute-start = (bf16[8,128]{1,0:T(8,128)(2,1)S(1)}, bf16[8,128]{1,0:T(8,128)(2,1)S(1)}, u32[]{:S(2)}, u32[]{:S(2)}) collective-permute-start(bf16[8,128]{1,0:T(8,128)(2,1)S(1)} %fusion.2), channel_id=1, source_target_pairs={{0,1},{1,0},{2,3},{3,2},{4,5},{5,4},{6,7},{7,6},{8,9},{9,8},{10,11... | collective-permute-start | bytes 6152 | tf_op jit(solution)/shard_map/ppermute | solution.py:326
  26.4 5.5 %collective-permute-start.1 = (bf16[16,128]{1,0:T(8,128)(2,1)S(1)}, bf16[16,128]{1,0:T(8,128)(2,1)S(1)}, u32[]{:S(2)}, u32[]{:S(2)}) collective-permute-start(bf16[16,128]{1,0:T(8,128)(2,1)S(1)} %pad_maximum_fusion.3), channel_id=1, source_target_pairs={{0,2},{2,0},{4,6},{6,4},{8,10},{10,8},{12,14},{14,12},{1,3},{3,1},... | collective-permute-start | bytes 12296 | tf_op jit(solution)/shard_map/ppermute | solution.py:326
  31.9 7.1 %collective-permute-start.2 = (bf16[32,128]{1,0:T(8,128)(2,1)S(1)}, bf16[32,128]{1,0:T(8,128)(2,1)S(1)}, u32[]{:S(2)}, u32[]{:S(2)}) collective-permute-start(bf16[32,128]{1,0:T(8,128)(2,1)S(1)} %pad_maximum_fusion.2), channel_id=1, source_target_pairs={{0,4},{2,6},{4,0},{6,2},{8,12},{10,14},{12,8},{14,10},{1,5},{3,7},... | collective-permute-start | bytes 24584 | tf_op jit(solution)/shard_map/ppermute | solution.py:326
  39.0 7.2 %collective-permute-start.3 = (bf16[64,128]{1,0:T(8,128)(2,1)S(1)}, bf16[64,128]{1,0:T(8,128)(2,1)S(1)}, u32[]{:S(2)}, u32[]{:S(2)}) collective-permute-start(bf16[64,128]{1,0:T(8,128)(2,1)S(1)} %pad_maximum_fusion.1), channel_id=1, source_target_pairs={{0,8},{2,10},{4,12},{6,14},{8,0},{10,2},{12,4},{14,6},{1,9},{3,11}... | collective-permute-start | bytes 49160 | tf_op jit(solution)/shard_map/ppermute | solution.py:326
  52.9 3.8 %collective-permute-start.4 = (bf16[512,512]{1,0:T(8,128)(2,1)S(1)}, bf16[512,512]{1,0:T(8,128)(2,1)S(1)}, u32[]{:S(2)}, u32[]{:S(2)}) collective-permute-start(bf16[512,512]{1,0:T(8,128)(2,1)S(1)} %bitcast.25), channel_id=1, source_target_pairs={{0,1},{1,0},{2,3},{3,2},{4,5},{5,4},{6,7},{7,6},{8,9},{9,8},{10,11... | collective-permute-start | bytes 1572872 | tf_op jit(solution)/shard_map/ppermute | solution.py:365
